TPU v7x, 32 devices: a whole 2x2x4 slice. The times are simulated.
32 devices in a mesh: dp: 8 (over y, x, core), seq: 4 (over z).
Axes of the slice: x: 2, y: 2, z: 4, core: 2. Of those that a mesh axis runs over, the one named last changes fastest.
Arguments:
- tokens: bfloat16 [16, 1024, 2048], P('dp', 'seq'), may hold values from -40 to 40
- exit_layer: int32 [16, 1024], P('dp', 'seq'), may hold values from 1 to 24, as said below
- first_gain: bfloat16 [2048], P(('dp', 'seq')), may hold values from 0.099609375 to 1.8984375
- first_shift: bfloat16 [2048], P(('dp', 'seq')), may hold values from -1.75 to 1.75
- query_weight: bfloat16 [2048, 2048], P(('dp', 'seq')), may hold values from -0.125 to 0.125
- query_bias: bfloat16 [2048], P(('dp', 'seq')), may hold values from -3 to 3
- key_weight: bfloat16 [2048, 2048], P(('dp', 'seq')), may hold values from -0.125 to 0.125
- value_weight: bfloat16 [2048, 2048], P(('dp', 'seq')), may hold values from -0.125 to 0.125
- value_bias: bfloat16 [2048], P(('dp', 'seq')), may hold values from -3 to 3
- output_weight: bfloat16 [2048, 2048], P(('dp', 'seq')), may hold values from -0.75 to 0.75
- output_bias: bfloat16 [2048], P(('dp', 'seq')), may hold values from -1.75 to 1.75
- second_gain: bfloat16 [2048], P(('dp', 'seq')), may hold values from 0.099609375 to 1.8984375
- second_shift: bfloat16 [2048], P(('dp', 'seq')), may hold values from -1.75 to 1.75
- expand_weight: bfloat16 [8192, 2048], P(('dp', 'seq')), may hold values from -0.125 to 0.125
- expand_bias: bfloat16 [8192], P(('dp', 'seq')), may hold values from -3 to 3
- shrink_weight: bfloat16 [2048, 8192], P(('dp', 'seq')), may hold values from -0.0625 to 0.0625
- shrink_bias: bfloat16 [2048], P(('dp', 'seq')), may hold values from -1.75 to 1.75
- cotangent: bfloat16 [16, 1024, 2048], P('dp', 'seq'), may hold values from -8 to 8
Outputs:
- layer_out: bfloat16 [16, 1024, 2048], P('dp', 'seq')
- tokens_grad: bfloat16 [16, 1024, 2048], P('dp', 'seq')
- first_gain_grad: float32 [2048], P(('dp', 'seq'))
- first_shift_grad: float32 [2048], P(('dp', 'seq'))
- query_weight_grad: float32 [2048, 2048], P(('dp', 'seq'))
- query_bias_grad: float32 [2048], P(('dp', 'seq'))
- key_weight_grad: float32 [2048, 2048], P(('dp', 'seq'))
- value_weight_grad: float32 [2048, 2048], P(('dp', 'seq'))
- value_bias_grad: float32 [2048], P(('dp', 'seq'))
- output_weight_grad: float32 [2048, 2048], P(('dp', 'seq'))
- output_bias_grad: float32 [2048], P(('dp', 'seq'))
- second_gain_grad: float32 [2048], P(('dp', 'seq'))
- second_shift_grad: float32 [2048], P(('dp', 'seq'))
- expand_weight_grad: float32 [8192, 2048], P(('dp', 'seq'))
- expand_bias_grad: float32 [8192], P(('dp', 'seq'))
- shrink_weight_grad: float32 [2048, 8192], P(('dp', 'seq'))
- shrink_bias_grad: float32 [2048], P(('dp', 'seq'))
Inputs may be any that keep to these rules, and one draw needn't show every extreme that they name: `exit_layer`: within each sequence the exit layer never rises from one position to the next; the first position of every sequence has 24; of the 2 sequences on each index of dp, one has every position above 12 except its last 16 positions, which are at or below 12.
All inputs are finite; a program needn't handle non-finite values.
Results may differ from a plain program's by a relative error of at most 0.012.
Values may be sent and summed in bfloat16 or wider, within the bound.
No kernel may reach another device: no remote copies, remote signals or barrier semaphores. Data moves between devices by JAX's collectives and lax.ppermute only.
A program may use at most 640 MiB of HBM per device.

v0:
```python
import jax
import jax.numpy as jnp
from jax import lax
from jax.sharding import PartitionSpec as P

HEAD_DIM = 64
LAYER = 12


EPS = 1e-05


def normalize(values):
    center = values - jnp.mean(values, axis=-1, keepdims=True)
    spread = jnp.mean(center * center, axis=-1, keepdims=True)
    return center * lax.rsqrt(spread + EPS)


def project(left, weight):
    return lax.dot_general(
        left, weight, (((1,), (1,)), ((), ())), preferred_element_type=jnp.float32
    )


def through(left, weight):
    return jnp.dot(left, weight, preferred_element_type=jnp.float32)


def outer_rows(grad_cols, inputs):
    return lax.dot_general(
        grad_cols, inputs, (((0,), (0,)), ((), ())), preferred_element_type=jnp.float32
    )


def place_cols(buffer, piece):
    return piece.astype(buffer.dtype)


def column_total(matrix):
    return jnp.sum(matrix, axis=0, dtype=jnp.float32)


def per_device(
    tokens,
    exit_layer,
    first_gain,
    first_shift,
    query_weight,
    query_bias,
    key_weight,
    value_weight,
    value_bias,
    output_weight,
    output_bias,
    second_gain,
    second_shift,
    expand_weight,
    expand_bias,
    shrink_weight,
    shrink_bias,
    cotangent,
):
    seq_count, local_len, width = tokens.shape
    hidden_width = shrink_weight.shape[1]
    total_rows = seq_count * local_len
    heads = width // HEAD_DIM
    inputs = tokens.reshape(total_rows, width).astype(jnp.float32)
    active = (exit_layer > LAYER).astype(jnp.float32).reshape(total_rows, 1)
    gain_one, shift_one = (
        lax.all_gather(first_gain, ("dp", "seq"), axis=0, tiled=True),
        lax.all_gather(first_shift, ("dp", "seq"), axis=0, tiled=True),
    )
    gain_one = gain_one.astype(jnp.float32)
    shift_one = shift_one.astype(jnp.float32)
    normed_in = normalize(inputs)
    first_rows = (normed_in * gain_one + shift_one).astype(jnp.bfloat16)
    blank = jnp.zeros((total_rows, width), jnp.bfloat16)
    attention_init = (blank, blank, blank) + ()
    w_query = lax.all_gather(query_weight, ("dp", "seq"), axis=0, tiled=True)
    b_query = lax.all_gather(query_bias, ("dp", "seq"), axis=0, tiled=True)
    w_key = lax.all_gather(key_weight, ("dp", "seq"), axis=0, tiled=True)
    w_value = lax.all_gather(value_weight, ("dp", "seq"), axis=0, tiled=True)
    b_value = lax.all_gather(value_bias, ("dp", "seq"), axis=0, tiled=True)
    queries = place_cols(
        attention_init[0], project(first_rows, w_query) + b_query.astype(jnp.float32)
    )
    key_rows = place_cols(attention_init[1], project(first_rows, w_key))
    value_rows = place_cols(
        attention_init[2], project(first_rows, w_value) + b_value.astype(jnp.float32)
    )
    stored = attention_init[3:]
    gathered = (queries, key_rows, value_rows) + stored
    queries, key_rows, value_rows = (gathered[0], gathered[1], gathered[2])
    query_local = queries.reshape(seq_count, local_len, width)
    key_local = key_rows.reshape(seq_count, local_len, width)
    value_local = value_rows.reshape(seq_count, local_len, width)
    alive_local = active.reshape(seq_count, local_len)
    key_all, value_all, alive_all = (
        lax.all_gather(key_local, "seq", axis=1, tiled=True),
        lax.all_gather(value_local, "seq", axis=1, tiled=True),
        lax.all_gather(alive_local.astype(jnp.bfloat16), "seq", axis=1, tiled=True),
    )
    full_len = key_all.shape[1]
    offset = lax.axis_index("seq") * local_len
    query_pos = offset + jnp.arange(local_len, dtype=jnp.int32)
    key_pos = jnp.arange(full_len, dtype=jnp.int32)
    causal = key_pos[None, :] <= query_pos[:, None]
    allowed = causal[None, None] & (alive_all.astype(jnp.float32)[:, None, None, :] > 0.5)
    factor = HEAD_DIM ** (-0.5)
    group = min(8, heads)
    group_width = group * HEAD_DIM
    group_total = heads // group

    def group_parts(start_col):
        q_part = lax.dynamic_slice_in_dim(query_local, start_col, group_width, 2).reshape(
            seq_count, local_len, group, HEAD_DIM
        )
        k_part = lax.dynamic_slice_in_dim(key_all, start_col, group_width, 2).reshape(
            seq_count, full_len, group, HEAD_DIM
        )
        v_part = lax.dynamic_slice_in_dim(value_all, start_col, group_width, 2).reshape(
            seq_count, full_len, group, HEAD_DIM
        )
        scores = (
            jnp.einsum("sqhd,skhd->shqk", q_part, k_part, preferred_element_type=jnp.float32)
            * factor
        )
        scores = jnp.where(allowed, scores, jnp.float32(-1e30))
        return (q_part, k_part, v_part, scores)

    def forward_group(group_index, state):
        mixed_all, log_total = state
        start_col = group_index * group_width
        q_part, k_part, v_part, scores = group_parts(start_col)
        row_max = jnp.max(scores, axis=-1, keepdims=True)
        raised = jnp.exp(scores - row_max)
        totals = jnp.sum(raised, axis=-1, keepdims=True)
        weights_low = (raised / totals).astype(jnp.bfloat16)
        outcome = jnp.einsum(
            "shqk,skhd->sqhd", weights_low, v_part, preferred_element_type=jnp.float32
        )
        mixed_all = lax.dynamic_update_slice_in_dim(
            mixed_all,
            outcome.reshape(seq_count, local_len, group_width).astype(jnp.bfloat16),
            start_col,
            2,
        )
        log_total = lax.dynamic_update_slice_in_dim(
            log_total, (row_max + jnp.log(totals))[..., 0], group_index * group, 1
        )
        return (mixed_all, log_total)

    mixed_all, log_total = lax.fori_loop(
        0,
        group_total,
        forward_group,
        (
            jnp.zeros((seq_count, local_len, width), jnp.bfloat16),
            jnp.zeros((seq_count, heads, local_len), jnp.float32),
        ),
    )
    mixed = mixed_all.reshape(total_rows, width)
    vector_blank = jnp.zeros((width,), jnp.bfloat16)
    output_init = (jnp.zeros((total_rows, width), jnp.float32), vector_blank, vector_blank) + ()
    w_out = lax.all_gather(output_weight, ("dp", "seq"), axis=0, tiled=True)
    b_out = lax.all_gather(output_bias, ("dp", "seq"), axis=0, tiled=True)
    g_piece = lax.all_gather(second_gain, ("dp", "seq"), axis=0, tiled=True)
    s_piece = lax.all_gather(second_shift, ("dp", "seq"), axis=0, tiled=True)
    branch = place_cols(output_init[0], project(mixed, w_out) + b_out.astype(jnp.float32))
    gain_two = g_piece
    shift_two = s_piece
    stored = output_init[3:]
    folded = (branch, gain_two, shift_two) + stored
    branch = folded[0]
    gain_two = folded[1].astype(jnp.float32)
    shift_two = folded[2].astype(jnp.float32)
    middle = inputs + active * branch
    normed_mid = normalize(middle)
    second_rows = (normed_mid * gain_two + shift_two).astype(jnp.bfloat16)
    expand_init = (jnp.zeros((total_rows, hidden_width), jnp.float32),) + ()
    w_expand = lax.all_gather(expand_weight, ("dp", "seq"), axis=0, tiled=True)
    b_expand = lax.all_gather(expand_bias, ("dp", "seq"), axis=0, tiled=True)
    hidden_pre = place_cols(
        expand_init[0], project(second_rows, w_expand) + b_expand.astype(jnp.float32)
    )
    stored = expand_init[1:]
    expanded = (hidden_pre,) + stored
    hidden_pre = expanded[0]

    def gelu_exact(pre_values):
        return jax.nn.gelu(pre_values, approximate=False)

    activated_full, gelu_back = jax.vjp(gelu_exact, hidden_pre)
    activated = activated_full.astype(jnp.bfloat16)
    shrink_init = (jnp.zeros((total_rows, width), jnp.float32),) + ()
    w_shrink = lax.all_gather(shrink_weight, ("dp", "seq"), axis=0, tiled=True)
    b_shrink = lax.all_gather(shrink_bias, ("dp", "seq"), axis=0, tiled=True)
    shrunk = place_cols(shrink_init[0], project(activated, w_shrink) + b_shrink.astype(jnp.float32))
    stored = shrink_init[1:]
    shrunk_all = (shrunk,) + stored
    shrunk = shrunk_all[0]
    layer_out = (middle + active * shrunk).astype(jnp.bfloat16).reshape(seq_count, local_len, width)
    grad_out = cotangent.reshape(total_rows, width).astype(jnp.float32)
    grad_shrunk = (active * grad_out).astype(jnp.bfloat16)
    grad_units = through(
        grad_shrunk, lax.all_gather(shrink_weight, ("dp", "seq"), axis=0, tiled=True)
    )
    grad_pre = gelu_back(grad_units)[0].astype(jnp.bfloat16)
    grad_second = through(
        grad_pre, lax.all_gather(expand_weight, ("dp", "seq"), axis=0, tiled=True)
    )
    mid_value, mid_back = jax.vjp(normalize, middle)
    grad_middle = grad_out + mid_back(grad_second * gain_two)[0]
    grad_branch = (active * grad_middle).astype(jnp.bfloat16)
    grad_mixed = through(
        grad_branch, lax.all_gather(output_weight, ("dp", "seq"), axis=0, tiled=True)
    )
    grad_mixed_local = grad_mixed.astype(jnp.bfloat16).reshape(seq_count, local_len, width)

    def backward_group(group_index, state):
        grad_query_all, grad_key_all, grad_value_all = state
        start_col = group_index * group_width
        q_part, k_part, v_part, scores = group_parts(start_col)
        g_part = lax.dynamic_slice_in_dim(grad_mixed_local, start_col, group_width, 2).reshape(
            seq_count, local_len, group, HEAD_DIM
        )
        lse_part = lax.dynamic_slice_in_dim(log_total, group_index * group, group, 1)
        soft = jnp.exp(scores - lse_part[..., None])
        grad_probs = jnp.einsum(
            "sqhd,skhd->shqk", g_part, v_part, preferred_element_type=jnp.float32
        )
        value_term = jnp.einsum(
            "shqk,sqhd->skhd", soft.astype(jnp.bfloat16), g_part, preferred_element_type=jnp.float32
        )
        centered = jnp.sum(soft * grad_probs, axis=-1, keepdims=True)
        grad_scores = (soft * (grad_probs - centered)).astype(jnp.bfloat16)
        query_term = (
            jnp.einsum("shqk,skhd->sqhd", grad_scores, k_part, preferred_element_type=jnp.float32)
            * factor
        )
        key_term = (
            jnp.einsum("shqk,sqhd->skhd", grad_scores, q_part, preferred_element_type=jnp.float32)
            * factor
        )
        grad_query_all = lax.dynamic_update_slice_in_dim(
            grad_query_all, query_term.reshape(seq_count, local_len, group_width), start_col, 2
        )
        grad_key_all = lax.dynamic_update_slice_in_dim(
            grad_key_all, key_term.reshape(seq_count, full_len, group_width), start_col, 2
        )
        grad_value_all = lax.dynamic_update_slice_in_dim(
            grad_value_all, value_term.reshape(seq_count, full_len, group_width), start_col, 2
        )
        return (grad_query_all, grad_key_all, grad_value_all)

    grad_query_all, grad_key_all, grad_value_all = lax.fori_loop(
        0,
        group_total,
        backward_group,
        (
            jnp.zeros((seq_count, local_len, width), jnp.float32),
            jnp.zeros((seq_count, full_len, width), jnp.float32),
            jnp.zeros((seq_count, full_len, width), jnp.float32),
        ),
    )
    key_sum, value_sum = (
        lax.psum_scatter(grad_key_all, "seq", scatter_dimension=1, tiled=True),
        lax.psum_scatter(grad_value_all, "seq", scatter_dimension=1, tiled=True),
    )
    grad_query = grad_query_all.astype(jnp.bfloat16).reshape(total_rows, width)
    grad_key = key_sum.astype(jnp.bfloat16).reshape(total_rows, width)
    grad_value = value_sum.astype(jnp.bfloat16).reshape(total_rows, width)
    total = through(grad_query, lax.all_gather(query_weight, ("dp", "seq"), axis=0, tiled=True))
    total = total + through(grad_key, lax.all_gather(key_weight, ("dp", "seq"), axis=0, tiled=True))
    grad_first = total + through(
        grad_value, lax.all_gather(value_weight, ("dp", "seq"), axis=0, tiled=True)
    )
    in_value, in_back = jax.vjp(normalize, inputs)
    tokens_grad = (
        (grad_middle + in_back(grad_first * gain_one)[0])
        .astype(jnp.bfloat16)
        .reshape(seq_count, local_len, width)
    )
    first_scaled = grad_first * normed_in
    second_scaled = grad_second * normed_mid
    vectors = jnp.stack(
        [
            column_total(grad_query),
            column_total(grad_value),
            column_total(grad_branch),
            column_total(grad_shrunk),
            column_total(first_scaled),
            column_total(grad_first),
            column_total(second_scaled),
            column_total(grad_second),
        ],
        axis=1,
    )
    padding = jnp.zeros((query_weight.shape[0] * lax.axis_size(("dp", "seq")), 120), jnp.float32)
    width_sums = lax.psum_scatter(
        jnp.concatenate(
            [
                outer_rows(grad_query, first_rows),
                outer_rows(grad_key, first_rows),
                outer_rows(grad_value, first_rows),
                outer_rows(grad_branch, mixed),
                outer_rows(grad_shrunk, activated),
                vectors,
                padding,
            ],
            axis=1,
        ),
        ("dp", "seq"),
        scatter_dimension=0,
        tiled=True,
    )
    base = 4 * width + hidden_width
    padding = jnp.zeros((expand_weight.shape[0] * lax.axis_size(("dp", "seq")), 127), jnp.float32)
    hidden_sums = lax.psum_scatter(
        jnp.concatenate(
            [outer_rows(grad_pre, second_rows), column_total(grad_pre)[:, None], padding], axis=1
        ),
        ("dp", "seq"),
        scatter_dimension=0,
        tiled=True,
    )
    return (
        layer_out,
        tokens_grad,
        width_sums[:, base + 4],
        width_sums[:, base + 5],
        width_sums[:, 0:width],
        width_sums[:, base],
        width_sums[:, width : 2 * width],
        width_sums[:, 2 * width : 3 * width],
        width_sums[:, base + 1],
        width_sums[:, 3 * width : 4 * width],
        width_sums[:, base + 2],
        width_sums[:, base + 6],
        width_sums[:, base + 7],
        hidden_sums[:, 0:width],
        hidden_sums[:, width],
        width_sums[:, 4 * width : base],
        width_sums[:, base + 3],
    )


def solution(mesh):
    in_specs = (
        P("dp", "seq", None),
        P("dp", "seq"),
        P(("dp", "seq")),
        P(("dp", "seq")),
        P(("dp", "seq"), None),
        P(("dp", "seq")),
        P(("dp", "seq"), None),
        P(("dp", "seq"), None),
        P(("dp", "seq")),
        P(("dp", "seq"), None),
        P(("dp", "seq")),
        P(("dp", "seq")),
        P(("dp", "seq")),
        P(("dp", "seq"), None),
        P(("dp", "seq")),
        P(("dp", "seq"), None),
        P(("dp", "seq")),
        P("dp", "seq", None),
    )
    out_specs = (
        P("dp", "seq", None),
        P("dp", "seq", None),
        P(("dp", "seq")),
        P(("dp", "seq")),
        P(("dp", "seq"), None),
        P(("dp", "seq")),
        P(("dp", "seq"), None),
        P(("dp", "seq"), None),
        P(("dp", "seq")),
        P(("dp", "seq"), None),
        P(("dp", "seq")),
        P(("dp", "seq")),
        P(("dp", "seq")),
        P(("dp", "seq"), None),
        P(("dp", "seq")),
        P(("dp", "seq"), None),
        P(("dp", "seq")),
    )
    return jax.shard_map(
        per_device, mesh=mesh, in_specs=in_specs, out_specs=out_specs, check_vma=False
    )
```

profile of v0, /device:TPU:9, one launch (start us, length us, event | category | flops | bytes accessed | tf_op | source)
XLA Modules:
  0.0 4661.9 jit_solution(7962313743390446303)
XLA Ops:
  15.4 41.7 all-reduce.8
  59.9 30.2 all-gather.10.cloned.1.call-done
  104.4 64.7 %all-gather.16.cloned.1.call-done = bf16[2048,2048]{1,0:T(8,128)(2,1)} async-done(((bf16[64,2048]{1,0:T(8,128)(2,1)}), bf16[2048,2048]{1,0:T(8,128)(2,1)}) %all-gather.16.cloned.1.call-update) | async-done | bytes 8388624 | tf_op jit(solution)/shard_map/all_gather | solution.py:81
  186.9 59.2 %all-gather = bf16[32,1,256]{2,1,0:T(2,128)(2,1)S(1)} all-gather(bf16[1,1,256]{2,1,0:T(2,128)(2,1)S(1)} %reshape.355), channel_id=1, replica_groups=mesh['dp'=8,'seq'=4] {'dp','seq'}, dimensions={0}, use_global_device_ids=true | all-gather | bytes 16896 | tf_op jit(solution)/shard_map/all_gather | solution.py:182
  269.5 125.1 %all-gather.12.cloned.1.call-done = bf16[2,1024,2048]{1,2,0:T(8,128)(2,1)} async-done(((bf16[2,256,2048]{1,2,0:T(8,128)(2,1)}), bf16[2,1024,2048]{1,2,0:T(8,128)(2,1)}) %all-gather.12.cloned.1.call-update) | async-done | bytes 8388624 | tf_op jit(solution)/shard_map/all_gather | solution.py:100
  394.6 149.3 %all-gather.18.cloned.1.call-done = bf16[2,1024,2048]{1,2,0:T(8,128)(2,1)} async-done(((bf16[2,256,2048]{1,2,0:T(8,128)(2,1)}), bf16[2,1024,2048]{1,2,0:T(8,128)(2,1)}) %all-gather.18.cloned.1.call-update) | async-done | bytes 8388624 | tf_op jit(solution)/shard_map/all_gather | solution.py:99
  545.6 81.0 %while.34 = (s32[]{:T(128)}, bf16[2,256,2048]{2,1,0:T(8,128)(2,1)}, f32[2,32,256]{2,1,0:T(8,128)S(1)}, bf16[2,1024,2048]{1,2,0:T(8,128)(2,1)}, bf16[2,256,2048]{...) while((s32[]{:T(128)}, bf16[2,256,2048]{2,1,0:T(8,128)(2,1)}, ...), condition=%wide.region_5.6_spmd.clone, body=%wide.region_2.5_spmd.clone.sunk | while | flops 1124855808 | bytes 69601528 | solution.py:153
  637.9 182.4 %all-gather.22.cloned.1.call-done = bf16[8192,2048]{1,0:T(8,128)(2,1)} async-done(((bf16[256,2048]{1,0:T(8,128)(2,1)}), bf16[8192,2048]{1,0:T(8,128)(2,1)}) %all-gather.22.cloned.1.call-update) | async-done | bytes 33554448 | tf_op jit(solution)/shard_map/all_gather | solution.py:181
  820.3 26.0 fusion.50
  846.3 169.9 %all-gather.24.cloned.1.call-done = bf16[2048,8192]{1,0:T(8,128)(2,1)} async-done(((bf16[64,8192]{1,0:T(8,128)(2,1)}), bf16[2048,8192]{1,0:T(8,128)(2,1)}) %all-gather.24.cloned.1.call-update) | async-done | bytes 33554448 | tf_op jit(solution)/shard_map/all_gather | solution.py:196
  1016.3 60.6 %convert_reduce_fusion = (f32[8192]{0:T(1024)}, bf16[512,8192]{1,0:T(8,128)(2,1)S(1)}, f32[512,8192]{1,0:T(8,128)}) fusion(f32[512,8192]{1,0:T(8,128)} %fusion.50, f32[8192]{0:T(1024)S(1)} %bitcast.215, bf16[512,2048]{1,0:T(8,128)(2,1)S(1)} %copy-done.16, bf16[2048,8192]{1,0:T(8,128)(2,1)} %all-gather.24.cloned.1.call-done), kind=kOutput, calls=%fused_computation.38 | convolution fusion | flops 17494433792 | bytes 77660160 | tf_op jit(solution)/shard_map/dot_general | solution.py:26
  1076.9 26.4 multiply_reduce_fusion.1
  1132.5 276.1 %while.35 = (s32[]{:T(128)}, bf16[2,256,2048]{2,1,0:T(8,128)(2,1)}, f32[2,1024,2048]{2,1,0:T(8,128)}, f32[2,1024,2048]{2,1,0:T(8,128)}, bf16[2,1024,2048]{1,2,0:...) while((s32[]{:T(128)}, bf16[2,256,2048]{2,1,0:T(8,128)(2,1)}, ...), condition=%wide.region_12.13_spmd.clone, body=%wide.region_10.0_spmd.clone.sunk | while | flops 2749362176 | bytes 278776160 | solution.py:256
  1155.7 13.6 multiply_reduce_fusion.5
  1224.5 13.6 multiply_reduce_fusion.5
  1362.3 13.6 multiply_reduce_fusion.5
  1409.4 32.1 fusion.49
  1443.9 159.6 %concatenate.7 = f32[8192,2176]{0,1:T(8,128)} concatenate(f32[8192,2048]{0,1:T(8,128)} %fusion.49, f32[8192,1]{0,1:T(1,128)S(1)} %bitcast.221, f32[8192,127]{0,1:T(8,128)} %broadcast_in_dim.126), dimensions={1} | concatenate | bytes 142606336 | tf_op jit(solution)/shard_map/concatenate | solution.py:320
  1652.3 31.8 fusion.60
  1689.5 279.6 %reduce-scatter.7.cloned.1.call-done = f32[2,256,2048]{2,1,0:T(8,128)} async-done(((f32[2,1024,2048]{2,1,0:T(8,128)}), f32[2,256,2048]{2,1,0:T(8,128)}) %reduce-scatter.7.cloned.1.call-update) | async-done | bytes 4194320 | tf_op jit(solution)/shard_map/reduce_scatter | solution.py:268
  2013.1 174.7 %concatenate.6 = f32[2048,16512]{1,0:T(8,128)} concatenate(f32[2048,2048]{1,0:T(8,128)} %convolution_bitcast_fusion.2, f32[2048,2048]{1,0:T(8,128)} %convolution_bitcast_fusion.1, f32[2048,2048]{1,0:T(8,128)} %convolution_bitcast_fusion, f32[2048,2048]{1,0:T(8,128)} %fusion.59, f32[2048,8192]{1,0:T(8,128)} %fusion.60, f32[2048,1]{1,0:T(8,128)} %copy.92, f32[2048,1]{1,0:T(8,128)} %copy.93, ...), dimensions={1} | concatenate | bytes 270532608 | tf_op jit(solution)/shard_map/concatenate | solution.py:301
  2188.6 25.3 add_convert_fusion.2
  2218.8 1251.3 %reduce-scatter.11.cloned.1.call-done = f32[256,2176]{0,1:T(8,128)} async-done(((f32[8192,2176]{0,1:T(8,128)}), f32[256,2176]{0,1:T(8,128)}) %reduce-scatter.11.cloned.1.call-update) | async-done | bytes 2228240 | tf_op jit(solution)/shard_map/reduce_scatter | solution.py:319
  3474.8 1172.1 %reduce-scatter.9.cloned.1.call-done = f32[64,16512]{1,0:T(8,128)} async-done(((f32[2048,16512]{1,0:T(8,128)}), f32[64,16512]{1,0:T(8,128)}) %reduce-scatter.9.cloned.1.call-update) | async-done | bytes 4227088 | tf_op jit(solution)/shard_map/reduce_scatter | solution.py:300
  (440 shorter events, 542.7 us)
Async XLA Ops:
  7.3 82.9 %all-gather.10.cloned.1.call-start = ((), (), s32[]{:S(2)}) async-start(), calls=%async_computation.4 | async-start | bytes 8650752 | tf_op jit(solution)/shard_map/all_gather | solution.py:82
  8.0 161.1 %all-gather.16.cloned.1.call-start = ((), (), s32[]{:S(2)}) async-start(), calls=%async_computation.7 | async-start | bytes 8650752 | tf_op jit(solution)/shard_map/all_gather | solution.py:81
  8.8 248.7 %all-gather.14.cloned.1.call-start = ((), (), s32[]{:S(2)}) async-start(), calls=%async_computation.6 | async-start | bytes 8650752 | tf_op jit(solution)/shard_map/all_gather | solution.py:79
  9.5 385.1 %all-gather.12.cloned.1.call-start = ((), (), s32[]{:S(2)}) async-start(), calls=%async_computation.5 | async-start | bytes 10485760 | tf_op jit(solution)/shard_map/all_gather | solution.py:100
  11.5 88.5 %copy-start.36 = (f32[1,2,2,128]{3,1,2,0:T(2,128)}, f32[1,2,2,128]{3,1,2,0:T(2,128)S(1)}, u32[]{:S(2)}) copy-start(f32[1,2,2,128]{3,1,2,0:T(2,128)S(1)} %copy.138) | copy-start | bytes 6148
  13.4 86.6 %copy-start.39 = (f32[512]{0:T(512)}, f32[512]{0:T(512)S(1)}, u32[]{:S(2)}) copy-start(f32[512]{0:T(512)S(1)} %rsqrt.25) | copy-start | bytes 6148
  104.2 439.8 %all-gather.18.cloned.1.call-start = ((), (), s32[]{:S(2)}) async-start(), calls=%async_computation.8 | async-start | bytes 10485760 | tf_op jit(solution)/shard_map/all_gather | solution.py:99
  182.4 444.3 %all-gather.20.cloned.1.call-start = ((), (), s32[]{:S(2)}) async-start(), calls=%async_computation.9 | async-start | bytes 8650752 | tf_op jit(solution)/shard_map/all_gather | solution.py:165
  182.9 637.4 %all-gather.22.cloned.1.call-start = ((), (), s32[]{:S(2)}) async-start(), calls=%async_computation.10 | async-start | bytes 34603008 | tf_op jit(solution)/shard_map/all_gather | solution.py:181
  183.7 832.6 %all-gather.24.cloned.1.call-start = ((), (), s32[]{:S(2)}) async-start(), calls=%async_computation.11 | async-start | bytes 34603008 | tf_op jit(solution)/shard_map/all_gather | solution.py:196
  184.4 1501.2 %reduce-scatter.5.cloned.1.call-start = ((), (), s32[]{:S(2)}) async-start(), calls=%async_computation.12 | async-start | bytes 20971520 | tf_op jit(solution)/shard_map/reduce_scatter | solution.py:267
  185.1 81.5 %copy-start.54 = (f32[1,2,2,128]{3,1,2,0:T(2,128)}, f32[1,2,2,128]{3,1,2,0:T(2,128)S(1)}, u32[]{:S(2)}) copy-start(f32[1,2,2,128]{3,1,2,0:T(2,128)S(1)} %copy.137) | copy-start | bytes 6148
  545.6 81.1 %copy-start.2 = (bf16[2,256,2048]{2,1,0:T(8,128)(2,1)S(1)}, bf16[2,256,2048]{2,1,0:T(8,128)(2,1)}, u32[]{:S(2)}) copy-start(bf16[2,256,2048]{2,1,0:T(8,128)(2,1)} %param.22) | copy-start | bytes 6291460
  545.6 81.1 %copy-start.55 = (f32[1,2,2,128]{3,1,2,0:T(2,128)S(1)}, f32[1,2,2,128]{3,1,2,0:T(2,128)}, u32[]{:S(2)}) copy-start(f32[1,2,2,128]{3,1,2,0:T(2,128)} %copy-done.54) | copy-start | bytes 6148
  545.6 81.1 %copy-start.70 = (f32[2048]{0:T(1024)S(1)}, f32[2048]{0:T(1024)}, u32[]{:S(2)}) copy-start(f32[2048]{0:T(1024)} %convert_element_type.177) | copy-start | bytes 24580
  634.7 185.6 %copy-start.46 = (f32[2048]{0:T(1024)S(1)}, f32[2048]{0:T(1024)}, u32[]{:S(2)}) copy-start(f32[2048]{0:T(1024)} %convert_element_type.178) | copy-start | bytes 24580
  634.7 185.6 %copy-start.68 = (f32[2048]{0:T(1024)S(1)}, f32[2048]{0:T(1024)}, u32[]{:S(2)}) copy-start(f32[2048]{0:T(1024)} %convert_element_type.179) | copy-start | bytes 24580
  634.8 468.5 %copy-start.48 = (f32[512]{0:T(512)}, f32[512]{0:T(512)S(1)}, u32[]{:S(2)}) copy-start(f32[512]{0:T(512)S(1)} %broadcast_multiply_fusion) | copy-start | bytes 6148
  637.9 465.4 %copy-start.65 = (f32[512]{0:T(512)}, f32[512]{0:T(512)S(1)}, u32[]{:S(2)}) copy-start(f32[512]{0:T(512)S(1)} %fusion.42) | copy-start | bytes 6148
  637.9 378.4 %copy-start.16 = (bf16[512,2048]{1,0:T(8,128)(2,1)S(1)}, bf16[512,2048]{1,0:T(8,128)(2,1)}, u32[]{:S(2)}) copy-start(bf16[512,2048]{1,0:T(8,128)(2,1)} %fusion.23) | copy-start | bytes 6291460
  637.9 378.4 %copy-start.34 = (f32[32,1,256]{2,1,0:T(1,128)S(1)}, f32[32,1,256]{2,1,0:T(1,128)}, u32[]{:S(2)}) copy-start(f32[32,1,256]{2,1,0:T(1,128)} %convert_element_type.205) | copy-start | bytes 98308
  1408.6 560.4 %reduce-scatter.7.cloned.1.call-start = ((), (), s32[]{:S(2)}) async-start(), calls=%async_computation.13 | async-start | bytes 20971520 | tf_op jit(solution)/shard_map/reduce_scatter | solution.py:268
  1409.2 2060.9 %reduce-scatter.11.cloned.1.call-start = ((), (), s32[]{:S(2)}) async-start(), calls=%async_computation.15 | async-start | bytes 73531392 | tf_op jit(solution)/shard_map/reduce_scatter | solution.py:319
  1603.6 3043.2 %reduce-scatter.9.cloned.1.call-start = ((), (), s32[]{:S(2)}) async-start(), calls=%async_computation.14 | async-start | bytes 139493376 | tf_op jit(solution)/shard_map/reduce_scatter | solution.py:300
  (95 other events, 941.1 us)
Sparse Core Ops, SparseCore 0:
  11.0 79.0 all-gather.9
  93.1 75.9 all-gather.15
  172.0 76.1 all-gather.13
  250.2 144.4 all-gather.11
  396.6 147.3 all-gather.17
  546.8 79.0 all-gather.19
  628.8 191.4 all-gather.21
  823.3 192.9 all-gather.23
  1408.7 276.8 reduce-scatter.4
  1688.0 281.0 reduce-scatter.6
  1971.4 1498.6 reduce-scatter.10
  3476.4 1170.4 reduce-scatter.8
where the time goes:
time: 4680 us; the launch traced here: 4660 us
  waiting for transfers between devices  3430 us (73%)
  local copies, waits for them, and re-layouts  538 us (11%)
  matrix products  460 us (10%)
  blocking collectives  110 us (2%)
  other arithmetic  107 us (2%)
    reduce_scatter x1, waiting for transfers between devices, per_device(): lax.psum_scatter(jnp.concatenate([outer_rows(grad_pre, second_rows), colu...  1250 us
    reduce_scatter x1, waiting for transfers between devices, per_device(): lax.psum_scatter(jnp.concatenate([outer_rows(grad_query, first_rows), out...  1170 us
    reduce_scatter x1, waiting for transfers between devices, per_device(): lax.psum_scatter(grad_value_all, 'seq', scatter_dimension=1, tiled=True)  280 us
    all_gather x1, waiting for transfers between devices, per_device(): w_expand = lax.all_gather(expand_weight, ('dp', 'seq'), axis=0, tiled=True)  182 us
    concatenate x1, local copies, waits for them, and re-layouts, per_device(): jnp.concatenate([outer_rows(grad_query, first_rows), outer_rows(grad_key,...  175 us
    all_gather x1, waiting for transfers between devices, per_device(): w_shrink = lax.all_gather(shrink_weight, ('dp', 'seq'), axis=0, tiled=True)  170 us
    concatenate x1, local copies, waits for them, and re-layouts, per_device(): jnp.concatenate([outer_rows(grad_pre, second_rows), column_total(grad_pre...  160 us
    all_gather x1, waiting for transfers between devices, per_device(): lax.all_gather(key_local, 'seq', axis=1, tiled=True)  149 us
  transfers between devices with their start and end apart: 12, of which 10 were waited for; matrix products, arithmetic and copies ran while one was open for 15% of the time, Pallas kernels for 0%

commit v1 on v0

--- a/solution.py
+++ b/solution.py
@@ -1,6 +1,10 @@
+import math
+
 import jax
 import jax.numpy as jnp
 from jax import lax
+from jax.experimental import pallas as pl
+from jax.experimental.pallas import tpu as pltpu
 from jax.sharding import PartitionSpec as P
 
 HEAD_DIM = 64
@@ -40,7 +44,474 @@
     return jnp.sum(matrix, axis=0, dtype=jnp.float32)
 
 
-def per_device(
+def swap(values, bit):
+    size = lax.axis_size("dp")
+    return lax.ppermute(values, "dp", [(i, i ^ bit) for i in range(size)])
+
+
+CORE, ALONG_X, ALONG_Y = 1, 2, 4
+
+
+def pick(flag, first, second):
+    return jnp.where(flag == 0, first, second)
+
+
+def ordered(flag, own, other, axis):
+    return pick(
+        flag, jnp.concatenate([own, other], axis), jnp.concatenate([other, own], axis)
+    )
+
+
+def arrange_kernel(place_ref, own, beside, across, corner, out, sems):
+    copies = [
+        pltpu.make_async_copy(piece, out.at[place_ref[0] ^ index], sems.at[index])
+        for index, piece in enumerate((own, beside, across, corner))
+    ]
+    for copy in copies:
+        copy.start()
+    for copy in copies:
+        copy.wait()
+
+
+def arrange(place, pieces):
+    shape = pieces[0].shape
+    size = 4 * math.prod(shape) * pieces[0].dtype.itemsize
+    return pl.pallas_call(
+        arrange_kernel,
+        out_shape=jax.ShapeDtypeStruct((4,) + shape, pieces[0].dtype),
+        in_specs=[pl.BlockSpec(memory_space=pltpu.SMEM)]
+        + [pl.BlockSpec(memory_space=pl.ANY)] * 4,
+        out_specs=pl.BlockSpec(memory_space=pl.ANY),
+        scratch_shapes=[pltpu.SemaphoreType.DMA((4,))],
+        cost_estimate=pl.CostEstimate(flops=0, bytes_accessed=2 * size, transcendentals=0),
+        name="arrange",
+    )(place.reshape(1), *pieces)
+
+
+def spread(values, place, corner_by):
+    beside = swap(values, ALONG_X)
+    across = swap(values, ALONG_Y)
+    corner = swap(beside, ALONG_Y) if corner_by == ALONG_Y else swap(across, ALONG_X)
+    return arrange(place, (values, beside, across, corner))
+
+
+def total_plane(pieces, corner_by):
+    own, beside, across, corner = pieces
+    if corner_by == ALONG_Y:
+        beside = add_low(beside, swap(corner, ALONG_Y))
+    else:
+        across = add_low(across, swap(corner, ALONG_X))
+    got_x = swap(beside, ALONG_X)
+    got_y = swap(across, ALONG_Y)
+    return (
+        own.astype(jnp.float32) + got_x.astype(jnp.float32) + got_y.astype(jnp.float32)
+    ).astype(jnp.bfloat16)
+
+
+def add_low(left, right):
+    return (left.astype(jnp.float32) + right.astype(jnp.float32)).astype(jnp.bfloat16)
+
+
+BLOCK = 256
+
+
+def softmax_block(index, keys_wide, query_wide):
+    start = index * BLOCK
+    tiles = []
+    if index > 0:
+        tiles.append(
+            lax.dot_general(
+                keys_wide[:start],
+                query_wide,
+                (((1,), (1,)), ((), ())),
+                preferred_element_type=jnp.float32,
+            )
+        )
+    last = lax.dot_general(
+        keys_wide[start : start + BLOCK],
+        query_wide,
+        (((1,), (1,)), ((), ())),
+        preferred_element_type=jnp.float32,
+    )
+    key_pos = lax.broadcasted_iota(jnp.int32, last.shape, 0)
+    query_pos = lax.broadcasted_iota(jnp.int32, last.shape, 1)
+    tiles.append(jnp.where(key_pos <= query_pos, last, jnp.float32(-1e30)))
+    peak = jnp.max(tiles[-1], axis=0, keepdims=True)
+    if index > 0:
+        peak = jnp.maximum(peak, jnp.max(tiles[0], axis=0, keepdims=True))
+    tiles = [jnp.exp(tile - peak) for tile in tiles]
+    total = sum(jnp.sum(tile, axis=0, keepdims=True) for tile in tiles)
+    inverse = 1.0 / total
+    return [tile * inverse for tile in tiles]
+
+
+def widen(head, rows_ref, mask_ref):
+    first = 3 * HEAD_DIM * head
+    query = rows_ref[:, first : first + HEAD_DIM] * jnp.bfloat16(HEAD_DIM**-0.5)
+    keys = rows_ref[:, first + HEAD_DIM : first + 2 * HEAD_DIM]
+    values = rows_ref[:, first + 2 * HEAD_DIM : first + 3 * HEAD_DIM]
+    even = jnp.full(query.shape, 1.0 / HEAD_DIM, jnp.bfloat16)
+    query_wide = jnp.concatenate([query, even], axis=1)
+    keys_wide = jnp.concatenate([keys, mask_ref[...]], axis=1)
+    return query, keys, values, query_wide, keys_wide
+
+
+def attend_kernel(rows_ref, mask_ref, out_ref):
+    blocks = rows_ref.shape[0] // BLOCK
+    results = [[], []]
+    for head in range(2):
+        _, _, values, query_wide, keys_wide = widen(head, rows_ref, mask_ref)
+        for index in range(blocks):
+            start, stop = index * BLOCK, (index + 1) * BLOCK
+            tiles = softmax_block(index, keys_wide, query_wide[start:stop])
+            low = jnp.concatenate([tile.astype(jnp.bfloat16) for tile in tiles], axis=0)
+            outcome = lax.dot_general(
+                values[:stop], low, (((0,), (0,)), ((), ())), preferred_element_type=jnp.float32
+            )
+            results[head].append(outcome.T)
+    for index in range(blocks):
+        both = jnp.concatenate([results[0][index], results[1][index]], axis=1)
+        out_ref[index * BLOCK : (index + 1) * BLOCK, :] = both.astype(jnp.bfloat16)
+
+
+def attend_back_kernel(rows_ref, grad_ref, mask_ref, out_ref, key_sum, value_sum):
+    blocks = rows_ref.shape[0] // BLOCK
+    columns = []
+    for head in range(2):
+        query, keys, values, query_wide, keys_wide = widen(head, rows_ref, mask_ref)
+        grad = grad_ref[:, head * HEAD_DIM : (head + 1) * HEAD_DIM]
+        query_parts = []
+        for index in reversed(range(blocks)):
+            start, stop = index * BLOCK, (index + 1) * BLOCK
+            tiles = softmax_block(index, keys_wide, query_wide[start:stop])
+            soft = jnp.concatenate(tiles, axis=0)
+            grad_rows = grad[start:stop]
+            grad_probs = lax.dot_general(
+                values[:stop],
+                grad_rows,
+                (((1,), (1,)), ((), ())),
+                preferred_element_type=jnp.float32,
+            )
+            weighted = soft * grad_probs
+            delta = jnp.sum(weighted, axis=0, keepdims=True)
+            grad_scores = (weighted - soft * delta).astype(jnp.bfloat16)
+            value_term = jnp.dot(
+                soft.astype(jnp.bfloat16), grad_rows, preferred_element_type=jnp.float32
+            )
+            key_term = jnp.dot(
+                grad_scores, query[start:stop], preferred_element_type=jnp.float32
+            )
+            if index == blocks - 1:
+                value_sum[...] = value_term
+                key_sum[...] = key_term
+            else:
+                value_sum[:stop, :] += value_term
+                key_sum[:stop, :] += key_term
+            outcome = lax.dot_general(
+                keys[:stop],
+                grad_scores,
+                (((0,), (0,)), ((), ())),
+                preferred_element_type=jnp.float32,
+            )
+            query_parts.insert(0, outcome.T * jnp.float32(HEAD_DIM**-0.5))
+        columns += [jnp.concatenate(query_parts, axis=0), key_sum[...], value_sum[...]]
+    out_ref[...] = jnp.concatenate([part.astype(jnp.bfloat16) for part in columns], axis=1)
+
+
+def attend(rows, mask):
+    count, columns = rows.shape
+    pairs = columns // (6 * HEAD_DIM)
+    work = pairs * 2 * count * count * HEAD_DIM
+    return pl.pallas_call(
+        attend_kernel,
+        grid=(pairs,),
+        in_specs=[
+            pl.BlockSpec((count, 6 * HEAD_DIM), lambda i: (0, i)),
+            pl.BlockSpec((count, HEAD_DIM), lambda i: (0, 0)),
+        ],
+        out_specs=pl.BlockSpec((count, 2 * HEAD_DIM), lambda i: (0, i)),
+        out_shape=jax.ShapeDtypeStruct((count, pairs * 2 * HEAD_DIM), jnp.bfloat16),
+        compiler_params=pltpu.CompilerParams(vmem_limit_bytes=48 << 20),
+        cost_estimate=pl.CostEstimate(
+            flops=16 * work, bytes_accessed=8 * count * columns, transcendentals=0
+        ),
+        name="attend",
+    )(rows, mask)
+
+
+def attend_back(rows, grad, mask):
+    count, columns = rows.shape
+    pairs = columns // (6 * HEAD_DIM)
+    work = pairs * 2 * count * count * HEAD_DIM
+    return pl.pallas_call(
+        attend_back_kernel,
+        grid=(pairs,),
+        in_specs=[
+            pl.BlockSpec((count, 6 * HEAD_DIM), lambda i: (0, i)),
+            pl.BlockSpec((count, 2 * HEAD_DIM), lambda i: (0, i)),
+            pl.BlockSpec((count, HEAD_DIM), lambda i: (0, 0)),
+        ],
+        out_specs=pl.BlockSpec((count, 6 * HEAD_DIM), lambda i: (0, i)),
+        out_shape=jax.ShapeDtypeStruct((count, columns), jnp.bfloat16),
+        scratch_shapes=[pltpu.VMEM((count, HEAD_DIM), jnp.float32)] * 2,
+        compiler_params=pltpu.CompilerParams(vmem_limit_bytes=48 << 20),
+        cost_estimate=pl.CostEstimate(
+            flops=40 * work, bytes_accessed=8 * count * columns, transcendentals=0
+        ),
+        name="attend_back",
+    )(rows, grad, mask)
+
+
+def normal_parts(values):
+    center = values - jnp.mean(values, axis=-1, keepdims=True)
+    spread_of = jnp.mean(center * center, axis=-1, keepdims=True)
+    scale = lax.rsqrt(spread_of + EPS)
+    return center * scale, scale
+
+
+def normal_back(normed, scale, grad):
+    mean_grad = jnp.mean(grad, axis=-1, keepdims=True)
+    mean_product = jnp.mean(grad * normed, axis=-1, keepdims=True)
+    return (grad - mean_grad - normed * mean_product) * scale
+
+
+def whole_sequence_device(
+    tokens,
+    exit_layer,
+    first_gain,
+    first_shift,
+    query_weight,
+    query_bias,
+    key_weight,
+    value_weight,
+    value_bias,
+    output_weight,
+    output_bias,
+    second_gain,
+    second_shift,
+    expand_weight,
+    expand_bias,
+    shrink_weight,
+    shrink_bias,
+    cotangent,
+):
+    seq_count, local_len, width = tokens.shape
+    heads_rows = query_weight.shape[0]
+    hidden_rows = expand_weight.shape[0]
+    dp_size, seq_size = lax.axis_size("dp"), lax.axis_size("seq")
+    dp, depth = lax.axis_index("dp"), lax.axis_index("seq")
+    core, place = dp % 2, dp // 2
+    parity = depth % 2
+    full_len = local_len * seq_size
+    half_len = full_len // 2
+    f32, low = jnp.float32, jnp.bfloat16
+
+    def route(flip):
+        pairs = []
+        for i in range(dp_size):
+            for j in range(seq_size):
+                target = 2 * (i % 2) + (j % 2 if not flip else 1 - j % 2)
+                pairs.append((i * seq_size + j, (i // 2 * 2 + j // 2) * seq_size + target))
+        return pairs
+
+    def to_chips(values):
+        first = pick(parity, values[0], values[1])
+        second = pick(parity, values[1], values[0])
+        first = lax.ppermute(first, ("dp", "seq"), route(False))
+        second = lax.ppermute(second, ("dp", "seq"), route(True))
+        half = ordered(parity, first[None], second[None], 0)
+        return ordered(core, half, swap(half, CORE), 0)
+
+    def from_chips(half):
+        half = half.reshape(2, local_len, width)
+        first = pick(parity, half[0], half[1])
+        second = pick(parity, half[1], half[0])
+        first = lax.ppermute(first, ("dp", "seq"), [(b, a) for a, b in route(False)])
+        second = lax.ppermute(second, ("dp", "seq"), [(b, a) for a, b in route(True)])
+        return ordered(parity, first[None], second[None], 0)
+
+    alive = (exit_layer > LAYER).astype(low)
+    flag_rows = jnp.broadcast_to(alive[:, None, :], (seq_count, 16, local_len))
+    flag_rows = jnp.pad(flag_rows, ((0, 0), (0, 0), (0, width - local_len)))
+    arrived = to_chips(jnp.concatenate([tokens, flag_rows], axis=1))
+    inputs = arrived[:, :local_len].reshape(full_len, width).astype(f32)
+    alive = arrived[:, local_len, :local_len].reshape(full_len, 1)
+    active = alive.astype(f32)
+    mask = jnp.broadcast_to((alive - 1) * jnp.bfloat16(1e30), (full_len, HEAD_DIM))
+    cotangent_full = to_chips(cotangent).reshape(full_len, width)
+
+    vectors = jnp.concatenate(
+        [
+            first_gain,
+            first_shift,
+            query_bias,
+            value_bias,
+            output_bias,
+            second_gain,
+            second_shift,
+            shrink_bias,
+            expand_bias,
+        ]
+    )
+    vectors = lax.all_gather(vectors, ("dp", "seq"), axis=0, tiled=True)
+    vectors = vectors.reshape(dp_size * seq_size, -1).astype(f32)
+
+    def vector(index):
+        return vectors[:, index * heads_rows : (index + 1) * heads_rows].reshape(-1)
+
+    def of_core(matrix):
+        cut = matrix.reshape(4, 2, seq_size, -1)
+        return lax.dynamic_index_in_dim(cut, core, 1, False).reshape(4 * seq_size, -1)
+
+    gain_one, shift_one = vector(0), vector(1)
+    bias_query = of_core(vectors[:, 2 * heads_rows : 3 * heads_rows])
+    bias_value = of_core(vectors[:, 3 * heads_rows : 4 * heads_rows])
+    bias_rows = jnp.stack([bias_query, jnp.zeros_like(bias_query), bias_value], 1).reshape(-1)
+    bias_out, gain_two, shift_two, bias_shrink = vector(4), vector(5), vector(6), vector(7)
+    bias_expand = of_core(vectors[:, 8 * heads_rows :]).reshape(-1)
+
+    def through_z(shard):
+        return lax.all_gather(shard, "seq", axis=0, tiled=True)
+
+    def core_columns(rows):
+        cut = rows.reshape(rows.shape[0], 4, 2, -1)
+        mine = lax.dynamic_index_in_dim(cut, core, 2, False).reshape(rows.shape[0], -1)
+        theirs = lax.dynamic_index_in_dim(cut, 1 - core, 2, False).reshape(rows.shape[0], -1)
+        return ordered(core, mine, swap(theirs, CORE), 0)
+
+    w_qkv = spread(
+        through_z(jnp.concatenate([query_weight, key_weight, value_weight], 0)), place, ALONG_X
+    ).reshape(-1, width)
+    w_out = spread(core_columns(through_z(output_weight)), place, ALONG_Y).reshape(width, -1)
+    w_expand = spread(through_z(expand_weight), place, ALONG_X).reshape(-1, width)
+    w_shrink = spread(core_columns(through_z(shrink_weight)), place, ALONG_Y).reshape(width, -1)
+
+    normed_in, scale_in = normal_parts(inputs)
+    first_rows = (normed_in * gain_one + shift_one).astype(low)
+    qkv = (project(first_rows, w_qkv) + bias_rows).astype(low)
+    mixed = attend(qkv, mask)
+
+    def both_cores(left, weight, dot):
+        parts = []
+        for start in (0, half_len):
+            own = dot(left[start : start + half_len], weight).astype(low)
+            parts.append(own.astype(f32) + swap(own, CORE).astype(f32))
+        return jnp.concatenate(parts, 0)
+
+    def half_rows(matrix, which):
+        return lax.dynamic_slice_in_dim(matrix, which * half_len, half_len, 0)
+
+    def own_half(left, weight, dot):
+        got = swap(dot(half_rows(left, 1 - core), weight).astype(low), CORE)
+        return dot(half_rows(left, core), weight) + got.astype(f32)
+
+    branch = both_cores(mixed, w_out, project) + bias_out
+    middle = inputs + active * branch
+    normed_mid, scale_mid = normal_parts(middle)
+    second_rows = (normed_mid * gain_two + shift_two).astype(low)
+    hidden_pre = project(second_rows, w_expand) + bias_expand
+    lifted = 0.5 * (1.0 + lax.erf(hidden_pre * (0.5**0.5)))
+    activated = (hidden_pre * lifted).astype(low)
+    slope = lifted + hidden_pre * jnp.exp(-0.5 * hidden_pre * hidden_pre) * ((0.5 / math.pi) ** 0.5)
+    slope = slope.astype(low)
+    shrunk = own_half(activated, w_shrink, project) + bias_shrink
+    out_half = (half_rows(middle, core) + half_rows(active, core) * shrunk).astype(low)
+    layer_out = from_chips(out_half)
+
+    def plane_pieces(matrix):
+        cut = matrix.reshape(matrix.shape[0], 4, -1)
+        return [lax.dynamic_index_in_dim(cut, place ^ d, 1, False) for d in range(4)]
+
+    def z_major(matrix):
+        cut = matrix.reshape(matrix.shape[0], 2, seq_size, heads_rows)
+        return cut.reshape(matrix.shape[0], -1)
+
+    def rows_total(grad, inputs_low, corner_by):
+        pieces = [outer_rows(part, inputs_low).astype(low) for part in plane_pieces(grad)]
+        return total_plane(pieces, corner_by)
+
+    def join_cores(total):
+        cut = total.reshape(2, -1, total.shape[1])
+        mine = lax.dynamic_index_in_dim(cut, core, 0, False)
+        theirs = swap(lax.dynamic_index_in_dim(cut, 1 - core, 0, False), CORE)
+        mine, theirs = (part.reshape(part.shape[0], 4, 1, -1) for part in (mine, theirs))
+        return ordered(core, mine, theirs, 2).reshape(mine.shape[0], -1)
+
+    def scatter_z(total):
+        return lax.psum_scatter(total, "seq", scatter_dimension=0, tiled=True).astype(f32)
+
+    grad_out = cotangent_full.astype(f32)
+    grad_shrunk = (active * grad_out).astype(low)
+    grad_units = through(grad_shrunk, w_shrink)
+    grad_pre = (grad_units * slope.astype(f32)).astype(low)
+    shrink_weight_grad = scatter_z(join_cores(rows_total(grad_shrunk, activated, ALONG_Y)))
+    grad_second = both_cores(grad_pre, w_expand, through)
+    expand_weight_grad = scatter_z(rows_total(grad_pre, second_rows, ALONG_X))
+    grad_middle = grad_out + normal_back(normed_mid, scale_mid, grad_second * gain_two)
+    grad_branch = (active * grad_middle).astype(low)
+    grad_mixed = through(grad_branch, w_out).astype(low)
+    output_weight_grad = scatter_z(join_cores(rows_total(grad_branch, mixed, ALONG_Y)))
+    grad_qkv = attend_back(qkv, grad_mixed, mask)
+    qkv_weight_grad = scatter_z(rows_total(grad_qkv, first_rows, ALONG_X))
+    grad_first = own_half(grad_qkv, w_qkv, through)
+    normed_half, scale_half = half_rows(normed_in, core), half_rows(scale_in, core)
+    grad_half = half_rows(grad_middle, core) + normal_back(
+        normed_half, scale_half, grad_first * gain_one
+    )
+    tokens_grad = from_chips(grad_half.astype(low))
+
+    def column_sum(matrix):
+        return jnp.sum(matrix.astype(f32), axis=0)
+
+    def all_devices(totals, rows):
+        return totals.reshape(dp_size * seq_size, rows)
+
+    def core_devices(totals, rows):
+        cut = totals.reshape(4, 1, seq_size, rows)
+        return ordered(core, cut, jnp.zeros_like(cut), 1).reshape(dp_size * seq_size, rows)
+
+    qkv_sums = column_sum(grad_qkv).reshape(4 * seq_size, 3, heads_rows)
+    sums = jnp.concatenate(
+        [
+            all_devices(column_sum(grad_first * normed_half), heads_rows),
+            all_devices(column_sum(grad_first), heads_rows),
+            core_devices(qkv_sums[:, 0], heads_rows),
+            core_devices(qkv_sums[:, 2], heads_rows),
+            all_devices(0.5 * column_sum(grad_branch), heads_rows),
+            all_devices(0.5 * column_sum(grad_second * normed_mid), heads_rows),
+            all_devices(0.5 * column_sum(grad_second), heads_rows),
+            all_devices(0.5 * column_sum(grad_shrunk), heads_rows),
+            core_devices(column_sum(grad_pre), hidden_rows),
+        ],
+        axis=1,
+    )
+    sums = lax.psum_scatter(sums.reshape(-1), ("dp", "seq"), scatter_dimension=0, tiled=True)
+
+    def vector_grad(index):
+        return sums[index * heads_rows : (index + 1) * heads_rows]
+
+    return (
+        layer_out,
+        tokens_grad,
+        vector_grad(0),
+        vector_grad(1),
+        qkv_weight_grad[:heads_rows],
+        vector_grad(2),
+        qkv_weight_grad[heads_rows : 2 * heads_rows],
+        qkv_weight_grad[2 * heads_rows :],
+        vector_grad(3),
+        output_weight_grad,
+        vector_grad(4),
+        vector_grad(5),
+        vector_grad(6),
+        expand_weight_grad,
+        sums[8 * heads_rows :],
+        shrink_weight_grad,
+        vector_grad(7),
+    )
+
+
+def general_device(
     tokens,
     exit_layer,
     first_gain,
@@ -296,52 +767,42 @@
         ],
         axis=1,
     )
-    padding = jnp.zeros((query_weight.shape[0] * lax.axis_size(("dp", "seq")), 120), jnp.float32)
-    width_sums = lax.psum_scatter(
-        jnp.concatenate(
-            [
-                outer_rows(grad_query, first_rows),
-                outer_rows(grad_key, first_rows),
-                outer_rows(grad_value, first_rows),
-                outer_rows(grad_branch, mixed),
-                outer_rows(grad_shrunk, activated),
-                vectors,
-                padding,
-            ],
-            axis=1,
-        ),
-        ("dp", "seq"),
-        scatter_dimension=0,
-        tiled=True,
-    )
-    base = 4 * width + hidden_width
-    padding = jnp.zeros((expand_weight.shape[0] * lax.axis_size(("dp", "seq")), 127), jnp.float32)
-    hidden_sums = lax.psum_scatter(
-        jnp.concatenate(
-            [outer_rows(grad_pre, second_rows), column_total(grad_pre)[:, None], padding], axis=1
-        ),
-        ("dp", "seq"),
-        scatter_dimension=0,
-        tiled=True,
+
+    def scattered(grad_cols, inputs):
+        return lax.psum_scatter(
+            outer_rows(grad_cols, inputs), ("dp", "seq"), scatter_dimension=0, tiled=True
+        )
+
+    vector_sums = lax.psum_scatter(vectors, ("dp", "seq"), scatter_dimension=0, tiled=True)
+    expand_bias_sums = lax.psum_scatter(
+        column_total(grad_pre), ("dp", "seq"), scatter_dimension=0, tiled=True
+    )
+    shrink_sums = scattered(grad_shrunk, activated)
+    grad_pre, second_rows, shrink_sums = lax.optimization_barrier(
+        (grad_pre, second_rows, shrink_sums)
+    )
+    expand_sums = scattered(grad_pre, second_rows)
+    grad_branch, grad_query, grad_key, grad_value, expand_sums = lax.optimization_barrier(
+        (grad_branch, grad_query, grad_key, grad_value, expand_sums)
     )
     return (
         layer_out,
         tokens_grad,
-        width_sums[:, base + 4],
-        width_sums[:, base + 5],
-        width_sums[:, 0:width],
-        width_sums[:, base],
-        width_sums[:, width : 2 * width],
-        width_sums[:, 2 * width : 3 * width],
-        width_sums[:, base + 1],
-        width_sums[:, 3 * width : 4 * width],
-        width_sums[:, base + 2],
-        width_sums[:, base + 6],
-        width_sums[:, base + 7],
-        hidden_sums[:, 0:width],
-        hidden_sums[:, width],
-        width_sums[:, 4 * width : base],
-        width_sums[:, base + 3],
+        vector_sums[:, 4],
+        vector_sums[:, 5],
+        scattered(grad_query, first_rows),
+        vector_sums[:, 0],
+        scattered(grad_key, first_rows),
+        scattered(grad_value, first_rows),
+        vector_sums[:, 1],
+        scattered(grad_branch, mixed),
+        vector_sums[:, 2],
+        vector_sums[:, 6],
+        vector_sums[:, 7],
+        expand_sums,
+        expand_bias_sums,
+        shrink_sums,
+        vector_sums[:, 3],
     )
 
 
@@ -385,6 +846,16 @@
         P(("dp", "seq"), None),
         P(("dp", "seq")),
     )
+    def per_device(*arrays):
+        tokens, query_weight = arrays[0], arrays[4]
+        fits = (
+            mesh.shape["dp"] == 8
+            and mesh.shape["seq"] == 4
+            and tokens.shape[0] == 2
+            and query_weight.shape[0] == HEAD_DIM
+        )
+        return (whole_sequence_device if fits else general_device)(*arrays)
+
     return jax.shard_map(
         per_device, mesh=mesh, in_specs=in_specs, out_specs=out_specs, check_vma=False
     )

time: 4680 us -> 3180 us (0.68)
  waiting for transfers between devices: 3430 us -> 686 us
  Pallas kernels: 0 us -> 1610 us
  local copies, waits for them, and re-layouts: 538 us -> 203 us
  matrix products: 460 us -> 264 us
  other arithmetic: 107 us -> 174 us
  starting transfers between devices: 0.68 us -> 54.1 us
  blocking collectives: 110 us -> 162 us
    reduce_scatter x4 -> x2, waiting for transfers between devices: 2700 us -> 0.01 us  [scatter_z(): lax.psum_scatter(total, 'seq', scatter_dimension=0, tiled=True).astype(f32)]
    pallas_call x0 -> x6, Pallas kernels: none -> 1610 us  [the longest x4 1530 us: arrange(): pl.pallas_call(arrange_kernel, out_shape=jax.ShapeDtypeStruct((4,) + shap...]
    all_gather x8 -> x4, waiting for transfers between devices: 722 us -> 109 us  [through_z(): return lax.all_gather(shard, 'seq', axis=0, tiled=True)]
    ppermute x0 -> x44, waiting for transfers between devices: none -> 575 us  [the longest x36 463 us: swap(): return lax.ppermute(values, 'dp', [(i, i ^ bit) for i in range(size)])]
    concatenate x2 -> x4, local copies, waits for them, and re-layouts: 334 us -> 9.61 us  [the longest x2 9.42 us: both_cores(): return jnp.concatenate(parts, 0)]
    dot_general x28 -> x0, matrix products: 155 us -> none  [the longest x4 54.5 us: backward_group(): jnp.einsum('sqhd,skhd->shqk', g_part, v_part, preferred_element_type=jnp....]
    all_gather x2 -> x1, blocking collectives: 67.9 us -> 162 us  [whole_sequence_device(): vectors = lax.all_gather(vectors, ('dp', 'seq'), axis=0, tiled=True)]
    dynamic_update_slice x28 -> x0, local copies, waits for them, and re-layouts: 82.7 us -> none  [the longest x8 52.8 us: backward_group(): lax.dynamic_update_slice_in_dim(grad_value_all, value_term.reshape(seq_co...]
  transfers between devices with their start and end apart: 12 -> 53, of which waited for: 10 -> 20; matrix products, arithmetic and copies ran while one was open for 15% -> 18% of each run, Pallas kernels for 0% -> 35%
where the time goes in v1:
time: 3180 us; the launch traced here: 3170 us
  Pallas kernels  1610 us (51%)
  waiting for transfers between devices  686 us (22%)
  matrix products  264 us (8%)
  local copies, waits for them, and re-layouts  203 us (6%)
  other arithmetic  174 us (5%)
  blocking collectives  162 us (5%)
  starting transfers between devices  54.1 us (2%)
    pallas_call x4, Pallas kernels, arrange(): pl.pallas_call(arrange_kernel, out_shape=jax.ShapeDtypeStruct((4,) + shap...  1530 us
    ppermute x36, waiting for transfers between devices, swap(): return lax.ppermute(values, 'dp', [(i, i ^ bit) for i in range(size)])  463 us
    all_gather x1, blocking collectives, whole_sequence_device(): vectors = lax.all_gather(vectors, ('dp', 'seq'), axis=0, tiled=True)  162 us
    all_gather x4, waiting for transfers between devices, through_z(): return lax.all_gather(shard, 'seq', axis=0, tiled=True)  109 us
    dot_general x16, matrix products, outer_rows(): lax.dot_general(grad_cols, inputs, (((0,), (0,)), ((), ())), preferred_el...  94.5 us
    dot_general x6, matrix products, through(): return jnp.dot(left, weight, preferred_element_type=jnp.float32)  87.9 us
    dot_general x6, matrix products, project(): lax.dot_general(left, weight, (((1,), (1,)), ((), ())), preferred_element...  81.6 us
    ppermute x2, waiting for transfers between devices, from_chips(): lax.ppermute(second, ('dp', 'seq'), [(b, a) for a, b in route(True)])  72.2 us
  transfers between devices with their start and end apart: 53, of which 20 were waited for; matrix products, arithmetic and copies ran while one was open for 18% of the time, Pallas kernels for 35%

profile of v1, /device:TPU:9, one launch (start us, length us, event | category | flops | bytes accessed | tf_op | source)
XLA Modules:
  0.0 3168.1 jit_solution(522535129913663643)
XLA Ops:
  17.1 88.7 %all-gather.6.cloned.1.call-done.own = bf16[768,2048]{1,0:T(8,128)(2,1)} async-done(((bf16[192,2048]{1,0:T(8,128)(2,1)}), bf16[768,2048]{1,0:T(8,128)(2,1)}) %all-gather.6.cloned.1.call-update) | async-done | bytes 3145744 | tf_op jit(solution)/shard_map/all_gather | solution.py:374
  116.4 20.7 all-gather.8.cloned.1.call-done
  154.2 161.6 %all-gather = bf16[32,1,768]{2,1,0:T(2,128)(2,1)S(1)} all-gather(bf16[1,1,768]{2,1,0:T(2,128)(2,1)S(1)} %reshape.915), channel_id=1, replica_groups=mesh['dp'=8,'seq'=4] {'dp','seq'}, dimensions={0}, use_global_device_ids=true | all-gather | bytes 50688 | tf_op jit(solution)/shard_map/all_gather | solution.py:356
  356.0 28.6 dynamic-slice_reduce_fusion.1
  397.1 128.2 %arrange.5 = bf16[4,512,1024]{2,1,0:T(8,128)(2,1)} custom-call(s32[1]{0:T(128)} %bitcast.9.place_ref, bf16[512,1024]{1,0:T(8,128)(2,1)} %copy-done.19, bf16[512,1024]{1,0:T(8,128)(2,1)} %collective-permute-done.7.beside, bf16[512,1024]{1,0:T(8,128)(2,1)} %collective-permute-done.8.across, bf16[512,1024]{1,0:T(8,128)(2,1)} %collective-permute-done.9.corner), custom_call_target="tpu_custom_call" | custom-call | bytes 8388608 | tf_op jit(solution)/shard_map/arrange/pallas_call | solution.py:79
  537.4 382.3 %arrange.4 = bf16[4,768,2048]{2,1,0:T(8,128)(2,1)} custom-call(s32[1]{0:T(128)} %bitcast.9.place_ref, bf16[768,2048]{1,0:T(8,128)(2,1)} %all-gather.6.cloned.1.call-done.own, bf16[768,2048]{1,0:T(8,128)(2,1)} %collective-permute-done.3.beside, bf16[768,2048]{1,0:T(8,128)(2,1)} %collective-permute-done.4.across, bf16[768,2048]{1,0:T(8,128)(2,1)} %collective-permute-done.5.corner), custom_call_target="tpu_custom_call" | custom-call | bytes 25165824 | tf_op jit(solution)/shard_map/arrange/pallas_call | solution.py:79
  919.7 18.5 add_convert_fusion.rows_ref
  938.4 29.8 attend.1
  1059.6 45.7 %collective-permute-done.12.beside = bf16[1024,2048]{1,0:T(8,128)(2,1)} collective-permute-done((bf16[1024,2048]{1,0:T(8,128)(2,1)}, bf16[1024,2048]{1,0:T(8,128)(2,1)}, u32[]{:S(2)}, u32[]{:S(2)}) %collective-permute-start.12) | collective-permute-done | bytes 4194336 | tf_op jit(solution)/shard_map/ppermute | solution.py:49
  1105.3 89.9 %collective-permute-done.14.corner = bf16[1024,2048]{1,0:T(8,128)(2,1)} collective-permute-done((bf16[1024,2048]{1,0:T(8,128)(2,1)}, bf16[1024,2048]{1,0:T(8,128)(2,1)}, u32[]{:S(2)}, u32[]{:S(2)}) %collective-permute-start.14) | collective-permute-done | bytes 4194336 | tf_op jit(solution)/shard_map/ppermute | solution.py:49
  1195.2 509.4 %arrange.6 = bf16[4,1024,2048]{2,1,0:T(8,128)(2,1)} custom-call(s32[1]{0:T(128)} %bitcast.9.place_ref, bf16[1024,2048]{1,0:T(8,128)(2,1)} %all-gather.10.cloned.1.call-done.own, bf16[1024,2048]{1,0:T(8,128)(2,1)} %collective-permute-done.12.beside, bf16[1024,2048]{1,0:T(8,128)(2,1)} %collective-permute-done.13.across, ...), custom_call_target="tpu_custom_call" | custom-call | bytes 33554432 | tf_op jit(solution)/shard_map/arrange/pallas_call | solution.py:79
  1704.5 25.8 multiply_convert_fusion.1
  1730.4 509.4 %arrange.7 = bf16[4,512,4096]{2,1,0:T(8,128)(2,1)} custom-call(s32[1]{0:T(128)} %bitcast.9.place_ref, bf16[512,4096]{1,0:T(8,128)(2,1)} %maximum_select_fusion.1.own, bf16[512,4096]{1,0:T(8,128)(2,1)} %collective-permute-done.16.beside, bf16[512,4096]{1,0:T(8,128)(2,1)} %collective-permute-done.17.across, bf16[512,4096]{1,0:T(8,128)(2,1)} %collective-permute-done.18.corner), custom_call_target="tpu_custom_call" | custom-call | bytes 33554432 | tf_op jit(solution)/shard_map/arrange/pallas_call | solution.py:79
  2239.8 27.8 convert_reduce_fusion
  2310.8 27.7 constant_dynamic-slice_fusion.4
  2387.6 50.4 %attend_back.1 = bf16[1024,3072]{1,0:T(8,128)(2,1)} custom-call(bf16[1024,3072]{1,0:T(8,128)(2,1)} %add_convert_fusion.rows_ref, bf16[1024,1024]{1,0:T(8,128)(2,1)S(1)} %convolution_convert_fusion.12.grad_ref, bf16[1024,64]{1,0:T(8,128)(2,1)S(1)} %copy-done.3), custom_call_target="tpu_custom_call" | custom-call | flops 42949672960 | bytes 25165824 | tf_op jit(solution)/shard_map/attend_back/pallas_call | solution.py:246
  2517.7 20.2 collective-permute-done.33
  2624.9 21.0 collective-permute-done.30
  2701.3 68.4 %collective-permute-done.40 = bf16[512,4096]{1,0:T(8,128)(2,1)S(1)} collective-permute-done((bf16[512,4096]{1,0:T(8,128)(2,1)}, bf16[512,4096]{1,0:T(8,128)(2,1)S(1)}, u32[]{:S(2)}, u32[]{:S(2)}) %collective-permute-start.40) | collective-permute-done | bytes 4194336 | tf_op jit(solution)/shard_map/ppermute | solution.py:49
  2777.5 82.1 %collective-permute-done.39 = bf16[1024,2048]{1,0:T(8,128)(2,1)} collective-permute-done((bf16[1024,2048]{1,0:T(8,128)(2,1)}, bf16[1024,2048]{1,0:T(8,128)(2,1)}, u32[]{:S(2)}, u32[]{:S(2)}) %collective-permute-start.39) | collective-permute-done | bytes 4194336 | tf_op jit(solution)/shard_map/ppermute | solution.py:49
  2876.8 72.7 %collective-permute-done.42 = bf16[512,4096]{1,0:T(8,128)(2,1)} collective-permute-done((bf16[512,4096]{1,0:T(8,128)(2,1)}, bf16[512,4096]{1,0:T(8,128)(2,1)}, u32[]{:S(2)}, u32[]{:S(2)}) %collective-permute-start.42) | collective-permute-done | bytes 4194336 | tf_op jit(solution)/shard_map/ppermute | solution.py:49
  3036.8 43.2 %collective-permute-done.21 = bf16[256,2048]{1,0:T(8,128)(2,1)S(1)} collective-permute-done((bf16[256,2048]{1,0:T(8,128)(2,1)}, bf16[256,2048]{1,0:T(8,128)(2,1)S(1)}, u32[]{:S(2)}, u32[]{:S(2)}) %collective-permute-start.21) | collective-permute-done | bytes 1048608 | tf_op jit(solution)/shard_map/ppermute | solution.py:330
  3080.0 23.8 collective-permute-done.20
  3107.4 29.0 collective-permute-done.29
  (458 shorter events, 647.7 us)
Async XLA Ops:
  10.2 337.9 %all-gather.12.cloned.1.call-start = ((), (), s32[]{:S(2)}) async-start(), calls=%async_computation.7 | async-start | bytes 5242880 | tf_op jit(solution)/shard_map/all_gather | solution.py:374
  11.0 518.1 %all-gather.10.cloned.1.call-start = ((), (), s32[]{:S(2)}) async-start(), calls=%async_computation.6 | async-start | bytes 5242880 | tf_op jit(solution)/shard_map/all_gather | solution.py:374
  17.1 3088.4 %all-reduce.10.cloned.1.call-start = ((), (), s32[]{:S(2)}) async-start(), calls=%async_computation.12 | async-start | bytes 196608
  105.8 250.1 %collective-permute-start.4 = (bf16[768,2048]{1,0:T(8,128)(2,1)}, bf16[768,2048]{1,0:T(8,128)(2,1)}, u32[]{:S(2)}, u32[]{:S(2)}) collective-permute-start(bf16[768,2048]{1,0:T(8,128)(2,1)} %all-gather.6.cloned.1.call-done.own), channel_id=1, source_target_pairs={{0,16},{4,20},{8,24},{12,28},{16,0},{20,4},{24,8},{28,12},{1,17},{... | collective-permute-start | bytes 9437192 | tf_op jit(solution)/shard_map/ppermute | solution.py:49
  116.4 223.4 %collective-permute-start.2 = (bf16[2,272,2048]{2,1,0:T(8,128)(2,1)}, bf16[2,272,2048]{2,1,0:T(8,128)(2,1)}, u32[]{:S(2)}, u32[]{:S(2)}) collective-permute-start(bf16[2,272,2048]{2,1,0:T(8,128)(2,1)} %maximum_select_fusion.4), channel_id=1, source_target_pairs={{0,4},{4,0},{8,12},{12,8},{16,20},{20,16},{24,28},{28,24},{1,5},{5... | collective-permute-start | bytes 6684680 | tf_op jit(solution)/shard_map/ppermute | solution.py:49
  147.1 168.8 %collective-permute-start.6 = (bf16[256,1024]{1,0:T(8,128)(2,1)}, bf16[256,1024]{1,0:T(8,128)(2,1)}, u32[]{:S(2)}, u32[]{:S(2)}) collective-permute-start(bf16[256,1024]{1,0:T(8,128)(2,1)} %bitcast.92), channel_id=1, source_target_pairs={{0,4},{4,0},{8,12},{12,8},{16,20},{20,16},{24,28},{28,24},{1,5},{5... | collective-permute-start | bytes 1572872 | tf_op jit(solution)/shard_map/ppermute | solution.py:49
  149.4 171.7 %collective-permute-start.23 = (bf16[256,2048]{1,0:T(8,128)(2,1)}, bf16[256,2048]{1,0:T(8,128)(2,1)S(1)}, u32[]{:S(2)}, u32[]{:S(2)}) collective-permute-start(bf16[256,2048]{1,0:T(8,128)(2,1)} %get-tuple-element.95), channel_id=1, source_target_pairs={{0,1},{1,0},{2,5},{3,4},{4,3},{5,2},{6,7},{7,6},{8,9},{9,8},{10,13... | collective-permute-start | bytes 3145736 | tf_op jit(solution)/shard_map/ppermute | solution.py:321
  150.1 171.1 %collective-permute-start.22 = (bf16[256,2048]{1,0:T(8,128)(2,1)}, bf16[256,2048]{1,0:T(8,128)(2,1)}, u32[]{:S(2)}, u32[]{:S(2)}) collective-permute-start(bf16[256,2048]{1,0:T(8,128)(2,1)} %get-tuple-element.94), channel_id=1, source_target_pairs={{0,0},{1,1},{2,4},{3,5},{4,2},{5,3},{6,6},{7,7},{8,8},{9,9},{10,12... | collective-permute-start | bytes 3145736 | tf_op jit(solution)/shard_map/ppermute | solution.py:320
  345.8 191.6 %collective-permute-start.3 = (bf16[768,2048]{1,0:T(8,128)(2,1)}, bf16[768,2048]{1,0:T(8,128)(2,1)}, u32[]{:S(2)}, u32[]{:S(2)}) collective-permute-start(bf16[768,2048]{1,0:T(8,128)(2,1)} %all-gather.6.cloned.1.call-done.own), channel_id=1, source_target_pairs={{0,8},{4,12},{8,0},{12,4},{16,24},{20,28},{24,16},{28,20},{1,9},{5... | collective-permute-start | bytes 9437192 | tf_op jit(solution)/shard_map/ppermute | solution.py:49
  355.9 181.5 %collective-permute-start.5 = (bf16[768,2048]{1,0:T(8,128)(2,1)}, bf16[768,2048]{1,0:T(8,128)(2,1)}, u32[]{:S(2)}, u32[]{:S(2)}) collective-permute-start(bf16[768,2048]{1,0:T(8,128)(2,1)} %collective-permute-done.4.across), channel_id=1, source_target_pairs={{0,8},{4,12},{8,0},{12,4},{16,24},{20,28},{24,16},{28,20},{1,9},{5... | collective-permute-start | bytes 9437192 | tf_op jit(solution)/shard_map/ppermute | solution.py:49
  397.1 581.3 %collective-permute-start.24 = (bf16[2,256,2048]{2,1,0:T(8,128)(2,1)S(1)}, bf16[2,256,2048]{2,1,0:T(8,128)(2,1)}, u32[]{:S(2)}, u32[]{:S(2)}) collective-permute-start(bf16[2,256,2048]{2,1,0:T(8,128)(2,1)S(1)} %maximum_select_fusion.6), channel_id=1, source_target_pairs={{0,4},{4,0},{8,12},{12,8},{16,20},{20,16},{24,28},{28,24},{1,5},{5... | collective-permute-start | bytes 6291464 | tf_op jit(solution)/shard_map/ppermute | solution.py:49
  529.1 484.5 %collective-permute-start.13 = (bf16[1024,2048]{1,0:T(8,128)(2,1)}, bf16[1024,2048]{1,0:T(8,128)(2,1)}, u32[]{:S(2)}, u32[]{:S(2)}) collective-permute-start(bf16[1024,2048]{1,0:T(8,128)(2,1)} %all-gather.10.cloned.1.call-done.own), channel_id=1, source_target_pairs={{0,16},{4,20},{8,24},{12,28},{16,0},{20,4},{24,8},{28,12},{1,17},{... | collective-permute-start | bytes 12582920 | tf_op jit(solution)/shard_map/ppermute | solution.py:49
  536.1 478.1 %collective-permute-start.16 = (bf16[512,4096]{1,0:T(8,128)(2,1)}, bf16[512,4096]{1,0:T(8,128)(2,1)}, u32[]{:S(2)}, u32[]{:S(2)}) collective-permute-start(bf16[512,4096]{1,0:T(8,128)(2,1)} %maximum_select_fusion.1.own), channel_id=1, source_target_pairs={{0,8},{4,12},{8,0},{12,4},{16,24},{20,28},{24,16},{28,20},{1,9},{5... | collective-permute-start | bytes 12582920 | tf_op jit(solution)/shard_map/ppermute | solution.py:49
  1013.6 716.8 %collective-permute-start.17 = (bf16[512,4096]{1,0:T(8,128)(2,1)}, bf16[512,4096]{1,0:T(8,128)(2,1)}, u32[]{:S(2)}, u32[]{:S(2)}) collective-permute-start(bf16[512,4096]{1,0:T(8,128)(2,1)} %maximum_select_fusion.1.own), channel_id=1, source_target_pairs={{0,16},{4,20},{8,24},{12,28},{16,0},{20,4},{24,8},{28,12},{1,17},{... | collective-permute-start | bytes 12582920 | tf_op jit(solution)/shard_map/ppermute | solution.py:49
  1014.3 180.9 %collective-permute-start.14 = (bf16[1024,2048]{1,0:T(8,128)(2,1)}, bf16[1024,2048]{1,0:T(8,128)(2,1)}, u32[]{:S(2)}, u32[]{:S(2)}) collective-permute-start(bf16[1024,2048]{1,0:T(8,128)(2,1)} %collective-permute-done.13.across), channel_id=1, source_target_pairs={{0,8},{4,12},{8,0},{12,4},{16,24},{20,28},{24,16},{28,20},{1,9},{5... | collective-permute-start | bytes 12582920 | tf_op jit(solution)/shard_map/ppermute | solution.py:49
  1015.7 714.7 %collective-permute-start.18 = (bf16[512,4096]{1,0:T(8,128)(2,1)}, bf16[512,4096]{1,0:T(8,128)(2,1)}, u32[]{:S(2)}, u32[]{:S(2)}) collective-permute-start(bf16[512,4096]{1,0:T(8,128)(2,1)} %collective-permute-done.16.beside), channel_id=1, source_target_pairs={{0,16},{4,20},{8,24},{12,28},{16,0},{20,4},{24,8},{28,12},{1,17},{... | collective-permute-start | bytes 12582920 | tf_op jit(solution)/shard_map/ppermute | solution.py:49
  2345.4 333.0 %collective-permute-start.38 = (bf16[1024,2048]{1,0:T(8,128)(2,1)}, bf16[1024,2048]{1,0:T(8,128)(2,1)}, u32[]{:S(2)}, u32[]{:S(2)}) collective-permute-start(bf16[1024,2048]{1,0:T(8,128)(2,1)} %convolution_convert_fusion.4), channel_id=1, source_target_pairs={{0,8},{4,12},{8,0},{12,4},{16,24},{20,28},{24,16},{28,20},{1,9},{5... | collective-permute-start | bytes 12582920 | tf_op jit(solution)/shard_map/ppermute | solution.py:49
  2606.7 543.3 %reduce-scatter.13.cloned.1.call-start = ((), (), s32[]{:S(2)}) async-start(), calls=%async_computation.10 | async-start | bytes 1310720
  2608.7 543.5 %reduce-scatter.9.cloned.1.call-start = ((), (), s32[]{:S(2)}) async-start(), calls=%async_computation.8 | async-start | bytes 3932160 | tf_op jit(solution)/shard_map/reduce_scatter | solution.py:441
  2667.4 487.1 %reduce-scatter.11.cloned.1.call-start = ((), (), s32[]{:S(2)}) async-start(), calls=%async_computation.9 | async-start | bytes 5242880 | tf_op jit(solution)/shard_map/reduce_scatter | solution.py:441
  2687.1 172.5 %collective-permute-start.39 = (bf16[1024,2048]{1,0:T(8,128)(2,1)}, bf16[1024,2048]{1,0:T(8,128)(2,1)}, u32[]{:S(2)}, u32[]{:S(2)}) collective-permute-start(bf16[1024,2048]{1,0:T(8,128)(2,1)} %add_convert_fusion.4), channel_id=1, source_target_pairs={{0,16},{4,20},{8,24},{12,28},{16,0},{20,4},{24,8},{28,12},{1,17},{... | collective-permute-start | bytes 12582920 | tf_op jit(solution)/shard_map/ppermute | solution.py:49
  2700.8 248.6 %collective-permute-start.42 = (bf16[512,4096]{1,0:T(8,128)(2,1)}, bf16[512,4096]{1,0:T(8,128)(2,1)}, u32[]{:S(2)}, u32[]{:S(2)}) collective-permute-start(bf16[512,4096]{1,0:T(8,128)(2,1)} %convolution_convert_fusion), channel_id=1, source_target_pairs={{0,16},{4,20},{8,24},{12,28},{16,0},{20,4},{24,8},{28,12},{1,17},{... | collective-permute-start | bytes 12582920 | tf_op jit(solution)/shard_map/ppermute | solution.py:49
  2776.1 173.4 %collective-permute-start.41 = (bf16[512,4096]{1,0:T(8,128)(2,1)}, bf16[512,4096]{1,0:T(8,128)(2,1)}, u32[]{:S(2)}, u32[]{:S(2)}) collective-permute-start(bf16[512,4096]{1,0:T(8,128)(2,1)} %add_convert_fusion.2), channel_id=1, source_target_pairs={{0,8},{4,12},{8,0},{12,4},{16,24},{20,28},{24,16},{28,20},{1,9},{5... | collective-permute-start | bytes 12582920 | tf_op jit(solution)/shard_map/ppermute | solution.py:49
  2868.4 288.9 %reduce-scatter.15.cloned.1.call-start = ((), (), s32[]{:S(2)}) async-start(), calls=%async_computation.11 | async-start | bytes 5242880
  (121 other events, 5451.1 us)
Sparse Core Ops, SparseCore 0:
  10.2 95.5 all-gather.5
  107.4 29.6 all-gather.7
  138.7 115.5 all-gather.11
  255.7 81.9 all-gather.9
  2606.8 122.9 all-reduce.9
  2731.9 25.7 reduce-scatter.12
  2760.1 60.4 reduce-scatter.8
  2868.5 81.3 reduce-scatter.10
  2980.4 106.0 reduce-scatter.14

commit v2 on v1

--- a/solution.py
+++ b/solution.py
@@ -62,47 +62,212 @@
     )
 
 
-def arrange_kernel(place_ref, own, beside, across, corner, out, sems):
-    copies = [
-        pltpu.make_async_copy(piece, out.at[place_ref[0] ^ index], sems.at[index])
-        for index, piece in enumerate((own, beside, across, corner))
-    ]
-    for copy in copies:
-        copy.start()
-    for copy in copies:
-        copy.wait()
-
-
-def arrange(place, pieces):
-    shape = pieces[0].shape
-    size = 4 * math.prod(shape) * pieces[0].dtype.itemsize
+def arrange(pieces, block, sources, targets):
+    count = len(pieces)
+    steps = len(sources)
+    table = jnp.stack([jnp.asarray(target, jnp.int32) for target in targets])
+
+    def kernel(table_ref, *refs):
+        step = pl.program_id(0)
+        for index in range(count):
+            mine = [at for at, source in enumerate(sources) if source[0] == index]
+
+            @pl.when((step >= mine[0]) & (step <= mine[-1]))
+            def _():
+                refs[count][...] = refs[index][...]
+
+    def place_of(index):
+        mine = [at for at, source in enumerate(sources) if source[0] == index]
+
+        def block_of(step, table_ref):
+            row, column = sources[mine[0]][1:]
+            for at in mine[1:]:
+                row = jnp.where(step >= at, sources[at][1], row)
+                column = jnp.where(step >= at, sources[at][2], column)
+            return row, column
+
+        return block_of
+
+    total = steps * block[0] * block[1]
     return pl.pallas_call(
-        arrange_kernel,
-        out_shape=jax.ShapeDtypeStruct((4,) + shape, pieces[0].dtype),
-        in_specs=[pl.BlockSpec(memory_space=pltpu.SMEM)]
-        + [pl.BlockSpec(memory_space=pl.ANY)] * 4,
-        out_specs=pl.BlockSpec(memory_space=pl.ANY),
-        scratch_shapes=[pltpu.SemaphoreType.DMA((4,))],
-        cost_estimate=pl.CostEstimate(flops=0, bytes_accessed=2 * size, transcendentals=0),
+        kernel,
+        grid_spec=pltpu.PrefetchScalarGridSpec(
+            num_scalar_prefetch=1,
+            grid=(steps,),
+            in_specs=[pl.BlockSpec(block, place_of(index)) for index in range(count)],
+            out_specs=pl.BlockSpec(block, lambda step, table_ref: (table_ref[step], 0)),
+        ),
+        out_shape=jax.ShapeDtypeStruct((steps * block[0], block[1]), pieces[0].dtype),
+        compiler_params=pltpu.CompilerParams(vmem_limit_bytes=48 << 20),
+        cost_estimate=pl.CostEstimate(flops=0, bytes_accessed=4 * total, transcendentals=0),
         name="arrange",
-    )(place.reshape(1), *pieces)
-
-
-def spread(values, place, corner_by):
+    )(table, *pieces)
+
+
+def split_kernel(table_ref, first, second, first_out, second_out):
+    first_out[...] = first[...]
+    second_out[...] = second[...]
+
+
+def split_columns(core, matrix, block):
+    rows, columns = matrix.shape
+    count = columns // block // 2
+    piece = jax.ShapeDtypeStruct((rows, columns // 2), matrix.dtype)
+    return pl.pallas_call(
+        split_kernel,
+        grid_spec=pltpu.PrefetchScalarGridSpec(
+            num_scalar_prefetch=1,
+            grid=(count,),
+            in_specs=[
+                pl.BlockSpec((rows, block), lambda i, core_ref: (0, 2 * i + core_ref[0])),
+                pl.BlockSpec((rows, block), lambda i, core_ref: (0, 2 * i + 1 - core_ref[0])),
+            ],
+            out_specs=[pl.BlockSpec((rows, block), lambda i, core_ref: (0, i))] * 2,
+        ),
+        out_shape=(piece, piece),
+        cost_estimate=pl.CostEstimate(
+            flops=0, bytes_accessed=4 * rows * columns, transcendentals=0
+        ),
+        name="split_columns",
+    )(core.reshape(1), matrix, matrix)
+
+
+def weave_kernel(core_ref, mine, theirs, out):
+    block = mine.shape[1]
+
+    @pl.when(core_ref[0] == 0)
+    def _():
+        out[:, :block] = mine[...]
+        out[:, block:] = theirs[...]
+
+    @pl.when(core_ref[0] == 1)
+    def _():
+        out[:, :block] = theirs[...]
+        out[:, block:] = mine[...]
+
+
+def weave_columns(core, mine, theirs, block):
+    rows, columns = mine.shape
+    return pl.pallas_call(
+        weave_kernel,
+        grid_spec=pltpu.PrefetchScalarGridSpec(
+            num_scalar_prefetch=1,
+            grid=(columns // block,),
+            in_specs=[pl.BlockSpec((rows, block), lambda i, core_ref: (0, i))] * 2,
+            out_specs=pl.BlockSpec((rows, 2 * block), lambda i, core_ref: (0, i)),
+        ),
+        out_shape=jax.ShapeDtypeStruct((rows, 2 * columns), mine.dtype),
+        cost_estimate=pl.CostEstimate(
+            flops=0, bytes_accessed=8 * rows * columns, transcendentals=0
+        ),
+        name="weave_columns",
+    )(core.reshape(1), mine, theirs)
+
+
+def outer_rows_of(index, lefts, rights, rows, tile=512, table=None):
+    count, columns = rights[0].shape
+    terms = len(lefts)
+    scalars = [jnp.asarray(index, jnp.int32).reshape(1)]
+    if table is not None:
+        scalars.append(jnp.stack([jnp.asarray(target, jnp.int32) for target in table]))
+
+    def kernel(*refs):
+        operands = refs[len(scalars) :]
+        total = 0.0
+        for left, right in zip(operands[:terms], operands[terms : 2 * terms]):
+            total = total + lax.dot_general(
+                left[...], right[...], (((0,), (0,)), ((), ())), preferred_element_type=jnp.float32
+            )
+        total = total.astype(jnp.bfloat16)
+        out = operands[-1]
+        if table is None:
+            out[...] = total
+        else:
+            for at in range(len(table)):
+                start = pl.multiple_of(refs[1][at] * HEAD_DIM, HEAD_DIM)
+                out[pl.ds(start, HEAD_DIM), :] = total[at * HEAD_DIM : (at + 1) * HEAD_DIM]
+
+    return pl.pallas_call(
+        kernel,
+        grid_spec=pltpu.PrefetchScalarGridSpec(
+            num_scalar_prefetch=len(scalars),
+            grid=(columns // tile,),
+            in_specs=[pl.BlockSpec((count, rows), lambda i, ref, *_: (0, ref[0]))] * terms
+            + [pl.BlockSpec((count, tile), lambda i, *_: (0, i))] * terms,
+            out_specs=pl.BlockSpec((rows, tile), lambda i, *_: (0, i)),
+        ),
+        out_shape=jax.ShapeDtypeStruct((rows, columns), jnp.bfloat16),
+        compiler_params=pltpu.CompilerParams(vmem_limit_bytes=48 << 20),
+        cost_estimate=pl.CostEstimate(
+            flops=2 * terms * count * rows * columns,
+            bytes_accessed=2 * (terms * count * (rows + columns) + rows * columns),
+            transcendentals=0,
+        ),
+        name="outer_rows_of",
+    )(*scalars, *lefts, *rights)
+
+
+def outer_sides(indices, left, right, rows):
+    count, columns = right.shape
+    pieces = len(indices) // 2
+    table = jnp.stack([jnp.asarray(index, jnp.int32) for index in indices])
+
+    def kernel(table_ref, left, right, *outs):
+        step = pl.program_id(0)
+        total = lax.dot_general(
+            left[...], right[...], (((0,), (0,)), ((), ())), preferred_element_type=jnp.float32
+        ).astype(jnp.bfloat16)
+        for piece, out in enumerate(outs):
+
+            @pl.when(step // 2 == piece)
+            def _():
+                out[...] = total
+
+    def side_of(piece):
+        return lambda step, table_ref: (0, jnp.clip(step - 2 * piece, 0, 1))
+
+    return pl.pallas_call(
+        kernel,
+        grid_spec=pltpu.PrefetchScalarGridSpec(
+            num_scalar_prefetch=1,
+            grid=(2 * pieces,),
+            in_specs=[
+                pl.BlockSpec((count, rows), lambda step, table_ref: (0, table_ref[step])),
+                pl.BlockSpec((count, columns), lambda step, table_ref: (0, 0)),
+            ],
+            out_specs=[pl.BlockSpec((rows, columns), side_of(piece)) for piece in range(pieces)],
+        ),
+        out_shape=[jax.ShapeDtypeStruct((rows, 2 * columns), jnp.bfloat16)] * pieces,
+        compiler_params=pltpu.CompilerParams(vmem_limit_bytes=48 << 20),
+        cost_estimate=pl.CostEstimate(
+            flops=4 * pieces * count * rows * columns,
+            bytes_accessed=4 * count * (pieces * rows + columns),
+            transcendentals=0,
+        ),
+        name="outer_sides",
+    )(table, left, right)
+
+
+def exchange(values):
+    half = values.shape[0] // 2
     beside = swap(values, ALONG_X)
     across = swap(values, ALONG_Y)
-    corner = swap(beside, ALONG_Y) if corner_by == ALONG_Y else swap(across, ALONG_X)
-    return arrange(place, (values, beside, across, corner))
-
-
-def total_plane(pieces, corner_by):
+    upper = swap(beside[:half], ALONG_Y)
+    lower = swap(across[half:], ALONG_X)
+    return [values, beside, across, upper, lower]
+
+
+def total_plane(pieces, wait):
     own, beside, across, corner = pieces
-    if corner_by == ALONG_Y:
-        beside = add_low(beside, swap(corner, ALONG_Y))
-    else:
-        across = add_low(across, swap(corner, ALONG_X))
+    half = own.shape[0] // 2
+    upper = swap(corner[:half], ALONG_Y)
+    lower = swap(corner[half:], ALONG_X)
+    beside = lax.dynamic_update_slice(beside, add_low(beside[:half], upper), (0, 0))
+    across = lax.dynamic_update_slice(across, add_low(across[half:], lower), (half, 0))
     got_x = swap(beside, ALONG_X)
     got_y = swap(across, ALONG_Y)
+    if wait is not None:
+        own = after(own, wait)
     return (
         own.astype(jnp.float32) + got_x.astype(jnp.float32) + got_y.astype(jnp.float32)
     ).astype(jnp.bfloat16)
@@ -262,6 +427,9 @@
     )(rows, grad, mask)
 
 
+ROWS = 128
+
+
 def normal_parts(values):
     center = values - jnp.mean(values, axis=-1, keepdims=True)
     spread_of = jnp.mean(center * center, axis=-1, keepdims=True)
@@ -273,6 +441,92 @@
     mean_grad = jnp.mean(grad, axis=-1, keepdims=True)
     mean_product = jnp.mean(grad * normed, axis=-1, keepdims=True)
     return (grad - mean_grad - normed * mean_product) * scale
+
+
+def first_kernel(start_ref, tokens, gain, shift, out):
+    normed, _ = normal_parts(tokens[...].astype(jnp.float32))
+    out[...] = (normed * gain[...] + shift[...]).astype(out.dtype)
+
+
+def middle_kernel(
+    start_ref, tokens, own, got, active, bias, gain, shift, middle_out, rows_out
+):
+    branch = own[...].astype(jnp.float32) + got[...].astype(jnp.float32) + bias[...]
+    middle = tokens[...].astype(jnp.float32) + active[...] * branch
+    middle_out[...] = middle
+    normed, _ = normal_parts(middle)
+    rows_out[...] = (normed * gain[...] + shift[...]).astype(rows_out.dtype)
+
+
+def add_totals(totals, parts):
+    first = pl.program_id(0) == 0
+    for index, part in enumerate(parts):
+        total = jnp.sum(part, axis=0, keepdims=True)
+        totals[index : index + 1, :] = total + jnp.where(
+            first, 0.0, totals[index : index + 1, :]
+        )
+
+
+def middle_back_kernel(
+    start_ref, cotangent, middle, own, got, peer, active, gain, grad_out, branch_out, totals
+):
+    grad_second = own[...] + got[...].astype(jnp.float32) + peer[...].astype(jnp.float32)
+    normed, scale = normal_parts(middle[...])
+    grad_middle = cotangent[...].astype(jnp.float32) + normal_back(
+        normed, scale, grad_second * gain[...]
+    )
+    grad_out[...] = grad_middle
+    grad_branch = (active[...] * grad_middle).astype(jnp.bfloat16)
+    branch_out[...] = grad_branch
+    add_totals(
+        totals, (grad_second * normed, grad_second, grad_branch.astype(jnp.float32))
+    )
+
+
+def first_back_kernel(start_ref, tokens, grad_middle, own, got, gain, grad_out, totals):
+    grad_first = own[...] + got[...].astype(jnp.float32)
+    normed, scale = normal_parts(tokens[...].astype(jnp.float32))
+    grad = grad_middle[...] + normal_back(normed, scale, grad_first * gain[...])
+    grad_out[...] = grad.astype(grad_out.dtype)
+    add_totals(totals, (grad_first * normed, grad_first))
+
+
+def by_rows(kernel, start, count, arrays, outs, name):
+    width = arrays[0][0].shape[1]
+    specs = {
+        "rows": pl.BlockSpec((ROWS, width), lambda i, start_ref: (i, 0)),
+        "from": pl.BlockSpec((ROWS, width), lambda i, start_ref: (start_ref[0] + i, 0)),
+        "vector": pl.BlockSpec((1, width), lambda i, start_ref: (0, 0)),
+        "totals": pl.BlockSpec((8, width), lambda i, start_ref: (0, 0)),
+        "flag": pl.BlockSpec((ROWS, 1), lambda i, start_ref: (i, 0)),
+        "flag from": pl.BlockSpec((ROWS, 1), lambda i, start_ref: (start_ref[0] + i, 0)),
+    }
+    shapes = [
+        jax.ShapeDtypeStruct((8 if kind == "totals" else count, width), dtype)
+        for kind, dtype in outs
+    ]
+    moved = sum(
+        count * width * array.dtype.itemsize for array, kind in arrays if kind in ("rows", "from")
+    ) + sum(math.prod(shape.shape) * shape.dtype.itemsize for shape in shapes)
+    return pl.pallas_call(
+        kernel,
+        grid_spec=pltpu.PrefetchScalarGridSpec(
+            num_scalar_prefetch=1,
+            grid=(count // ROWS,),
+            in_specs=[specs[kind] for _, kind in arrays],
+            out_specs=[specs[kind] for kind, _ in outs],
+        ),
+        out_shape=shapes,
+        compiler_params=pltpu.CompilerParams(vmem_limit_bytes=48 << 20),
+        cost_estimate=pl.CostEstimate(
+            flops=20 * count * width, bytes_accessed=moved, transcendentals=0
+        ),
+        name=name,
+    )(start, *[array for array, _ in arrays])
+
+
+def after(value, *others):
+    return lax.optimization_barrier((value, others))[0]
 
 
 def whole_sequence_device(
@@ -301,6 +555,7 @@
     dp_size, seq_size = lax.axis_size("dp"), lax.axis_size("seq")
     dp, depth = lax.axis_index("dp"), lax.axis_index("seq")
     core, place = dp % 2, dp // 2
+    along_x, along_y = place % 2, place // 2
     parity = depth % 2
     full_len = local_len * seq_size
     half_len = full_len // 2
@@ -333,12 +588,16 @@
     alive = (exit_layer > LAYER).astype(low)
     flag_rows = jnp.broadcast_to(alive[:, None, :], (seq_count, 16, local_len))
     flag_rows = jnp.pad(flag_rows, ((0, 0), (0, 0), (0, width - local_len)))
-    arrived = to_chips(jnp.concatenate([tokens, flag_rows], axis=1))
-    inputs = arrived[:, :local_len].reshape(full_len, width).astype(f32)
-    alive = arrived[:, local_len, :local_len].reshape(full_len, 1)
-    active = alive.astype(f32)
-    mask = jnp.broadcast_to((alive - 1) * jnp.bfloat16(1e30), (full_len, HEAD_DIM))
-    cotangent_full = to_chips(cotangent).reshape(full_len, width)
+
+    devices = dp_size * seq_size
+    all_dp = jnp.arange(dp_size, dtype=jnp.int32)[:, None]
+    all_seq = jnp.arange(seq_size, dtype=jnp.int32)[None, :]
+    relative = ((all_dp ^ dp) * seq_size + (depth - all_seq) % seq_size).reshape(-1)
+
+    def shift_z(values, steps):
+        return lax.ppermute(
+            values, "seq", [(i, (i + steps) % seq_size) for i in range(seq_size)]
+        )
 
     vectors = jnp.concatenate(
         [
@@ -352,12 +611,16 @@
             shrink_bias,
             expand_bias,
         ]
-    )
-    vectors = lax.all_gather(vectors, ("dp", "seq"), axis=0, tiled=True)
-    vectors = vectors.reshape(dp_size * seq_size, -1).astype(f32)
+    )[None]
+    for bit in (CORE, ALONG_X, ALONG_Y):
+        vectors = jnp.concatenate([vectors, swap(vectors, bit)], 0)
+    vectors = jnp.stack(
+        [vectors] + [shift_z(vectors, steps) for steps in range(1, seq_size)], 1
+    )
+    vectors = vectors.reshape(devices, -1)[relative].astype(f32)
 
     def vector(index):
-        return vectors[:, index * heads_rows : (index + 1) * heads_rows].reshape(-1)
+        return vectors[:, index * heads_rows : (index + 1) * heads_rows].reshape(1, -1)
 
     def of_core(matrix):
         cut = matrix.reshape(4, 2, seq_size, -1)
@@ -368,124 +631,287 @@
     bias_value = of_core(vectors[:, 3 * heads_rows : 4 * heads_rows])
     bias_rows = jnp.stack([bias_query, jnp.zeros_like(bias_query), bias_value], 1).reshape(-1)
     bias_out, gain_two, shift_two, bias_shrink = vector(4), vector(5), vector(6), vector(7)
-    bias_expand = of_core(vectors[:, 8 * heads_rows :]).reshape(-1)
+    def of_quarter(matrix):
+        cut = matrix.reshape(2, 4, seq_size, -1)
+        return lax.dynamic_index_in_dim(cut, 2 * along_x + core, 1, False)
+
+    bias_expand = of_quarter(vectors[:, 8 * heads_rows :]).reshape(-1)
 
     def through_z(shard):
         return lax.all_gather(shard, "seq", axis=0, tiled=True)
 
-    def core_columns(rows):
-        cut = rows.reshape(rows.shape[0], 4, 2, -1)
-        mine = lax.dynamic_index_in_dim(cut, core, 2, False).reshape(rows.shape[0], -1)
-        theirs = lax.dynamic_index_in_dim(cut, 1 - core, 2, False).reshape(rows.shape[0], -1)
-        return ordered(core, mine, swap(theirs, CORE), 0)
-
-    w_qkv = spread(
-        through_z(jnp.concatenate([query_weight, key_weight, value_weight], 0)), place, ALONG_X
-    ).reshape(-1, width)
-    w_out = spread(core_columns(through_z(output_weight)), place, ALONG_Y).reshape(width, -1)
-    w_expand = spread(through_z(expand_weight), place, ALONG_X).reshape(-1, width)
-    w_shrink = spread(core_columns(through_z(shrink_weight)), place, ALONG_Y).reshape(width, -1)
-
-    normed_in, scale_in = normal_parts(inputs)
-    first_rows = (normed_in * gain_one + shift_one).astype(low)
+    places = [place ^ d for d in range(4)]
+    sides = [core, 1 - core]
+    depth_rows = heads_rows * seq_size
+    hidden_block = hidden_rows * seq_size
+
+    z_qkv = through_z(jnp.concatenate([query_weight, key_weight, value_weight], 0))
+
+    mine, theirs = split_columns(core, shrink_weight, hidden_block)
+    shard_shrink = jnp.concatenate([mine, swap(theirs, CORE)], 0)
+    mine, theirs = split_columns(along_x, shard_shrink, hidden_block)
+    shard_shrink = jnp.concatenate([mine, swap(theirs, ALONG_X)], 0)
+
+    z_out = through_z(after(output_weight, z_qkv))
+    z_expand = through_z(after(expand_weight, z_out))
+    z_shrink = through_z(after(shard_shrink, z_expand))
+
+    arrived = to_chips(after(jnp.concatenate([tokens, flag_rows], axis=1), z_qkv))
+    inputs = arrived[:, :local_len].reshape(full_len, width)
+    alive = arrived[:, local_len, :local_len].reshape(full_len, 1)
+    active = alive.astype(f32)
+    mask = jnp.broadcast_to((alive - 1) * jnp.bfloat16(1e30), (full_len, HEAD_DIM))
+
+    pieces_qkv = exchange(after(z_qkv, vectors, shard_shrink))
+    mine, theirs = split_columns(core, z_out, depth_rows)
+    rows_out = jnp.concatenate([mine, swap(theirs, CORE)], 1)
+    pieces_out = exchange(after(rows_out, pieces_qkv))
+    across_expand = swap(after(z_expand, pieces_out), ALONG_Y)
+    across_shrink = swap(after(z_shrink, across_expand), ALONG_Y)
+    cotangent_full = to_chips(after(cotangent, z_expand)).reshape(full_len, width)
+
+    half_qkv = 3 * depth_rows // 2
+    w_qkv = arrange(
+        pieces_qkv,
+        (half_qkv, width),
+        [(p, r, 0) for p in range(3) for r in range(2)] + [(3, 0, 0), (4, 0, 0)],
+        [2 * places[d] + r for d in range(4) for r in range(2)],
+    )
+    half_out = depth_rows // 2
+    w_out = arrange(
+        pieces_out,
+        (half_out, width // 2),
+        [(p, r, i) for p in range(3) for r in range(2) for i in range(2)]
+        + [(p, 0, i) for p in (3, 4) for i in range(2)],
+        [2 * (2 * places[d] + sides[i]) + r for d in range(4) for r in range(2) for i in range(2)],
+    )
+    w_expand = arrange(
+        [z_expand, across_expand],
+        (hidden_block // 2, width),
+        [(p, r, 0) for p in range(2) for r in range(2)],
+        [2 * (along_y ^ p) + r for p in range(2) for r in range(2)],
+    )
+    w_shrink = arrange(
+        [z_shrink, across_shrink],
+        (heads_rows, 2 * hidden_block),
+        [(p, (4 * j + 2 * s + t), 0) for p in range(2) for j in range(seq_size) for s in range(2) for t in range(2)],
+        [
+            ((2 * (along_y ^ p) + (along_x ^ s)) * 2 + (core ^ t)) * seq_size + j
+            for p in range(2)
+            for j in range(seq_size)
+            for s in range(2)
+            for t in range(2)
+        ],
+    )
+
+    no_start = jnp.zeros((1,), jnp.int32)
+    half_start = (core * (half_len // ROWS)).reshape(1)
+
+    def half_rows(matrix, which):
+        return lax.dynamic_slice_in_dim(matrix, which * half_len, half_len, 0)
+
+    def own_half(left, weight, dot):
+        got = swap(dot(half_rows(left, 1 - core), weight).astype(low), CORE)
+        return dot(half_rows(left, core), weight), got
+
+    def of_peer(matrix):
+        got = swap(half_rows(matrix, core), ALONG_X)
+        return ordered(core, got, swap(got, CORE), 0)
+
+    (first_rows,) = by_rows(
+        first_kernel,
+        no_start,
+        full_len,
+        [(inputs, "rows"), (gain_one, "vector"), (shift_one, "vector")],
+        [("rows", low)],
+        "first_norm",
+    )
     qkv = (project(first_rows, w_qkv) + bias_rows).astype(low)
     mixed = attend(qkv, mask)
-
-    def both_cores(left, weight, dot):
-        parts = []
-        for start in (0, half_len):
-            own = dot(left[start : start + half_len], weight).astype(low)
-            parts.append(own.astype(f32) + swap(own, CORE).astype(f32))
-        return jnp.concatenate(parts, 0)
-
-    def half_rows(matrix, which):
-        return lax.dynamic_slice_in_dim(matrix, which * half_len, half_len, 0)
-
-    def own_half(left, weight, dot):
-        got = swap(dot(half_rows(left, 1 - core), weight).astype(low), CORE)
-        return dot(half_rows(left, core), weight) + got.astype(f32)
-
-    branch = both_cores(mixed, w_out, project) + bias_out
-    middle = inputs + active * branch
-    normed_mid, scale_mid = normal_parts(middle)
-    second_rows = (normed_mid * gain_two + shift_two).astype(low)
-    hidden_pre = project(second_rows, w_expand) + bias_expand
-    lifted = 0.5 * (1.0 + lax.erf(hidden_pre * (0.5**0.5)))
-    activated = (hidden_pre * lifted).astype(low)
-    slope = lifted + hidden_pre * jnp.exp(-0.5 * hidden_pre * hidden_pre) * ((0.5 / math.pi) ** 0.5)
-    slope = slope.astype(low)
-    shrunk = own_half(activated, w_shrink, project) + bias_shrink
-    out_half = (half_rows(middle, core) + half_rows(active, core) * shrunk).astype(low)
-    layer_out = from_chips(out_half)
-
-    def plane_pieces(matrix):
-        cut = matrix.reshape(matrix.shape[0], 4, -1)
-        return [lax.dynamic_index_in_dim(cut, place ^ d, 1, False) for d in range(4)]
-
-    def z_major(matrix):
-        cut = matrix.reshape(matrix.shape[0], 2, seq_size, heads_rows)
-        return cut.reshape(matrix.shape[0], -1)
-
-    def rows_total(grad, inputs_low, corner_by):
-        pieces = [outer_rows(part, inputs_low).astype(low) for part in plane_pieces(grad)]
-        return total_plane(pieces, corner_by)
-
-    def join_cores(total):
-        cut = total.reshape(2, -1, total.shape[1])
-        mine = lax.dynamic_index_in_dim(cut, core, 0, False)
-        theirs = swap(lax.dynamic_index_in_dim(cut, 1 - core, 0, False), CORE)
-        mine, theirs = (part.reshape(part.shape[0], 4, 1, -1) for part in (mine, theirs))
-        return ordered(core, mine, theirs, 2).reshape(mine.shape[0], -1)
+    branch = project(mixed, w_out).astype(low)
+    middle, second_rows = by_rows(
+        middle_kernel,
+        no_start,
+        full_len,
+        [
+            (inputs, "rows"),
+            (branch, "rows"),
+            (swap(branch, CORE), "rows"),
+            (active, "flag"),
+            (bias_out, "vector"),
+            (gain_two, "vector"),
+            (shift_two, "vector"),
+        ],
+        [("rows", f32), ("rows", low)],
+        "middle_norm",
+    )
+    second_peer = of_peer(second_rows)
+    grad_shrunk = (active * cotangent_full.astype(f32)).astype(low)
+    grad_shrunk_peer = of_peer(grad_shrunk)
+
+    def lift(rows):
+        hidden_pre = project(rows, w_expand) + bias_expand
+        lifted = 0.5 * (1.0 + lax.erf(hidden_pre * (0.5**0.5)))
+        bell = jnp.exp(-0.5 * hidden_pre * hidden_pre) * ((0.5 / math.pi) ** 0.5)
+        return (hidden_pre * lifted).astype(low), (lifted + hidden_pre * bell).astype(low)
+
+    activated, slope = lift(second_rows)
+    activated_peer, slope_peer = lift(second_peer)
 
     def scatter_z(total):
-        return lax.psum_scatter(total, "seq", scatter_dimension=0, tiled=True).astype(f32)
-
-    grad_out = cotangent_full.astype(f32)
-    grad_shrunk = (active * grad_out).astype(low)
-    grad_units = through(grad_shrunk, w_shrink)
+        return lax.psum_scatter(total, "seq", scatter_dimension=0, tiled=True)
+
+    z_first = [
+        (j * 2 + (along_x ^ s)) * 2 + (core ^ t)
+        for s in range(2)
+        for t in range(2)
+        for j in range(seq_size)
+    ]
+    shrink_parts = [
+        outer_rows_of(
+            along_y ^ d,
+            (grad_shrunk, grad_shrunk_peer),
+            (activated, activated_peer),
+            4 * depth_rows,
+            table=z_first,
+        )
+        for d in (1, 0)
+    ]
+    shrink_got = swap(after(shrink_parts[0], across_shrink), ALONG_Y)
+
+    grad_units_peer = through(after(grad_shrunk_peer, shrink_parts[0]), w_shrink)
+    grad_pre_peer = (grad_units_peer * slope_peer.astype(f32)).astype(low)
+    grad_units = through(after(grad_shrunk, grad_pre_peer), w_shrink)
     grad_pre = (grad_units * slope.astype(f32)).astype(low)
-    shrink_weight_grad = scatter_z(join_cores(rows_total(grad_shrunk, activated, ALONG_Y)))
-    grad_second = both_cores(grad_pre, w_expand, through)
-    expand_weight_grad = scatter_z(rows_total(grad_pre, second_rows, ALONG_X))
-    grad_middle = grad_out + normal_back(normed_mid, scale_mid, grad_second * gain_two)
-    grad_branch = (active * grad_middle).astype(low)
+
+    peer_half, peer_got = own_half(grad_pre_peer, w_expand, through)
+    peer_half = (peer_half + peer_got.astype(f32)).astype(low)
+    second_from_peer = swap(peer_half, ALONG_X)
+    second_half, second_got = own_half(after(grad_pre, peer_half), w_expand, through)
+    expand_parts = [
+        outer_rows_of(
+            along_y ^ d,
+            (after(grad_pre, second_half), grad_pre_peer),
+            (second_rows, second_peer),
+            hidden_block,
+        )
+        for d in (1, 0)
+    ]
+    shrink_sum = add_low(shrink_parts[1], after(shrink_got, expand_parts[0]))
+    expand_got = swap(after(expand_parts[0], shrink_got), ALONG_Y)
+
+    grad_middle, grad_branch_half, middle_totals = by_rows(
+        middle_back_kernel,
+        half_start,
+        half_len,
+        [
+            (cotangent_full, "from"),
+            (middle, "from"),
+            (after(second_half, expand_parts[1]), "rows"),
+            (second_got, "rows"),
+            (second_from_peer, "rows"),
+            (active, "flag from"),
+            (gain_two, "vector"),
+        ],
+        [("rows", f32), ("rows", low), ("totals", f32)],
+        "middle_norm_back",
+    )
+    grad_branch = ordered(core, grad_branch_half, swap(grad_branch_half, CORE), 0)
+
     grad_mixed = through(grad_branch, w_out).astype(low)
-    output_weight_grad = scatter_z(join_cores(rows_total(grad_branch, mixed, ALONG_Y)))
-    grad_qkv = attend_back(qkv, grad_mixed, mask)
-    qkv_weight_grad = scatter_z(rows_total(grad_qkv, first_rows, ALONG_X))
-    grad_first = own_half(grad_qkv, w_qkv, through)
-    normed_half, scale_half = half_rows(normed_in, core), half_rows(scale_in, core)
-    grad_half = half_rows(grad_middle, core) + normal_back(
-        normed_half, scale_half, grad_first * gain_one
-    )
-    tokens_grad = from_chips(grad_half.astype(low))
+    out_parts = list(outer_sides(
+        [2 * places[d] + sides[i] for d in range(4) for i in range(2)],
+        after(grad_branch, grad_mixed),
+        mixed,
+        depth_rows,
+    ))
+    out_parts[3] = after(out_parts[3], shrink_got)
+    grad_qkv = attend_back(qkv, after(grad_mixed, out_parts[0]), mask)
+    out_sum = total_plane(out_parts, grad_qkv)
+    expand_sum = add_low(expand_parts[1], after(expand_got, grad_qkv))
+
+    qkv_parts = {}
+    left = grad_qkv
+    for d in (3, 1, 2, 0):
+        qkv_parts[d] = outer_rows_of(places[d], (left,), (first_rows,), 3 * depth_rows)
+        left = after(left, qkv_parts[d])
+    qkv_sum = total_plane([qkv_parts[d] for d in range(4)], None)
+    grad_first, grad_first_got = own_half(left, w_qkv, through)
+    grad_half, first_totals = by_rows(
+        first_back_kernel,
+        half_start,
+        half_len,
+        [
+            (inputs, "from"),
+            (grad_middle, "rows"),
+            (grad_first, "rows"),
+            (grad_first_got, "rows"),
+            (gain_one, "vector"),
+        ],
+        [("rows", low), ("totals", f32)],
+        "first_norm_back",
+    )
+    tokens_grad = from_chips(grad_half)
+
+    shrunk_peer, shrunk_peer_got = own_half(after(activated_peer, grad_half), w_shrink, project)
+    shrunk_from_peer = swap((shrunk_peer + shrunk_peer_got.astype(f32)).astype(low), ALONG_X)
+    shrunk, shrunk_got = own_half(after(activated, shrunk_peer), w_shrink, project)
+    shrunk = shrunk + shrunk_got.astype(f32) + shrunk_from_peer.astype(f32) + bias_shrink
+    out_half_rows = (half_rows(middle, core) + half_rows(active, core) * shrunk).astype(low)
+    layer_out = from_chips(out_half_rows)
+
+    shrink_rows = scatter_z(shrink_sum)
+    half = shrink_rows.shape[0] // 2
+    shrink_rows = weave_columns(
+        along_x, shrink_rows[:half], swap(shrink_rows[half:], ALONG_X), hidden_block
+    )
+    shrink_weight_grad = weave_columns(
+        core, shrink_rows[:heads_rows], swap(shrink_rows[heads_rows:], CORE), hidden_block
+    ).astype(f32)
+    expand_weight_grad = scatter_z(expand_sum).astype(f32)
+    out_rows = weave_columns(
+        core, out_sum[:, : width // 2], swap(out_sum[:, width // 2 :], CORE), depth_rows
+    )
+    output_weight_grad = scatter_z(out_rows).astype(f32)
+    qkv_weight_grad = scatter_z(qkv_sum).astype(f32)
 
     def column_sum(matrix):
         return jnp.sum(matrix.astype(f32), axis=0)
 
     def all_devices(totals, rows):
-        return totals.reshape(dp_size * seq_size, rows)
+        return totals.reshape(devices, rows)
 
     def core_devices(totals, rows):
         cut = totals.reshape(4, 1, seq_size, rows)
-        return ordered(core, cut, jnp.zeros_like(cut), 1).reshape(dp_size * seq_size, rows)
+        return ordered(core, cut, jnp.zeros_like(cut), 1).reshape(devices, rows)
+
+    def quarter_devices(totals, rows):
+        cut = totals.reshape(2, 1, seq_size, rows)
+        none = jnp.zeros_like(cut)
+        quarters = [jnp.where(2 * along_x + core == q, cut, none) for q in range(4)]
+        return jnp.concatenate(quarters, 1).reshape(devices, rows)
 
     qkv_sums = column_sum(grad_qkv).reshape(4 * seq_size, 3, heads_rows)
     sums = jnp.concatenate(
         [
-            all_devices(column_sum(grad_first * normed_half), heads_rows),
-            all_devices(column_sum(grad_first), heads_rows),
+            all_devices(first_totals[0], heads_rows),
+            all_devices(first_totals[1], heads_rows),
             core_devices(qkv_sums[:, 0], heads_rows),
             core_devices(qkv_sums[:, 2], heads_rows),
-            all_devices(0.5 * column_sum(grad_branch), heads_rows),
-            all_devices(0.5 * column_sum(grad_second * normed_mid), heads_rows),
-            all_devices(0.5 * column_sum(grad_second), heads_rows),
+            all_devices(middle_totals[2], heads_rows),
+            all_devices(middle_totals[0], heads_rows),
+            all_devices(middle_totals[1], heads_rows),
             all_devices(0.5 * column_sum(grad_shrunk), heads_rows),
-            core_devices(column_sum(grad_pre), hidden_rows),
+            quarter_devices(column_sum(grad_pre) + column_sum(grad_pre_peer), hidden_rows),
         ],
         axis=1,
     )
-    sums = lax.psum_scatter(sums.reshape(-1), ("dp", "seq"), scatter_dimension=0, tiled=True)
+    to_relative = ((all_dp ^ dp) * seq_size + (all_seq + depth) % seq_size).reshape(-1)
+    sums = sums[to_relative].reshape(dp_size, seq_size, -1)
+    for bit in (ALONG_Y, ALONG_X, CORE):
+        sums = sums[:bit] + swap(sums[bit:], bit)
+    sums = sums[0]
+    sums = sums[0] + sum(shift_z(sums[steps], steps) for steps in range(1, seq_size))
 
     def vector_grad(index):
         return sums[index * heads_rows : (index + 1) * heads_rows]

time: 3180 us -> 1240 us (0.39)
  Pallas kernels: 1610 us -> 265 us
  blocking collectives: 162 us -> 0 us
  local copies, waits for them, and re-layouts: 203 us -> 54.3 us
  waiting for transfers between devices: 686 us -> 546 us
  matrix products: 264 us -> 180 us
  other arithmetic: 174 us -> 95.8 us
    pallas_call x4 -> x23, Pallas kernels: 1530 us -> 185 us  [the longest x8 80.4 us: outer_rows_of(): pl.pallas_call(kernel, grid_spec=pltpu.PrefetchScalarGridSpec(num_scalar_...]
    ppermute x36 -> x47, waiting for transfers between devices: 463 us -> 268 us  [swap(): return lax.ppermute(values, 'dp', [(i, i ^ bit) for i in range(size)])]
    all_gather x1 -> x0, blocking collectives: 162 us -> none  [whole_sequence_device(): vectors = lax.all_gather(vectors, ('dp', 'seq'), axis=0, tiled=True)]
    ppermute x2, waiting for transfers between devices: 0.01 us -> 95.3 us  [to_chips(): second = lax.ppermute(second, ('dp', 'seq'), route(True))]
    dot_general x16 -> x0, matrix products: 94.5 us -> none  [outer_rows(): lax.dot_general(grad_cols, inputs, (((0,), (0,)), ((), ())), preferred_el...]
    dynamic_slice x8 -> x0, local copies, waits for them, and re-layouts: 84.7 us -> none  [the longest x2 41.9 us: plane_pieces(): lax.dynamic_index_in_dim(cut, place ^ d, 1, False)]
    all_gather x4, waiting for transfers between devices: 109 us -> 30.9 us  [through_z(): return lax.all_gather(shard, 'seq', axis=0, tiled=True)]
    ppermute x2, waiting for transfers between devices: 5.82 us -> 82 us  [to_chips(): first = lax.ppermute(first, ('dp', 'seq'), route(False))]
  transfers between devices with their start and end apart: 53 -> 69, of which waited for: 20 -> 25; matrix products, arithmetic and copies ran while one was open for 18% -> 23% of each run, Pallas kernels for 35% -> 20%
where the time goes in v2:
time: 1240 us; the launch traced here: 1230 us
  waiting for transfers between devices  546 us (44%)
  Pallas kernels  265 us (21%)
  matrix products  180 us (15%)
  other arithmetic  95.8 us (8%)
  starting transfers between devices  74 us (6%)
  local copies, waits for them, and re-layouts  54.3 us (4%)
  between operations  15.3 us (1%)
    ppermute x47, waiting for transfers between devices, swap(): return lax.ppermute(values, 'dp', [(i, i ^ bit) for i in range(size)])  268 us
    ppermute x2, waiting for transfers between devices, to_chips(): second = lax.ppermute(second, ('dp', 'seq'), route(True))  95.3 us
    dot_general x9, matrix products, through(): return jnp.dot(left, weight, preferred_element_type=jnp.float32)  91.7 us
    dot_general x8, matrix products, project(): lax.dot_general(left, weight, (((1,), (1,)), ((), ())), preferred_element...  88.3 us
    ppermute x2, waiting for transfers between devices, to_chips(): first = lax.ppermute(first, ('dp', 'seq'), route(False))  82 us
    pallas_call x8, Pallas kernels, outer_rows_of(): pl.pallas_call(kernel, grid_spec=pltpu.PrefetchScalarGridSpec(num_scalar_...  80.4 us
    pallas_call x1, Pallas kernels, attend_back(): pl.pallas_call(attend_back_kernel, grid=(pairs,), in_specs=[pl.BlockSpec(...  50.1 us
    pallas_call x4, Pallas kernels, arrange(): pl.pallas_call(kernel, grid_spec=pltpu.PrefetchScalarGridSpec(num_scalar_...  42.9 us
  transfers between devices with their start and end apart: 69, of which 25 were waited for; matrix products, arithmetic and copies ran while one was open for 23% of the time, Pallas kernels for 20%

profile of v2, /device:TPU:9, one launch (start us, length us, event | category | flops | bytes accessed | tf_op | source)
XLA Modules:
  0.0 1231.1 jit_solution(8842049874462785096)
XLA Ops:
  42.4 30.9 %all-gather.5.cloned.1.call-done.refs_0_ = bf16[768,2048]{1,0:T(8,128)(2,1)} async-done(((bf16[192,2048]{1,0:T(8,128)(2,1)}), bf16[768,2048]{1,0:T(8,128)(2,1)}) %all-gather.5.cloned.1.call-update) | async-done | bytes 3145744 | tf_op jit(solution)/shard_map/all_gather | solution.py:641
  83.1 40.5 %collective-permute-done = bf16[272,2048]{1,0:T(8,128)(2,1)S(1)} collective-permute-done((bf16[272,2048]{1,0:T(8,128)(2,1)}, bf16[272,2048]{1,0:T(8,128)(2,1)S(1)}, u32[]{:S(2)}, u32[]{:S(2)}) %collective-permute-start) | collective-permute-done | bytes 1114144 | tf_op jit(solution)/shard_map/ppermute | solution.py:575
  123.5 25.0 %collective-permute-done.1 = bf16[272,2048]{1,0:T(8,128)(2,1)S(1)} collective-permute-done((bf16[272,2048]{1,0:T(8,128)(2,1)S(1)}, bf16[272,2048]{1,0:T(8,128)(2,1)S(1)}, u32[]{:S(2)}, u32[]{:S(2)}) %collective-permute-start.1) | collective-permute-done | bytes 1114144 | tf_op jit(solution)/shard_map/ppermute | solution.py:576
  175.7 17.9 %collective-permute-done.14.refs_4_ = bf16[384,2048]{1,0:T(8,128)(2,1)S(1)} collective-permute-done((bf16[384,2048]{1,0:T(8,128)(2,1)}, bf16[384,2048]{1,0:T(8,128)(2,1)S(1)}, u32[]{:S(2)}, u32[]{:S(2)}) %collective-permute-start.14) | collective-permute-done | bytes 1572896 | tf_op jit(solution)/shard_map/ppermute | solution.py:49
  209.0 17.2 %add_convert_fusion.rows_ref = bf16[1024,3072]{1,0:T(8,128)(2,1)} fusion(bf16[1024,2048]{1,0:T(8,128)(2,1)S(1)} %first_norm.1.refs_2_, bf16[3072,2048]{1,0:T(8,128)(2,1)} %arrange.4, f32[3072]{0:T(1024)S(1)} %add.630), kind=kOutput, calls=%fused_computation.5 | convolution fusion | flops 12891193344 | bytes 23080960 | tf_op jit(solution)/shard_map/dot_general | solution.py:24
  228.2 29.8 %attend.1.right = bf16[1024,1024]{1,0:T(8,128)(2,1)S(1)} custom-call(bf16[1024,3072]{1,0:T(8,128)(2,1)} %add_convert_fusion.rows_ref, bf16[1024,64]{1,0:T(8,128)(2,1)S(1)} %broadcast_in_dim.49.mask_ref), custom_call_target="tpu_custom_call" | custom-call | flops 17179869184 | bytes 25165824 | tf_op jit(solution)/shard_map/attend/pallas_call | solution.py:390
  280.0 41.5 %collective-permute-done.24 = bf16[256,2048]{1,0:T(8,128)(2,1)S(1)} collective-permute-done((bf16[256,2048]{1,0:T(8,128)(2,1)}, bf16[256,2048]{1,0:T(8,128)(2,1)S(1)}, u32[]{:S(2)}, u32[]{:S(2)}) %collective-permute-start.24) | collective-permute-done | bytes 1048608 | tf_op jit(solution)/shard_map/ppermute | solution.py:575
  321.6 70.2 %collective-permute-done.25 = bf16[256,2048]{1,0:T(8,128)(2,1)S(1)} collective-permute-done((bf16[256,2048]{1,0:T(8,128)(2,1)S(1)}, bf16[256,2048]{1,0:T(8,128)(2,1)S(1)}, u32[]{:S(2)}, u32[]{:S(2)}) %collective-permute-start.25) | collective-permute-done | bytes 1048608 | tf_op jit(solution)/shard_map/ppermute | solution.py:576
  417.0 37.2 %collective-permute-done.22 = bf16[512,2048]{1,0:T(8,128)(2,1)} collective-permute-done((bf16[512,2048]{1,0:T(8,128)(2,1)S(1)}, bf16[512,2048]{1,0:T(8,128)(2,1)}, u32[]{:S(2)}, u32[]{:S(2)}) %collective-permute-start.22) | collective-permute-done | bytes 2097184 | tf_op jit(solution)/shard_map/ppermute | solution.py:49
  459.6 28.4 %collective-permute-done.21.refs_1_ = bf16[1024,2048]{1,0:T(8,128)(2,1)} collective-permute-done((bf16[1024,2048]{1,0:T(8,128)(2,1)}, bf16[1024,2048]{1,0:T(8,128)(2,1)}, u32[]{:S(2)}, u32[]{:S(2)}) %collective-permute-start.21) | collective-permute-done | bytes 4194336 | tf_op jit(solution)/shard_map/ppermute | solution.py:49
  518.3 15.5 %multiply_convert_fusion.5 = (bf16[1024,2048]{1,0:T(8,128)(2,1)}, bf16[1024,2048]{1,0:T(8,128)(2,1)}, f32[1024,2048]{1,0:T(8,128)}) fusion(f32[2048]{0:T(1024)S(1)} %bitcast.201, f32[1024,2048]{1,0:T(8,128)} %fusion.58, bf16[1024,2048]{1,0:T(8,128)(2,1)S(1)} %copy-done.10, bf16[2048,2048]{1,0:T(8,128)(2,1)S(1)} %copy-done.23), kind=kOutput, calls=%fused_computation.27 | convolution fusion | flops 8615100416 | bytes 37756928 | tf_op jit(solution)/shard_map/dot_general | solution.py:24
  538.1 14.0 %outer_rows_of.8 = bf16[1024,2048]{1,0:T(8,128)(2,1)S(1)} custom-call(s32[1]{0:T(128)} %bitcast.53.refs_0_, s32[16]{0:T(128)S(1)} %stack.358.refs_1_, bf16[1024,2048]{1,0:T(8,128)(2,1)} %copy-done.20, bf16[1024,2048]{1,0:T(8,128)(2,1)} %maximum_select_fusion.3.refs_3_, bf16[1024,2048]{1,0:T(8,128)(2,1)} %get-tuple-element.95.refs_4_, ...), custom_call_target="tpu_custom_call" | custom-call | flops 8589934592 | bytes 16777216 | tf_op jit(solution)/shard_map/outer_rows_of/pallas_call | solution.py:190
  552.1 40.8 %collective-permute-done.29.refs_1_ = bf16[1024,2048]{1,0:T(8,128)(2,1)S(1)} collective-permute-done((bf16[1024,2048]{1,0:T(8,128)(2,1)}, bf16[1024,2048]{1,0:T(8,128)(2,1)S(1)}, u32[]{:S(2)}, u32[]{:S(2)}) %collective-permute-start.29) | collective-permute-done | bytes 4194336 | tf_op jit(solution)/shard_map/ppermute | solution.py:49
  594.9 17.0 %arrange.7 = bf16[2048,2048]{1,0:T(8,128)(2,1)} custom-call(s32[32]{0:T(128)S(1)} %stack.391.table_ref, bf16[1024,2048]{1,0:T(8,128)(2,1)S(1)} %copy-done.4, bf16[1024,2048]{1,0:T(8,128)(2,1)} %copy-done.24), custom_call_target="tpu_custom_call" | custom-call | bytes 16777216 | tf_op jit(solution)/shard_map/arrange/pallas_call | solution.py:92
  611.9 16.1 %convert_reduce_fusion.1 = (f32[2048]{0:T(1024)S(1)}, bf16[1024,2048]{1,0:T(8,128)(2,1)S(1)}) fusion(f32[1024,2048]{1,0:T(8,128)} %fusion.58, f32[2048]{0:T(1024)S(1)} %bitcast.202, bf16[1024,2048]{1,0:T(8,128)(2,1)} %maximum_select_fusion.3.refs_3_, bf16[2048,2048]{1,0:T(8,128)(2,1)} %arrange.7), kind=kOutput, calls=%fused_computation.18 | convolution fusion | flops 8621389824 | bytes 25182208 | tf_op jit(solution)/shard_map/dot_general | solution.py:30
  640.8 14.8 %convert_reduce_fusion.2 = (f32[2048]{0:T(1024)S(1)}, bf16[1024,2048]{1,0:T(8,128)(2,1)}) fusion(f32[1024,2048]{1,0:T(8,128)} %get-tuple-element.170, f32[2048]{0:T(1024)S(1)} %bitcast.203, bf16[1024,2048]{1,0:T(8,128)(2,1)S(1)} %copy-done.21, bf16[2048,2048]{1,0:T(8,128)(2,1)S(1)} %copy-done.22), kind=kOutput, calls=%fused_computation.19 | convolution fusion | flops 8621389824 | bytes 25182208 | tf_op jit(solution)/shard_map/dot_general | solution.py:30
  696.2 15.2 %collective-permute-done.32.peer = bf16[512,2048]{1,0:T(8,128)(2,1)S(1)} collective-permute-done((bf16[512,2048]{1,0:T(8,128)(2,1)S(1)}, bf16[512,2048]{1,0:T(8,128)(2,1)S(1)}, u32[]{:S(2)}, u32[]{:S(2)}) %collective-permute-start.32) | collective-permute-done | bytes 2097184 | tf_op jit(solution)/shard_map/ppermute | solution.py:49
  797.1 50.1 %attend_back.1.refs_1_ = bf16[1024,3072]{1,0:T(8,128)(2,1)} custom-call(bf16[1024,3072]{1,0:T(8,128)(2,1)} %add_convert_fusion.rows_ref, bf16[1024,1024]{1,0:T(8,128)(2,1)S(1)} %convolution_convert_fusion.5.grad_ref, bf16[1024,64]{1,0:T(8,128)(2,1)S(1)} %copy-done.14), custom_call_target="tpu_custom_call" | custom-call | flops 42949672960 | bytes 25165824 | tf_op jit(solution)/shard_map/attend_back/pallas_call | solution.py:411
  860.9 44.2 %collective-permute-done.56 = bf16[256,2048]{1,0:T(8,128)(2,1)S(1)} collective-permute-done((bf16[256,2048]{1,0:T(8,128)(2,1)}, bf16[256,2048]{1,0:T(8,128)(2,1)S(1)}, u32[]{:S(2)}, u32[]{:S(2)}) %collective-permute-start.56) | collective-permute-done | bytes 1048608 | tf_op jit(solution)/shard_map/ppermute | solution.py:49
  963.3 16.2 %collective-permute-done.50 = bf16[384,2048]{1,0:T(8,128)(2,1)S(1)} collective-permute-done((bf16[384,2048]{1,0:T(8,128)(2,1)}, bf16[384,2048]{1,0:T(8,128)(2,1)S(1)}, u32[]{:S(2)}, u32[]{:S(2)}) %collective-permute-start.50) | collective-permute-done | bytes 1572896 | tf_op jit(solution)/shard_map/ppermute | solution.py:49
  1025.4 26.6 %collective-permute-done.42 = f32[4,4,768]{2,1,0:T(4,128)S(1)} collective-permute-done((f32[4,4,768]{2,1,0:T(4,128)S(1)}, f32[4,4,768]{2,1,0:T(4,128)S(1)}, u32[]{:S(2)}, u32[]{:S(2)}) %collective-permute-start.42) | collective-permute-done | bytes 49184 | tf_op jit(solution)/shard_map/ppermute | solution.py:49
  1095.9 15.6 %collective-permute-done.37 = bf16[512,2048]{1,0:T(8,128)(2,1)S(1)} collective-permute-done((bf16[512,2048]{1,0:T(8,128)(2,1)}, bf16[512,2048]{1,0:T(8,128)(2,1)S(1)}, u32[]{:S(2)}, u32[]{:S(2)}) %collective-permute-start.37) | collective-permute-done | bytes 2097184 | tf_op jit(solution)/shard_map/ppermute | solution.py:49
  1125.7 39.6 %collective-permute-done.46 = f32[768]{0:T(1024)S(1)} collective-permute-done((f32[768]{0:T(1024)S(1)}, f32[768]{0:T(1024)S(1)}, u32[]{:S(2)}, u32[]{:S(2)}) %collective-permute-start.46) | collective-permute-done | bytes 3104 | tf_op jit(solution)/shard_map/ppermute | solution.py:598
  1193.2 21.7 %collective-permute-done.39 = bf16[256,2048]{1,0:T(8,128)(2,1)} collective-permute-done((bf16[256,2048]{1,0:T(8,128)(2,1)S(1)}, bf16[256,2048]{1,0:T(8,128)(2,1)}, u32[]{:S(2)}, u32[]{:S(2)}) %collective-permute-start.39) | collective-permute-done | bytes 1048608 | tf_op jit(solution)/shard_map/ppermute | solution.py:585
  (388 shorter events, 529.6 us)
Async XLA Ops:
  9.3 141.2 %all-gather.7.cloned.1.call-start = ((), (), s32[]{:S(2)}) async-start(), calls=%async_computation.5 | async-start | bytes 1310720 | tf_op jit(solution)/shard_map/all_gather | solution.py:641
  73.2 81.3 %collective-permute-start.12 = (bf16[768,2048]{1,0:T(8,128)(2,1)}, bf16[768,2048]{1,0:T(8,128)(2,1)}, u32[]{:S(2)}, u32[]{:S(2)}) collective-permute-start(bf16[768,2048]{1,0:T(8,128)(2,1)} %all-gather.5.cloned.1.call-done.refs_0_), channel_id=1, source_target_pairs={{0,16},{4,20},{8,24},{12,28},{16,0},{20,4},{24,8},{28,12},{1,17},{... | collective-permute-start | bytes 9437192 | tf_op jit(solution)/shard_map/ppermute | solution.py:49
  74.4 83.1 %collective-permute-start.11 = (bf16[768,2048]{1,0:T(8,128)(2,1)}, bf16[768,2048]{1,0:T(8,128)(2,1)}, u32[]{:S(2)}, u32[]{:S(2)}) collective-permute-start(bf16[768,2048]{1,0:T(8,128)(2,1)} %all-gather.5.cloned.1.call-done.refs_0_), channel_id=1, source_target_pairs={{0,8},{4,12},{8,0},{12,4},{16,24},{20,28},{24,16},{28,20},{1,9},{5... | collective-permute-start | bytes 9437192 | tf_op jit(solution)/shard_map/ppermute | solution.py:49
  83.0 192.7 %all-gather.9.cloned.1.call-start = ((), (), s32[]{:S(2)}) async-start(), calls=%async_computation.6 | async-start | bytes 5242880 | tf_op jit(solution)/shard_map/all_gather | solution.py:641
  160.8 339.7 %all-gather.11.cloned.1.call-start = ((), (), s32[]{:S(2)}) async-start(), calls=%async_computation.7 | async-start | bytes 5242880 | tf_op jit(solution)/shard_map/all_gather | solution.py:641
  273.5 122.5 %collective-permute-start.20 = (bf16[1024,2048]{1,0:T(8,128)(2,1)}, bf16[1024,2048]{1,0:T(8,128)(2,1)}, u32[]{:S(2)}, u32[]{:S(2)}) collective-permute-start(bf16[1024,2048]{1,0:T(8,128)(2,1)} %convolution_convert_fusion.own), channel_id=1, source_target_pairs={{0,4},{4,0},{8,12},{12,8},{16,20},{20,16},{24,28},{28,24},{1,5},{5... | collective-permute-start | bytes 12582920 | tf_op jit(solution)/shard_map/ppermute | solution.py:49
  278.8 113.0 %collective-permute-start.25 = (bf16[256,2048]{1,0:T(8,128)(2,1)S(1)}, bf16[256,2048]{1,0:T(8,128)(2,1)S(1)}, u32[]{:S(2)}, u32[]{:S(2)}) collective-permute-start(bf16[256,2048]{1,0:T(8,128)(2,1)S(1)} %get-tuple-element.131), channel_id=1, source_target_pairs={{0,1},{1,0},{2,5},{3,4},{4,3},{5,2},{6,7},{7,6},{8,9},{9,8},{10,13... | collective-permute-start | bytes 3145736 | tf_op jit(solution)/shard_map/ppermute | solution.py:576
  279.8 814.0 %reduce-scatter.11.cloned.1.call-start = ((), (), s32[]{:S(2)}) async-start(), calls=%async_computation.11 | async-start | bytes 5242880 | tf_op jit(solution)/shard_map/reduce_scatter | solution.py:762
  395.9 92.0 %collective-permute-start.21 = (bf16[1024,2048]{1,0:T(8,128)(2,1)}, bf16[1024,2048]{1,0:T(8,128)(2,1)}, u32[]{:S(2)}, u32[]{:S(2)}) collective-permute-start(bf16[1024,2048]{1,0:T(8,128)(2,1)} %all-gather.9.cloned.1.call-done.refs_0_), channel_id=1, source_target_pairs={{0,16},{4,20},{8,24},{12,28},{16,0},{20,4},{24,8},{28,12},{1,17},{... | collective-permute-start | bytes 12582920 | tf_op jit(solution)/shard_map/ppermute | solution.py:49
  415.9 83.3 %collective-permute-start.27 = (bf16[512,2048]{1,0:T(8,128)(2,1)S(1)}, bf16[512,2048]{1,0:T(8,128)(2,1)}, u32[]{:S(2)}, u32[]{:S(2)}) collective-permute-start(bf16[512,2048]{1,0:T(8,128)(2,1)S(1)} %constant_dynamic-slice_fusion), channel_id=1, source_target_pairs={{0,8},{4,12},{8,0},{12,4},{16,24},{20,28},{24,16},{28,20},{1,9},{5... | collective-permute-start | bytes 6291464 | tf_op jit(solution)/shard_map/ppermute | solution.py:49
  500.5 92.3 %collective-permute-start.29 = (bf16[1024,2048]{1,0:T(8,128)(2,1)}, bf16[1024,2048]{1,0:T(8,128)(2,1)S(1)}, u32[]{:S(2)}, u32[]{:S(2)}) collective-permute-start(bf16[1024,2048]{1,0:T(8,128)(2,1)} %all-gather.11.cloned.1.call-done.refs_0_), channel_id=1, source_target_pairs={{0,16},{4,20},{8,24},{12,28},{16,0},{20,4},{24,8},{28,12},{1,17},{... | collective-permute-start | bytes 12582920 | tf_op jit(solution)/shard_map/ppermute | solution.py:49
  639.4 111.4 %collective-permute-start.52 = (bf16[1024,2048]{1,0:T(8,128)(2,1)S(1)}, bf16[1024,2048]{1,0:T(8,128)(2,1)}, u32[]{:S(2)}, u32[]{:S(2)}) collective-permute-start(bf16[1024,2048]{1,0:T(8,128)(2,1)S(1)} %outer_rows_of.8), channel_id=1, source_target_pairs={{0,16},{4,20},{8,24},{12,28},{16,0},{20,4},{24,8},{28,12},{1,17},{... | collective-permute-start | bytes 12582920 | tf_op jit(solution)/shard_map/ppermute | solution.py:49
  757.3 420.7 %reduce-scatter.7.cloned.1.call-start = ((), (), s32[]{:S(2)}) async-start(), calls=%async_computation.9 | async-start | bytes 1310720 | tf_op jit(solution)/shard_map/reduce_scatter | solution.py:762
  779.6 164.9 %collective-permute-start.58 = (bf16[1024,2048]{1,0:T(8,128)(2,1)}, bf16[1024,2048]{1,0:T(8,128)(2,1)}, u32[]{:S(2)}, u32[]{:S(2)}) collective-permute-start(bf16[1024,2048]{1,0:T(8,128)(2,1)} %copy-done.17), channel_id=1, source_target_pairs={{0,16},{4,20},{8,24},{12,28},{16,0},{20,4},{24,8},{28,12},{1,17},{... | collective-permute-start | bytes 12582920 | tf_op jit(solution)/shard_map/ppermute | solution.py:49
  793.9 111.2 %collective-permute-start.56 = (bf16[256,2048]{1,0:T(8,128)(2,1)}, bf16[256,2048]{1,0:T(8,128)(2,1)S(1)}, u32[]{:S(2)}, u32[]{:S(2)}) collective-permute-start(bf16[256,2048]{1,0:T(8,128)(2,1)} %fusion.33), channel_id=1, source_target_pairs={{0,16},{4,20},{8,24},{12,28},{16,0},{20,4},{24,8},{28,12},{1,17},{... | collective-permute-start | bytes 3145736 | tf_op jit(solution)/shard_map/ppermute | solution.py:49
  796.0 109.1 %collective-permute-start.54 = (bf16[256,2048]{1,0:T(8,128)(2,1)}, bf16[256,2048]{1,0:T(8,128)(2,1)S(1)}, u32[]{:S(2)}, u32[]{:S(2)}) collective-permute-start(bf16[256,2048]{1,0:T(8,128)(2,1)} %fusion.32), channel_id=1, source_target_pairs={{0,8},{4,12},{8,0},{12,4},{16,24},{20,28},{24,16},{28,20},{1,9},{5... | collective-permute-start | bytes 3145736 | tf_op jit(solution)/shard_map/ppermute | solution.py:49
  926.6 292.3 %reduce-scatter.9.cloned.1.call-start = ((), (), s32[]{:S(2)}) async-start(), calls=%async_computation.10 | async-start | bytes 5242880 | tf_op jit(solution)/shard_map/reduce_scatter | solution.py:762
  951.1 270.6 %reduce-scatter.5.cloned.1.call-start = ((), (), s32[]{:S(2)}) async-start(), calls=%async_computation.8 | async-start | bytes 3932160 | tf_op jit(solution)/shard_map/reduce_scatter | solution.py:762
  982.7 70.0 %collective-permute-start.51 = (bf16[768,2048]{1,0:T(8,128)(2,1)}, bf16[768,2048]{1,0:T(8,128)(2,1)}, u32[]{:S(2)}, u32[]{:S(2)}) collective-permute-start(bf16[768,2048]{1,0:T(8,128)(2,1)} %fusion.31), channel_id=1, source_target_pairs={{0,16},{4,20},{8,24},{12,28},{16,0},{20,4},{24,8},{28,12},{1,17},{... | collective-permute-start | bytes 9437192 | tf_op jit(solution)/shard_map/ppermute | solution.py:49
  1025.4 70.5 %collective-permute-start.35 = (bf16[512,2048]{1,0:T(8,128)(2,1)}, bf16[512,2048]{1,0:T(8,128)(2,1)}, u32[]{:S(2)}, u32[]{:S(2)}) collective-permute-start(bf16[512,2048]{1,0:T(8,128)(2,1)} %convolution_convert_fusion.2), channel_id=1, source_target_pairs={{0,4},{4,0},{8,12},{12,8},{16,20},{20,16},{24,28},{28,24},{1,5},{5... | collective-permute-start | bytes 6291464 | tf_op jit(solution)/shard_map/ppermute | solution.py:49
  1081.6 92.5 %collective-permute-start.40 = (bf16[256,2048]{1,0:T(8,128)(2,1)}, bf16[256,2048]{1,0:T(8,128)(2,1)}, u32[]{:S(2)}, u32[]{:S(2)}) collective-permute-start(bf16[256,2048]{1,0:T(8,128)(2,1)} %get-tuple-element.126), channel_id=1, source_target_pairs={{0,0},{1,1},{4,2},{5,3},{2,4},{3,5},{6,6},{7,7},{8,8},{9,9},{12,10... | collective-permute-start | bytes 3145736 | tf_op jit(solution)/shard_map/ppermute | solution.py:584
  1083.5 90.6 %collective-permute-start.41 = (bf16[256,2048]{1,0:T(8,128)(2,1)S(1)}, bf16[256,2048]{1,0:T(8,128)(2,1)}, u32[]{:S(2)}, u32[]{:S(2)}) collective-permute-start(bf16[256,2048]{1,0:T(8,128)(2,1)S(1)} %get-tuple-element.127), channel_id=1, source_target_pairs={{1,0},{0,1},{5,2},{4,3},{3,4},{2,5},{7,6},{6,7},{9,8},{8,9},{13,10... | collective-permute-start | bytes 3145736 | tf_op jit(solution)/shard_map/ppermute | solution.py:585
  1084.9 80.3 %collective-permute-start.46 = (f32[768]{0:T(1024)S(1)}, f32[768]{0:T(1024)S(1)}, u32[]{:S(2)}, u32[]{:S(2)}) collective-permute-start(f32[768]{0:T(1024)S(1)} %get-tuple-element.112), channel_id=1, source_target_pairs={{0,2},{1,3},{2,0},{3,1},{4,6},{5,7},{6,4},{7,5},{8,10},{9,11},{10,... | collective-permute-start | bytes 9224 | tf_op jit(solution)/shard_map/ppermute | solution.py:598
  1095.9 71.2 %collective-permute-start.47 = (f32[768]{0:T(1024)S(1)}, f32[768]{0:T(1024)S(1)}, u32[]{:S(2)}, u32[]{:S(2)}) collective-permute-start(f32[768]{0:T(1024)S(1)} %get-tuple-element.113), channel_id=1, source_target_pairs={{0,3},{1,0},{2,1},{3,2},{4,7},{5,4},{6,5},{7,6},{8,11},{9,8},{10,9... | collective-permute-start | bytes 9224 | tf_op jit(solution)/shard_map/ppermute | solution.py:598
  (91 other events, 1964.4 us)
Sparse Core Ops, SparseCore 0:
  10.2 62.9 all-gather.4
  83.2 42.0 all-gather.6
  160.9 78.5 all-gather.8
  279.9 112.0 all-gather.10
  757.4 75.5 reduce-scatter.10
  926.8 23.1 reduce-scatter.6
  952.2 77.4 reduce-scatter.8
  1062.2 84.7 reduce-scatter.4

commit v3 on v2

--- a/solution.py
+++ b/solution.py
@@ -5,7 +5,7 @@
 from jax import lax
 from jax.experimental import pallas as pl
 from jax.experimental.pallas import tpu as pltpu
-from jax.sharding import PartitionSpec as P
+from jax.sharding import Mesh, PartitionSpec as P
 
 HEAD_DIM = 64
 LAYER = 12
@@ -44,12 +44,14 @@
     return jnp.sum(matrix, axis=0, dtype=jnp.float32)
 
 
-def swap(values, bit):
-    size = lax.axis_size("dp")
-    return lax.ppermute(values, "dp", [(i, i ^ bit) for i in range(size)])
-
-
-CORE, ALONG_X, ALONG_Y = 1, 2, 4
+BRIEF = pl.CostEstimate(flops=1, bytes_accessed=1, transcendentals=0)
+
+CORE, ALONG_X, ALONG_Y = "core", "x", "y"
+DEVICES = ("y", "x", "core", "seq")
+
+
+def swap(values, axis):
+    return lax.ppermute(values, axis, [(0, 1), (1, 0)])
 
 
 def pick(flag, first, second):
@@ -99,7 +101,7 @@
         ),
         out_shape=jax.ShapeDtypeStruct((steps * block[0], block[1]), pieces[0].dtype),
         compiler_params=pltpu.CompilerParams(vmem_limit_bytes=48 << 20),
-        cost_estimate=pl.CostEstimate(flops=0, bytes_accessed=4 * total, transcendentals=0),
+        cost_estimate=BRIEF,
         name="arrange",
     )(table, *pieces)
 
@@ -125,9 +127,7 @@
             out_specs=[pl.BlockSpec((rows, block), lambda i, core_ref: (0, i))] * 2,
         ),
         out_shape=(piece, piece),
-        cost_estimate=pl.CostEstimate(
-            flops=0, bytes_accessed=4 * rows * columns, transcendentals=0
-        ),
+        cost_estimate=BRIEF,
         name="split_columns",
     )(core.reshape(1), matrix, matrix)
 
@@ -157,54 +157,44 @@
             out_specs=pl.BlockSpec((rows, 2 * block), lambda i, core_ref: (0, i)),
         ),
         out_shape=jax.ShapeDtypeStruct((rows, 2 * columns), mine.dtype),
-        cost_estimate=pl.CostEstimate(
-            flops=0, bytes_accessed=8 * rows * columns, transcendentals=0
-        ),
+        cost_estimate=BRIEF,
         name="weave_columns",
     )(core.reshape(1), mine, theirs)
 
 
-def outer_rows_of(index, lefts, rights, rows, tile=512, table=None):
+def outer_rows_of(lefts, rights, rows, sources, tile=512, runs=None):
     count, columns = rights[0].shape
-    terms = len(lefts)
-    scalars = [jnp.asarray(index, jnp.int32).reshape(1)]
-    if table is not None:
-        scalars.append(jnp.stack([jnp.asarray(target, jnp.int32) for target in table]))
-
-    def kernel(*refs):
-        operands = refs[len(scalars) :]
+    terms, blocks = len(lefts), len(sources)
+    table = jnp.stack([jnp.asarray(index, jnp.int32) for index in [*sources, *(runs or [])]])
+
+    def kernel(table_ref, *refs):
         total = 0.0
-        for left, right in zip(operands[:terms], operands[terms : 2 * terms]):
+        for left, right in zip(refs[:terms], refs[terms : 2 * terms]):
             total = total + lax.dot_general(
                 left[...], right[...], (((0,), (0,)), ((), ())), preferred_element_type=jnp.float32
             )
         total = total.astype(jnp.bfloat16)
-        out = operands[-1]
-        if table is None:
-            out[...] = total
+        if runs is None:
+            refs[-1][...] = total
         else:
-            for at in range(len(table)):
-                start = pl.multiple_of(refs[1][at] * HEAD_DIM, HEAD_DIM)
-                out[pl.ds(start, HEAD_DIM), :] = total[at * HEAD_DIM : (at + 1) * HEAD_DIM]
+            for at in range(len(runs)):
+                start = pl.multiple_of(table_ref[blocks + at] * HEAD_DIM, HEAD_DIM)
+                refs[-1][pl.ds(start, HEAD_DIM), :] = total[at * HEAD_DIM : (at + 1) * HEAD_DIM]
 
     return pl.pallas_call(
         kernel,
         grid_spec=pltpu.PrefetchScalarGridSpec(
-            num_scalar_prefetch=len(scalars),
-            grid=(columns // tile,),
-            in_specs=[pl.BlockSpec((count, rows), lambda i, ref, *_: (0, ref[0]))] * terms
-            + [pl.BlockSpec((count, tile), lambda i, *_: (0, i))] * terms,
-            out_specs=pl.BlockSpec((rows, tile), lambda i, *_: (0, i)),
-        ),
-        out_shape=jax.ShapeDtypeStruct((rows, columns), jnp.bfloat16),
+            num_scalar_prefetch=1,
+            grid=(blocks, columns // tile),
+            in_specs=[pl.BlockSpec((count, rows), lambda i, j, ref: (0, ref[i]))] * terms
+            + [pl.BlockSpec((count, tile), lambda i, j, ref: (0, j))] * terms,
+            out_specs=pl.BlockSpec((rows, tile), lambda i, j, ref: (i, j)),
+        ),
+        out_shape=jax.ShapeDtypeStruct((blocks * rows, columns), jnp.bfloat16),
         compiler_params=pltpu.CompilerParams(vmem_limit_bytes=48 << 20),
-        cost_estimate=pl.CostEstimate(
-            flops=2 * terms * count * rows * columns,
-            bytes_accessed=2 * (terms * count * (rows + columns) + rows * columns),
-            transcendentals=0,
-        ),
+        cost_estimate=BRIEF,
         name="outer_rows_of",
-    )(*scalars, *lefts, *rights)
+    )(table, *lefts, *rights)
 
 
 def outer_sides(indices, left, right, rows):
@@ -239,38 +229,193 @@
         ),
         out_shape=[jax.ShapeDtypeStruct((rows, 2 * columns), jnp.bfloat16)] * pieces,
         compiler_params=pltpu.CompilerParams(vmem_limit_bytes=48 << 20),
-        cost_estimate=pl.CostEstimate(
-            flops=4 * pieces * count * rows * columns,
-            bytes_accessed=4 * count * (pieces * rows + columns),
-            transcendentals=0,
-        ),
+        cost_estimate=BRIEF,
         name="outer_sides",
     )(table, left, right)
 
 
-def exchange(values):
-    half = values.shape[0] // 2
-    beside = swap(values, ALONG_X)
-    across = swap(values, ALONG_Y)
-    upper = swap(beside[:half], ALONG_Y)
-    lower = swap(across[half:], ALONG_X)
-    return [values, beside, across, upper, lower]
-
-
-def total_plane(pieces, wait):
-    own, beside, across, corner = pieces
-    half = own.shape[0] // 2
-    upper = swap(corner[:half], ALONG_Y)
-    lower = swap(corner[half:], ALONG_X)
-    beside = lax.dynamic_update_slice(beside, add_low(beside[:half], upper), (0, 0))
-    across = lax.dynamic_update_slice(across, add_low(across[half:], lower), (half, 0))
-    got_x = swap(beside, ALONG_X)
-    got_y = swap(across, ALONG_Y)
-    if wait is not None:
-        own = after(own, wait)
-    return (
-        own.astype(jnp.float32) + got_x.astype(jnp.float32) + got_y.astype(jnp.float32)
-    ).astype(jnp.bfloat16)
+def regroup(bits, matrix, seq_size):
+    rows, columns = matrix.shape
+    block = 256
+
+    def kernel(bits_ref, matrix, out):
+        for flips in range(8):
+            y_flip, x_flip, core_flip = flips // 4, flips // 2 % 2, flips % 2
+
+            @pl.when(4 * bits_ref[0] + 2 * bits_ref[1] + bits_ref[2] == flips)
+            def _():
+                runs = [
+                    (((y ^ y_flip) * 2 + (x ^ x_flip)) * 2 + (side ^ core_flip)) * seq_size + z
+                    for z in range(seq_size)
+                    for y in range(2)
+                    for x in range(2)
+                    for side in range(2)
+                ]
+                out[...] = jnp.concatenate(
+                    [matrix[:, run * HEAD_DIM : (run + 1) * HEAD_DIM] for run in runs], axis=1
+                )
+
+    return pl.pallas_call(
+        kernel,
+        grid_spec=pltpu.PrefetchScalarGridSpec(
+            num_scalar_prefetch=1,
+            grid=(rows // block,),
+            in_specs=[pl.BlockSpec((block, columns), lambda i, bits_ref: (i, 0))],
+            out_specs=pl.BlockSpec((block, columns), lambda i, bits_ref: (i, 0)),
+        ),
+        out_shape=jax.ShapeDtypeStruct((rows, columns), matrix.dtype),
+        compiler_params=pltpu.CompilerParams(vmem_limit_bytes=48 << 20),
+        cost_estimate=BRIEF,
+        name="regroup",
+    )(bits, matrix)
+
+
+def regroup_back(bits, mine, got, seq_size, dtype):
+    rows, columns = mine.shape
+    block = 128
+
+    def kernel(bits_ref, mine, got, out):
+        for flips in range(8):
+            y_flip, x_flip, core_flip = flips // 4, flips // 2 % 2, flips % 2
+
+            @pl.when(4 * bits_ref[0] + 2 * bits_ref[1] + bits_ref[2] == flips)
+            def _():
+                runs = [
+                    ((z * 2 + (y ^ y_flip)) * 2 + (x ^ x_flip)) * 2 + (side ^ core_flip)
+                    for y in range(2)
+                    for x in range(2)
+                    for side in range(2)
+                    for z in range(seq_size)
+                ]
+                own = [mine[:, run * HEAD_DIM : (run + 1) * HEAD_DIM] for run in runs]
+                runs = [run ^ 1 for run in runs]
+                other = [got[:, run * HEAD_DIM : (run + 1) * HEAD_DIM] for run in runs]
+                out[...] = (
+                    jnp.concatenate(own, axis=1)
+                    + jnp.concatenate(other, axis=1).astype(jnp.float32)
+                ).astype(dtype)
+
+    spec = pl.BlockSpec((block, columns), lambda i, bits_ref: (i, 0))
+    return pl.pallas_call(
+        kernel,
+        grid_spec=pltpu.PrefetchScalarGridSpec(
+            num_scalar_prefetch=1,
+            grid=(rows // block,),
+            in_specs=[spec, spec],
+            out_specs=spec,
+        ),
+        out_shape=jax.ShapeDtypeStruct((rows, columns), dtype),
+        compiler_params=pltpu.CompilerParams(vmem_limit_bytes=48 << 20),
+        cost_estimate=BRIEF,
+        name="regroup_back",
+    )(bits, mine, got)
+
+
+def half_dot(which, left, right, by_columns, dtype, tile=512, places=None):
+    lefts = left if places is not None else (left,)
+    rows, depth = lefts[0].shape
+    columns = right.shape[0] if by_columns else right.shape[1]
+    contract = 1 if by_columns else 0
+    count = len(lefts)
+    table = jnp.stack([which, *(places or [])])
+
+    def kernel(table_ref, *refs):
+        total = 0.0
+        for index in range(count):
+            total = total + lax.dot_general(
+                refs[index][...],
+                refs[count + index][...],
+                (((1,), (contract,)), ((), ())),
+                preferred_element_type=jnp.float32,
+            )
+        refs[-1][...] = total.astype(dtype)
+
+    def right_block(index):
+        if by_columns:
+            return pl.BlockSpec((tile, depth), lambda i, table_ref: (i, 0))
+        if places is None:
+            return pl.BlockSpec((depth, tile), lambda i, table_ref: (0, i))
+        return pl.BlockSpec((depth, tile), lambda i, table_ref: (table_ref[1 + index], i))
+
+    return pl.pallas_call(
+        kernel,
+        grid_spec=pltpu.PrefetchScalarGridSpec(
+            num_scalar_prefetch=1,
+            grid=(columns // tile,),
+            in_specs=[
+                pl.BlockSpec((rows // 2, depth), lambda i, table_ref: (table_ref[0], 0))
+            ]
+            * count
+            + [right_block(index) for index in range(count)],
+            out_specs=pl.BlockSpec((rows // 2, tile), lambda i, table_ref: (0, i)),
+        ),
+        out_shape=jax.ShapeDtypeStruct((rows // 2, columns), dtype),
+        compiler_params=pltpu.CompilerParams(vmem_limit_bytes=48 << 20),
+        cost_estimate=BRIEF,
+        name="half_dot",
+    )(table, *lefts, *[right] * count)
+
+
+def multiply(lefts, rights, by_columns, tile=512, bias=None, slope=None, lift=False):
+    rows = lefts[0].shape[0]
+    terms = len(lefts)
+    columns = rights[0].shape[0] if by_columns else rights[0].shape[1]
+    contract = 1 if by_columns else 0
+    extra = [] if bias is None else [bias]
+    extra += [] if slope is None else [slope]
+    across = pl.BlockSpec((rows, tile), lambda i: (0, i))
+    row = pl.BlockSpec((1, tile), lambda i: (0, i))
+    wide = jax.ShapeDtypeStruct((rows, columns), jnp.bfloat16)
+    outs = [(across, wide)]
+    if lift:
+        outs.append((across, wide))
+    if slope is not None:
+        outs.append((row, jax.ShapeDtypeStruct((1, columns), jnp.float32)))
+
+    def kernel(*refs):
+        total = 0.0
+        for left, right in zip(refs[:terms], refs[terms : 2 * terms]):
+            total = total + lax.dot_general(
+                left[...],
+                right[...],
+                (((1,), (contract,)), ((), ())),
+                preferred_element_type=jnp.float32,
+            )
+        rest = refs[2 * terms :]
+        if bias is not None:
+            total = total + rest[0][...]
+        out = rest[len(extra)]
+        if lift:
+            lifted = 0.5 * (1.0 + lax.erf(total * (0.5**0.5)))
+            bell = jnp.exp(-0.5 * total * total) * ((0.5 / math.pi) ** 0.5)
+            out[...] = (total * lifted).astype(jnp.bfloat16)
+            rest[len(extra) + 1][...] = (lifted + total * bell).astype(jnp.bfloat16)
+        elif slope is not None:
+            low = (total * rest[len(extra) - 1][...].astype(jnp.float32)).astype(jnp.bfloat16)
+            out[...] = low
+            rest[len(extra) + 1][...] = jnp.sum(low.astype(jnp.float32), axis=0, keepdims=True)
+        else:
+            out[...] = total.astype(jnp.bfloat16)
+
+    def right_spec(right):
+        if by_columns:
+            return pl.BlockSpec((tile, right.shape[1]), lambda i: (i, 0))
+        return pl.BlockSpec((right.shape[0], tile), lambda i: (0, i))
+
+    result = pl.pallas_call(
+        kernel,
+        grid=(columns // tile,),
+        in_specs=[pl.BlockSpec(left.shape, lambda i: (0, 0)) for left in lefts]
+        + [right_spec(right) for right in rights]
+        + ([] if bias is None else [row])
+        + ([] if slope is None else [across]),
+        out_specs=[spec for spec, _ in outs],
+        out_shape=[shape for _, shape in outs],
+        compiler_params=pltpu.CompilerParams(vmem_limit_bytes=48 << 20),
+        cost_estimate=BRIEF,
+        name="multiply",
+    )(*lefts, *rights, *extra)
+    return result if len(outs) > 1 else result[0]
 
 
 def add_low(left, right):
@@ -397,34 +542,40 @@
         out_specs=pl.BlockSpec((count, 2 * HEAD_DIM), lambda i: (0, i)),
         out_shape=jax.ShapeDtypeStruct((count, pairs * 2 * HEAD_DIM), jnp.bfloat16),
         compiler_params=pltpu.CompilerParams(vmem_limit_bytes=48 << 20),
-        cost_estimate=pl.CostEstimate(
-            flops=16 * work, bytes_accessed=8 * count * columns, transcendentals=0
-        ),
+        cost_estimate=BRIEF,
         name="attend",
     )(rows, mask)
 
 
-def attend_back(rows, grad, mask):
+def attend_back(rows, grad, mask, place):
     count, columns = rows.shape
-    pairs = columns // (6 * HEAD_DIM)
-    work = pairs * 2 * count * count * HEAD_DIM
+    pairs = columns // (6 * HEAD_DIM) // 4
+
+    def kernel(place_ref, *refs):
+        attend_back_kernel(*refs)
+
     return pl.pallas_call(
-        attend_back_kernel,
-        grid=(pairs,),
-        in_specs=[
-            pl.BlockSpec((count, 6 * HEAD_DIM), lambda i: (0, i)),
-            pl.BlockSpec((count, 2 * HEAD_DIM), lambda i: (0, i)),
-            pl.BlockSpec((count, HEAD_DIM), lambda i: (0, 0)),
-        ],
-        out_specs=pl.BlockSpec((count, 6 * HEAD_DIM), lambda i: (0, i)),
-        out_shape=jax.ShapeDtypeStruct((count, columns), jnp.bfloat16),
-        scratch_shapes=[pltpu.VMEM((count, HEAD_DIM), jnp.float32)] * 2,
+        kernel,
+        grid_spec=pltpu.PrefetchScalarGridSpec(
+            num_scalar_prefetch=1,
+            grid=(pairs,),
+            in_specs=[
+                pl.BlockSpec(
+                    (count, 6 * HEAD_DIM), lambda i, place_ref: (0, pairs * place_ref[0] + i)
+                ),
+                pl.BlockSpec(
+                    (count, 2 * HEAD_DIM), lambda i, place_ref: (0, pairs * place_ref[0] + i)
+                ),
+                pl.BlockSpec((count, HEAD_DIM), lambda i, place_ref: (0, 0)),
+            ],
+            out_specs=pl.BlockSpec((count, 6 * HEAD_DIM), lambda i, place_ref: (0, i)),
+            scratch_shapes=[pltpu.VMEM((count, HEAD_DIM), jnp.float32)] * 2,
+        ),
+        out_shape=jax.ShapeDtypeStruct((count, columns // 4), jnp.bfloat16),
         compiler_params=pltpu.CompilerParams(vmem_limit_bytes=48 << 20),
-        cost_estimate=pl.CostEstimate(
-            flops=40 * work, bytes_accessed=8 * count * columns, transcendentals=0
-        ),
+        cost_estimate=BRIEF,
         name="attend_back",
-    )(rows, grad, mask)
+    )(place.reshape(1), rows, grad, mask)
 
 
 ROWS = 128
@@ -449,9 +600,11 @@
 
 
 def middle_kernel(
-    start_ref, tokens, own, got, active, bias, gain, shift, middle_out, rows_out
+    start_ref, tokens, own, upper, lower, active, bias, gain, shift, middle_out, rows_out
 ):
-    branch = own[...].astype(jnp.float32) + got[...].astype(jnp.float32) + bias[...]
+    in_upper = pl.program_id(0) < pl.num_programs(0) // 2
+    got = jnp.where(in_upper, upper[...], lower[...])
+    branch = own[...].astype(jnp.float32) + got.astype(jnp.float32) + bias[...]
     middle = tokens[...].astype(jnp.float32) + active[...] * branch
     middle_out[...] = middle
     normed, _ = normal_parts(middle)
@@ -468,9 +621,22 @@
 
 
 def middle_back_kernel(
-    start_ref, cotangent, middle, own, got, peer, active, gain, grad_out, branch_out, totals
+    start_ref,
+    cotangent,
+    middle,
+    own,
+    upper,
+    lower,
+    peer,
+    active,
+    gain,
+    grad_out,
+    branch_out,
+    totals,
 ):
-    grad_second = own[...] + got[...].astype(jnp.float32) + peer[...].astype(jnp.float32)
+    in_upper = pl.program_id(0) < pl.num_programs(0) // 2
+    got = jnp.where(in_upper, upper[...], lower[...])
+    grad_second = own[...] + got.astype(jnp.float32) + peer[...].astype(jnp.float32)
     normed, scale = normal_parts(middle[...])
     grad_middle = cotangent[...].astype(jnp.float32) + normal_back(
         normed, scale, grad_second * gain[...]
@@ -498,6 +664,12 @@
         "from": pl.BlockSpec((ROWS, width), lambda i, start_ref: (start_ref[0] + i, 0)),
         "vector": pl.BlockSpec((1, width), lambda i, start_ref: (0, 0)),
         "totals": pl.BlockSpec((8, width), lambda i, start_ref: (0, 0)),
+        "upper": pl.BlockSpec(
+            (ROWS, width), lambda i, start_ref: (jnp.minimum(i, count // ROWS // 2 - 1), 0)
+        ),
+        "lower": pl.BlockSpec(
+            (ROWS, width), lambda i, start_ref: (jnp.maximum(i - count // ROWS // 2, 0), 0)
+        ),
         "flag": pl.BlockSpec((ROWS, 1), lambda i, start_ref: (i, 0)),
         "flag from": pl.BlockSpec((ROWS, 1), lambda i, start_ref: (start_ref[0] + i, 0)),
     }
@@ -518,15 +690,29 @@
         ),
         out_shape=shapes,
         compiler_params=pltpu.CompilerParams(vmem_limit_bytes=48 << 20),
-        cost_estimate=pl.CostEstimate(
-            flops=20 * count * width, bytes_accessed=moved, transcendentals=0
-        ),
+        cost_estimate=BRIEF,
         name=name,
     )(start, *[array for array, _ in arrays])
 
 
 def after(value, *others):
     return lax.optimization_barrier((value, others))[0]
+
+
+MIDDLE_KINDS = ("rows", "rows", "upper", "lower", "flag", "vector", "vector", "vector")
+BACK_KINDS = ("from", "from", "rows", "upper", "lower", "rows", "flag from", "vector")
+
+
+class Line:
+    def __init__(self):
+        self.last = None
+
+    def __call__(self, function, *arrays):
+        if self.last is not None:
+            arrays = lax.optimization_barrier((arrays, self.last))[0]
+        result = function(*arrays)
+        self.last = jax.tree.leaves(result)[0]
+        return result
 
 
 def whole_sequence_device(
@@ -552,10 +738,12 @@
     seq_count, local_len, width = tokens.shape
     heads_rows = query_weight.shape[0]
     hidden_rows = expand_weight.shape[0]
-    dp_size, seq_size = lax.axis_size("dp"), lax.axis_size("seq")
-    dp, depth = lax.axis_index("dp"), lax.axis_index("seq")
-    core, place = dp % 2, dp // 2
-    along_x, along_y = place % 2, place // 2
+    seq_size = lax.axis_size("seq")
+    dp_size = lax.axis_size(DEVICES) // seq_size
+    depth, core = lax.axis_index("seq"), lax.axis_index("core")
+    along_x, along_y = lax.axis_index("x"), lax.axis_index("y")
+    place = 2 * along_y + along_x
+    dp = 2 * place + core
     parity = depth % 2
     full_len = local_len * seq_size
     half_len = full_len // 2
@@ -569,25 +757,31 @@
                 pairs.append((i * seq_size + j, (i // 2 * 2 + j // 2) * seq_size + target))
         return pairs
 
-    def to_chips(values):
-        first = pick(parity, values[0], values[1])
-        second = pick(parity, values[1], values[0])
-        first = lax.ppermute(first, ("dp", "seq"), route(False))
-        second = lax.ppermute(second, ("dp", "seq"), route(True))
-        half = ordered(parity, first[None], second[None], 0)
-        return ordered(core, half, swap(half, CORE), 0)
-
-    def from_chips(half):
-        half = half.reshape(2, local_len, width)
-        first = pick(parity, half[0], half[1])
-        second = pick(parity, half[1], half[0])
-        first = lax.ppermute(first, ("dp", "seq"), [(b, a) for a, b in route(False)])
-        second = lax.ppermute(second, ("dp", "seq"), [(b, a) for a, b in route(True)])
+    def send(first, second, back):
+        routes = [[(b, a) if back else (a, b) for a, b in route(flip)] for flip in (False, True)]
+        return lax.ppermute(first, DEVICES, routes[0]), lax.ppermute(second, DEVICES, routes[1])
+
+    def by_parity(values):
+        return pick(parity, values[0], values[1]), pick(parity, values[1], values[0])
+
+    def paired(first, second):
         return ordered(parity, first[None], second[None], 0)
 
-    alive = (exit_layer > LAYER).astype(low)
-    flag_rows = jnp.broadcast_to(alive[:, None, :], (seq_count, 16, local_len))
-    flag_rows = jnp.pad(flag_rows, ((0, 0), (0, 0), (0, width - local_len)))
+    def by_core(own, other):
+        return ordered(core, own, other, 0)
+
+    def half_rows(matrix, which):
+        return lax.dynamic_slice_in_dim(matrix, which * half_len, half_len, 0)
+
+    line = Line()
+    depth_rows = heads_rows * seq_size
+    hidden_block = hidden_rows * seq_size
+    places = [place ^ d for d in range(4)]
+    sides = [core, 1 - core]
+    bits = jnp.stack([along_y, along_x, core])
+
+    def through_z(shard):
+        return lax.all_gather(shard, "seq", axis=0, tiled=True)
 
     devices = dp_size * seq_size
     all_dp = jnp.arange(dp_size, dtype=jnp.int32)[:, None]
@@ -599,25 +793,45 @@
             values, "seq", [(i, (i + steps) % seq_size) for i in range(seq_size)]
         )
 
-    vectors = jnp.concatenate(
-        [
-            first_gain,
-            first_shift,
-            query_bias,
-            value_bias,
-            output_bias,
-            second_gain,
-            second_shift,
-            shrink_bias,
-            expand_bias,
-        ]
-    )[None]
-    for bit in (CORE, ALONG_X, ALONG_Y):
-        vectors = jnp.concatenate([vectors, swap(vectors, bit)], 0)
-    vectors = jnp.stack(
-        [vectors] + [shift_z(vectors, steps) for steps in range(1, seq_size)], 1
-    )
-    vectors = vectors.reshape(devices, -1)[relative].astype(f32)
+    def stacked(own, other):
+        return jnp.concatenate([own, other], 0)
+
+    vectors = [first_gain, first_shift, query_bias, value_bias, output_bias, second_gain]
+    vectors += [second_shift, shrink_bias, expand_bias]
+    shard_a = line(
+        lambda *parts: jnp.concatenate(parts, 0),
+        query_weight,
+        key_weight,
+        value_weight,
+        output_weight,
+    )
+    z_a = through_z(shard_a)
+    vectors = line(lambda *parts: jnp.concatenate(parts)[None, None], *vectors)
+    shifted = [shift_z(vectors, steps) for steps in range(1, seq_size)]
+    alive = (exit_layer > LAYER).astype(low)
+    flag_rows = jnp.broadcast_to(alive[:, None, :], (seq_count, 16, local_len))
+    flag_rows = jnp.pad(flag_rows, ((0, 0), (0, 0), (0, width - local_len)))
+    message = line(
+        lambda *arrays: by_parity(jnp.concatenate(arrays, axis=1)), tokens, flag_rows, cotangent
+    )
+    vectors = line(lambda *parts: jnp.concatenate(parts, 1), vectors, *shifted)
+    mine, theirs = line(lambda rows: split_columns(core, rows, hidden_block), shrink_weight)
+    theirs = swap(theirs, CORE)
+    vectors = line(stacked, vectors, swap(vectors, ALONG_Y))
+    shard_shrink = line(stacked, mine, theirs)
+    mine, theirs = line(lambda rows: split_columns(along_x, rows, hidden_block), shard_shrink)
+    theirs = swap(theirs, ALONG_X)
+    vectors = line(stacked, vectors, swap(vectors, ALONG_X))
+    shard_shrink = line(stacked, mine, theirs)
+    vectors = line(stacked, vectors, swap(vectors, CORE))
+    vectors = line(
+        lambda rows: rows.reshape(2, 2, 2, seq_size, -1)
+        .transpose(2, 1, 0, 3, 4)
+        .reshape(devices, -1)[relative]
+        .astype(f32),
+        vectors,
+    )
+    shrink_across = swap(shard_shrink, ALONG_Y)
 
     def vector(index):
         return vectors[:, index * heads_rows : (index + 1) * heads_rows].reshape(1, -1)
@@ -626,254 +840,286 @@
         cut = matrix.reshape(4, 2, seq_size, -1)
         return lax.dynamic_index_in_dim(cut, core, 1, False).reshape(4 * seq_size, -1)
 
+    def of_quarter(matrix):
+        cut = matrix.reshape(2, 4, seq_size, -1)
+        return lax.dynamic_index_in_dim(cut, 2 * along_x + core, 1, False)
+
     gain_one, shift_one = vector(0), vector(1)
     bias_query = of_core(vectors[:, 2 * heads_rows : 3 * heads_rows])
     bias_value = of_core(vectors[:, 3 * heads_rows : 4 * heads_rows])
-    bias_rows = jnp.stack([bias_query, jnp.zeros_like(bias_query), bias_value], 1).reshape(-1)
+    bias_rows = jnp.stack([bias_query, jnp.zeros_like(bias_query), bias_value], 1).reshape(1, -1)
     bias_out, gain_two, shift_two, bias_shrink = vector(4), vector(5), vector(6), vector(7)
-    def of_quarter(matrix):
-        cut = matrix.reshape(2, 4, seq_size, -1)
-        return lax.dynamic_index_in_dim(cut, 2 * along_x + core, 1, False)
-
-    bias_expand = of_quarter(vectors[:, 8 * heads_rows :]).reshape(-1)
-
-    def through_z(shard):
-        return lax.all_gather(shard, "seq", axis=0, tiled=True)
-
-    places = [place ^ d for d in range(4)]
-    sides = [core, 1 - core]
-    depth_rows = heads_rows * seq_size
-    hidden_block = hidden_rows * seq_size
-
-    z_qkv = through_z(jnp.concatenate([query_weight, key_weight, value_weight], 0))
-
-    mine, theirs = split_columns(core, shrink_weight, hidden_block)
-    shard_shrink = jnp.concatenate([mine, swap(theirs, CORE)], 0)
-    mine, theirs = split_columns(along_x, shard_shrink, hidden_block)
-    shard_shrink = jnp.concatenate([mine, swap(theirs, ALONG_X)], 0)
-
-    z_out = through_z(after(output_weight, z_qkv))
-    z_expand = through_z(after(expand_weight, z_out))
-    z_shrink = through_z(after(shard_shrink, z_expand))
-
-    arrived = to_chips(after(jnp.concatenate([tokens, flag_rows], axis=1), z_qkv))
-    inputs = arrived[:, :local_len].reshape(full_len, width)
-    alive = arrived[:, local_len, :local_len].reshape(full_len, 1)
+    bias_expand = of_quarter(vectors[:, 8 * heads_rows :]).reshape(1, -1)
+
+    half_qkv = 3 * depth_rows // 2
+
+    def cut_a(rows):
+        cut = rows.reshape(seq_size, -1, width)
+        return (
+            cut[:, : 3 * heads_rows].reshape(-1, width),
+            cut[:, 3 * heads_rows :].reshape(-1, width),
+        )
+
+    arrived = send(*(after(part, z_a) for part in message), False)
+    z_qkv, z_out = line(cut_a, z_a)
+    beside_qkv, across_qkv = swap(z_qkv, ALONG_X), swap(z_qkv, ALONG_Y)
+    mine, theirs = line(lambda rows: split_columns(core, rows, depth_rows), z_out)
+    rows_out = line(
+        lambda own, other: jnp.concatenate([own, other], 1), mine, swap(theirs, CORE)
+    )
+    upper = line(lambda rows: rows[:half_qkv], beside_qkv)
+    lower = line(lambda rows: rows[half_qkv:], across_qkv)
+    upper, lower = swap(upper, ALONG_Y), swap(lower, ALONG_X)
+    half = line(paired, *arrived)
+    z_expand = through_z(after(expand_weight, half))
+    joined = line(by_core, half, swap(half, CORE))
+    inputs = joined[:, :local_len].reshape(full_len, width)
+    alive = joined[:, local_len, :local_len].reshape(full_len, 1)
+    cotangent_full = joined[:, local_len + 16 :].reshape(full_len, width)
     active = alive.astype(f32)
     mask = jnp.broadcast_to((alive - 1) * jnp.bfloat16(1e30), (full_len, HEAD_DIM))
 
-    pieces_qkv = exchange(after(z_qkv, vectors, shard_shrink))
-    mine, theirs = split_columns(core, z_out, depth_rows)
-    rows_out = jnp.concatenate([mine, swap(theirs, CORE)], 1)
-    pieces_out = exchange(after(rows_out, pieces_qkv))
-    across_expand = swap(after(z_expand, pieces_out), ALONG_Y)
-    across_shrink = swap(after(z_shrink, across_expand), ALONG_Y)
-    cotangent_full = to_chips(after(cotangent, z_expand)).reshape(full_len, width)
-
-    half_qkv = 3 * depth_rows // 2
-    w_qkv = arrange(
-        pieces_qkv,
-        (half_qkv, width),
-        [(p, r, 0) for p in range(3) for r in range(2)] + [(3, 0, 0), (4, 0, 0)],
-        [2 * places[d] + r for d in range(4) for r in range(2)],
-    )
-    half_out = depth_rows // 2
-    w_out = arrange(
-        pieces_out,
-        (half_out, width // 2),
-        [(p, r, i) for p in range(3) for r in range(2) for i in range(2)]
-        + [(p, 0, i) for p in (3, 4) for i in range(2)],
-        [2 * (2 * places[d] + sides[i]) + r for d in range(4) for r in range(2) for i in range(2)],
-    )
-    w_expand = arrange(
-        [z_expand, across_expand],
-        (hidden_block // 2, width),
-        [(p, r, 0) for p in range(2) for r in range(2)],
-        [2 * (along_y ^ p) + r for p in range(2) for r in range(2)],
-    )
-    w_shrink = arrange(
-        [z_shrink, across_shrink],
-        (heads_rows, 2 * hidden_block),
-        [(p, (4 * j + 2 * s + t), 0) for p in range(2) for j in range(seq_size) for s in range(2) for t in range(2)],
-        [
-            ((2 * (along_y ^ p) + (along_x ^ s)) * 2 + (core ^ t)) * seq_size + j
-            for p in range(2)
-            for j in range(seq_size)
-            for s in range(2)
-            for t in range(2)
-        ],
-    )
-
     no_start = jnp.zeros((1,), jnp.int32)
     half_start = (core * (half_len // ROWS)).reshape(1)
 
-    def half_rows(matrix, which):
-        return lax.dynamic_slice_in_dim(matrix, which * half_len, half_len, 0)
-
-    def own_half(left, weight, dot):
-        got = swap(dot(half_rows(left, 1 - core), weight).astype(low), CORE)
-        return dot(half_rows(left, core), weight), got
-
-    def of_peer(matrix):
-        got = swap(half_rows(matrix, core), ALONG_X)
-        return ordered(core, got, swap(got, CORE), 0)
-
-    (first_rows,) = by_rows(
-        first_kernel,
-        no_start,
-        full_len,
-        [(inputs, "rows"), (gain_one, "vector"), (shift_one, "vector")],
-        [("rows", low)],
-        "first_norm",
-    )
-    qkv = (project(first_rows, w_qkv) + bias_rows).astype(low)
-    mixed = attend(qkv, mask)
-    branch = project(mixed, w_out).astype(low)
-    middle, second_rows = by_rows(
-        middle_kernel,
-        no_start,
-        full_len,
-        [
-            (inputs, "rows"),
-            (branch, "rows"),
-            (swap(branch, CORE), "rows"),
-            (active, "flag"),
-            (bias_out, "vector"),
-            (gain_two, "vector"),
-            (shift_two, "vector"),
-        ],
-        [("rows", f32), ("rows", low)],
-        "middle_norm",
-    )
-    second_peer = of_peer(second_rows)
-    grad_shrunk = (active * cotangent_full.astype(f32)).astype(low)
-    grad_shrunk_peer = of_peer(grad_shrunk)
-
-    def lift(rows):
-        hidden_pre = project(rows, w_expand) + bias_expand
-        lifted = 0.5 * (1.0 + lax.erf(hidden_pre * (0.5**0.5)))
-        bell = jnp.exp(-0.5 * hidden_pre * hidden_pre) * ((0.5 / math.pi) ** 0.5)
-        return (hidden_pre * lifted).astype(low), (lifted + hidden_pre * bell).astype(low)
-
-    activated, slope = lift(second_rows)
-    activated_peer, slope_peer = lift(second_peer)
-
+    grad_shrunk = line(
+        lambda flags, grads: (flags * grads.astype(f32)).astype(low), active, cotangent_full
+    )
+    sent_gs = line(lambda rows: half_rows(rows, core), grad_shrunk)
+    gs_got = swap(sent_gs, ALONG_X)
+    (first_rows,) = line(
+        lambda *arrays: by_rows(
+            first_kernel,
+            no_start,
+            full_len,
+            list(zip(arrays, ("rows", "vector", "vector"))),
+            [("rows", low)],
+            "first_norm",
+        ),
+        inputs,
+        gain_one,
+        shift_one,
+    )
+    w_qkv = line(
+        lambda *pieces: arrange(
+            pieces,
+            (half_qkv, width),
+            [(p, r, 0) for p in range(3) for r in range(2)] + [(3, 0, 0), (4, 0, 0)],
+            [2 * places[d] + r for d in range(4) for r in range(2)],
+        ),
+        z_qkv,
+        beside_qkv,
+        across_qkv,
+        upper,
+        lower,
+    )
+    rows_out = after(rows_out, w_qkv)
+    out_beside, out_across = swap(rows_out, ALONG_X), swap(rows_out, ALONG_Y)
+    across_expand = swap(z_expand, ALONG_Y)
+
+    qkv = line(
+        lambda rows, weight: multiply((rows,), (weight,), True, bias=bias_rows), first_rows, w_qkv
+    )
+    out_corner = swap(line(lambda rows: rows * jnp.bfloat16(1), out_across), ALONG_X)
+    mixed = line(attend, qkv, mask)
+    w_out = line(
+        lambda *pieces: arrange(
+            pieces,
+            (depth_rows, width // 2),
+            [(p, 0, i) for p in range(4) for i in range(2)],
+            [2 * places[d] + sides[i] for d in range(4) for i in range(2)],
+        ),
+        after(rows_out, z_expand),
+        out_beside,
+        out_across,
+        out_corner,
+    )
+    branch = line(lambda rows, weight: multiply((rows,), (weight,), True), mixed, w_out)
+    branch_got = [swap(part, CORE) for part in jnp.split(branch, 2)]
+    shard_shrink = line(stacked, shard_shrink, shrink_across)
+    w_shrink = through_z(after(shard_shrink, z_expand, branch))
+    middle, second_rows = line(
+        lambda *arrays: by_rows(
+            middle_kernel,
+            no_start,
+            full_len,
+            list(zip(arrays, MIDDLE_KINDS)),
+            [("rows", f32), ("rows", low)],
+            "middle_norm",
+        ),
+        inputs,
+        branch,
+        *branch_got,
+        active,
+        bias_out,
+        gain_two,
+        shift_two,
+    )
+    second_half = line(lambda rows: half_rows(rows, core), second_rows)
+    second_got = swap(second_half, ALONG_X)
+    gs_own = line(lambda rows: regroup(bits, rows, seq_size), grad_shrunk)
+    w_expand = line(
+        lambda *pieces: arrange(
+            pieces,
+            (hidden_block // 2, width),
+            [(p, r, 0) for p in range(2) for r in range(2)],
+            [2 * (along_y ^ p) + r for p in range(2) for r in range(2)],
+        ),
+        z_expand,
+        across_expand,
+    )
+
+    def lift(rows, weight):
+        return multiply((rows,), (weight,), True, bias=bias_expand, lift=True)
+
+    activated, slope = line(lift, second_rows, w_expand)
+    second_peer = line(by_core, second_got, swap(second_got, CORE))
+    activated_peer, slope_peer = line(lift, second_peer, w_expand)
+
+    gs_peer = line(by_core, gs_got, swap(gs_got, CORE))
+    gs_peer = line(lambda rows: regroup(bits, rows, seq_size), gs_peer)
     def scatter_z(total):
         return lax.psum_scatter(total, "seq", scatter_dimension=0, tiled=True)
 
-    z_first = [
-        (j * 2 + (along_x ^ s)) * 2 + (core ^ t)
-        for s in range(2)
-        for t in range(2)
-        for j in range(seq_size)
-    ]
-    shrink_parts = [
-        outer_rows_of(
-            along_y ^ d,
-            (grad_shrunk, grad_shrunk_peer),
-            (activated, activated_peer),
-            4 * depth_rows,
-            table=z_first,
-        )
-        for d in (1, 0)
-    ]
-    shrink_got = swap(after(shrink_parts[0], across_shrink), ALONG_Y)
-
-    grad_units_peer = through(after(grad_shrunk_peer, shrink_parts[0]), w_shrink)
-    grad_pre_peer = (grad_units_peer * slope_peer.astype(f32)).astype(low)
-    grad_units = through(after(grad_shrunk, grad_pre_peer), w_shrink)
-    grad_pre = (grad_units * slope.astype(f32)).astype(low)
-
-    peer_half, peer_got = own_half(grad_pre_peer, w_expand, through)
-    peer_half = (peer_half + peer_got.astype(f32)).astype(low)
+    def units(grads, weight, slopes):
+        return multiply((grads,), (weight,), False, slope=slopes)
+
+    def their_half(left, weight, by_columns=False):
+        return half_dot(1 - core, left, weight, by_columns, low)
+
+    def my_half(left, weight, by_columns=False):
+        return half_dot(core, left, weight, by_columns, f32)
+
+    def add_rounded(left, right):
+        return (left.astype(f32) + right.astype(f32)).astype(low)
+
+    shrink_part = line(
+        lambda own, peer, rows, rows_peer: outer_rows_of(
+            (own, peer), (rows, rows_peer), width // 2, range(2)
+        ),
+        gs_own,
+        gs_peer,
+        activated,
+        activated_peer,
+    )
+    shrink_rows = scatter_z(shrink_part)
+    grad_pre_peer, peer_sums = line(units, gs_peer, w_shrink, slope_peer)
+    theirs = line(their_half, grad_pre_peer, w_expand)
+    mine = line(my_half, grad_pre_peer, w_expand)
+    peer_half = line(add_rounded, mine, swap(theirs, CORE))
     second_from_peer = swap(peer_half, ALONG_X)
-    second_half, second_got = own_half(after(grad_pre, peer_half), w_expand, through)
-    expand_parts = [
-        outer_rows_of(
-            along_y ^ d,
-            (after(grad_pre, second_half), grad_pre_peer),
-            (second_rows, second_peer),
-            hidden_block,
-        )
-        for d in (1, 0)
-    ]
-    shrink_sum = add_low(shrink_parts[1], after(shrink_got, expand_parts[0]))
-    expand_got = swap(after(expand_parts[0], shrink_got), ALONG_Y)
-
-    grad_middle, grad_branch_half, middle_totals = by_rows(
-        middle_back_kernel,
-        half_start,
-        half_len,
-        [
-            (cotangent_full, "from"),
-            (middle, "from"),
-            (after(second_half, expand_parts[1]), "rows"),
-            (second_got, "rows"),
-            (second_from_peer, "rows"),
-            (active, "flag from"),
-            (gain_two, "vector"),
-        ],
-        [("rows", f32), ("rows", low), ("totals", f32)],
-        "middle_norm_back",
-    )
-    grad_branch = ordered(core, grad_branch_half, swap(grad_branch_half, CORE), 0)
-
-    grad_mixed = through(grad_branch, w_out).astype(low)
-    out_parts = list(outer_sides(
-        [2 * places[d] + sides[i] for d in range(4) for i in range(2)],
-        after(grad_branch, grad_mixed),
+    grad_pre, own_sums = line(units, gs_own, w_shrink, slope)
+    theirs = line(their_half, grad_pre, w_expand)
+    second_got = [swap(part, CORE) for part in jnp.split(theirs, 2)]
+    second_mine = line(my_half, grad_pre, w_expand)
+    def expand_part(d):
+        return line(
+            lambda *arrays: outer_rows_of(arrays[:2], arrays[2:], hidden_block, [along_y ^ d]),
+            grad_pre,
+            grad_pre_peer,
+            second_rows,
+            second_peer,
+        )
+
+    expand_across = expand_part(1)
+    expand_got = swap(expand_across, ALONG_Y)
+
+    grad_middle, grad_branch_half, middle_totals = line(
+        lambda *arrays: by_rows(
+            middle_back_kernel,
+            half_start,
+            half_len,
+            list(zip(arrays, BACK_KINDS)),
+            [("rows", f32), ("rows", low), ("totals", f32)],
+            "middle_norm_back",
+        ),
+        cotangent_full,
+        middle,
+        second_mine,
+        *second_got,
+        second_from_peer,
+        active,
+        gain_two,
+    )
+    branch_got = swap(grad_branch_half, CORE)
+
+    grad_branch = line(by_core, grad_branch_half, branch_got)
+    grad_mixed = line(
+        lambda grads, weight: multiply((grads,), (weight,), False, tile=256), grad_branch, w_out
+    )
+    out_part = line(
+        lambda grads, rows: outer_sides(
+            [2 * places[d] + sides[i] for d in range(4) for i in range(2)], grads, rows, depth_rows
+        ),
+        grad_branch,
         mixed,
-        depth_rows,
-    ))
-    out_parts[3] = after(out_parts[3], shrink_got)
-    grad_qkv = attend_back(qkv, after(grad_mixed, out_parts[0]), mask)
-    out_sum = total_plane(out_parts, grad_qkv)
-    expand_sum = add_low(expand_parts[1], after(expand_got, grad_qkv))
-
-    qkv_parts = {}
-    left = grad_qkv
-    for d in (3, 1, 2, 0):
-        qkv_parts[d] = outer_rows_of(places[d], (left,), (first_rows,), 3 * depth_rows)
-        left = after(left, qkv_parts[d])
-    qkv_sum = total_plane([qkv_parts[d] for d in range(4)], None)
-    grad_first, grad_first_got = own_half(left, w_qkv, through)
-    grad_half, first_totals = by_rows(
-        first_back_kernel,
-        half_start,
-        half_len,
-        [
-            (inputs, "from"),
-            (grad_middle, "rows"),
-            (grad_first, "rows"),
-            (grad_first_got, "rows"),
-            (gain_one, "vector"),
-        ],
-        [("rows", low), ("totals", f32)],
-        "first_norm_back",
-    )
-    tokens_grad = from_chips(grad_half)
-
-    shrunk_peer, shrunk_peer_got = own_half(after(activated_peer, grad_half), w_shrink, project)
-    shrunk_from_peer = swap((shrunk_peer + shrunk_peer_got.astype(f32)).astype(low), ALONG_X)
-    shrunk, shrunk_got = own_half(after(activated, shrunk_peer), w_shrink, project)
-    shrunk = shrunk + shrunk_got.astype(f32) + shrunk_from_peer.astype(f32) + bias_shrink
-    out_half_rows = (half_rows(middle, core) + half_rows(active, core) * shrunk).astype(low)
-    layer_out = from_chips(out_half_rows)
-
-    shrink_rows = scatter_z(shrink_sum)
-    half = shrink_rows.shape[0] // 2
-    shrink_rows = weave_columns(
-        along_x, shrink_rows[:half], swap(shrink_rows[half:], ALONG_X), hidden_block
-    )
-    shrink_weight_grad = weave_columns(
-        core, shrink_rows[:heads_rows], swap(shrink_rows[heads_rows:], CORE), hidden_block
-    ).astype(f32)
-    expand_weight_grad = scatter_z(expand_sum).astype(f32)
-    out_rows = weave_columns(
-        core, out_sum[:, : width // 2], swap(out_sum[:, width // 2 :], CORE), depth_rows
-    )
-    output_weight_grad = scatter_z(out_rows).astype(f32)
-    qkv_weight_grad = scatter_z(qkv_sum).astype(f32)
+    )
+    out_parts = [out_part[d] for d in range(4)]
+    out_corner = swap(out_parts[3], ALONG_X)
+    out_got_x = swap(out_parts[1], ALONG_X)
+
+    def attend_piece(d):
+        return line(
+            lambda rows, grads, flags: attend_back(rows, grads, flags, places[d]),
+            qkv,
+            grad_mixed,
+            mask,
+        )
+
+    def qkv_part(d, rows, source):
+        return line(
+            lambda grads, inputs_low: outer_rows_of((grads,), (inputs_low,), rows, [source]),
+            grad_qkv[d],
+            first_rows,
+        )
+
+    grad_qkv = {3: attend_piece(3)}
+    corner_got = swap(qkv_part(3, 2 * half_qkv, 0), ALONG_X)
+    grad_qkv[1] = attend_piece(1)
+    qkv_x = swap(qkv_part(1, 2 * half_qkv, 0), ALONG_X)
+    grad_qkv[2] = attend_piece(2)
+    across = qkv_part(2, 2 * half_qkv, 0)
+    expand_here = expand_part(0)
+    qkv_y = swap(line(add_rounded, across, corner_got), ALONG_Y)
+    expand_sum = line(add_rounded, expand_here, expand_got)
+    expand_rows = scatter_z(expand_sum)
+    grad_qkv[0] = attend_piece(0)
+    here = qkv_part(0, 2 * half_qkv, 0)
+    grads_qkv = tuple(grad_qkv[d] for d in range(4))
+
+    def first_half(which, dtype):
+        return lambda *arrays: half_dot(which, arrays[:4], arrays[4], False, dtype, places=places)
+
+    peer_theirs = line(
+        lambda rows, weight: their_half(rows, weight, True), activated_peer, w_shrink
+    )
+    peer_got = swap(peer_theirs, CORE)
+    first_theirs = line(first_half(1 - core, low), *grads_qkv, w_qkv)
+    first_got = swap(first_theirs, CORE)
+    peer_mine = line(lambda rows, weight: my_half(rows, weight, True), activated_peer, w_shrink)
+    first_mine = line(first_half(core, f32), *grads_qkv, w_qkv)
+    qkv_sum = line(
+        lambda *parts: sum(part.astype(f32) for part in parts).astype(low), here, qkv_x, qkv_y
+    )
+    qkv_rows = scatter_z(qkv_sum)
+    grad_half, first_totals = line(
+        lambda *arrays: by_rows(
+            first_back_kernel,
+            half_start,
+            half_len,
+            list(zip(arrays, ("from", "rows", "rows", "rows", "vector"))),
+            [("rows", low), ("totals", f32)],
+            "first_norm_back",
+        ),
+        inputs,
+        grad_middle,
+        first_mine,
+        first_got,
+        gain_one,
+    )
+    tokens_parts = send(
+        *line(lambda rows: by_parity(rows.reshape(2, local_len, width)), grad_half), True
+    )
 
     def column_sum(matrix):
         return jnp.sum(matrix.astype(f32), axis=0)
@@ -891,27 +1137,99 @@
         quarters = [jnp.where(2 * along_x + core == q, cut, none) for q in range(4)]
         return jnp.concatenate(quarters, 1).reshape(devices, rows)
 
-    qkv_sums = column_sum(grad_qkv).reshape(4 * seq_size, 3, heads_rows)
-    sums = jnp.concatenate(
-        [
-            all_devices(first_totals[0], heads_rows),
-            all_devices(first_totals[1], heads_rows),
-            core_devices(qkv_sums[:, 0], heads_rows),
-            core_devices(qkv_sums[:, 2], heads_rows),
-            all_devices(middle_totals[2], heads_rows),
-            all_devices(middle_totals[0], heads_rows),
-            all_devices(middle_totals[1], heads_rows),
-            all_devices(0.5 * column_sum(grad_shrunk), heads_rows),
-            quarter_devices(column_sum(grad_pre) + column_sum(grad_pre_peer), hidden_rows),
-        ],
-        axis=1,
-    )
-    to_relative = ((all_dp ^ dp) * seq_size + (all_seq + depth) % seq_size).reshape(-1)
-    sums = sums[to_relative].reshape(dp_size, seq_size, -1)
-    for bit in (ALONG_Y, ALONG_X, CORE):
-        sums = sums[:bit] + swap(sums[bit:], bit)
-    sums = sums[0]
-    sums = sums[0] + sum(shift_z(sums[steps], steps) for steps in range(1, seq_size))
+    def all_sums(first, middle_sums, shrunk_grads, own, peer, *grads):
+        qkv_sums = jnp.stack([column_sum(part) for part in grads])[jnp.stack(places)]
+        qkv_sums = qkv_sums.reshape(4 * seq_size, 3, heads_rows)
+        sums = jnp.concatenate(
+            [
+                all_devices(first[0], heads_rows),
+                all_devices(first[1], heads_rows),
+                core_devices(qkv_sums[:, 0], heads_rows),
+                core_devices(qkv_sums[:, 2], heads_rows),
+                all_devices(middle_sums[2], heads_rows),
+                all_devices(middle_sums[0], heads_rows),
+                all_devices(middle_sums[1], heads_rows),
+                all_devices(0.5 * column_sum(shrunk_grads), heads_rows),
+                quarter_devices(own + peer, hidden_rows),
+            ],
+            axis=1,
+        )
+        return sums.reshape(dp_size, seq_size, -1)[jnp.arange(dp_size) ^ dp]
+
+    def fold(values, got):
+        return values[: got.shape[0]] + got
+
+    sums = line(
+        all_sums, first_totals, middle_totals, grad_shrunk, own_sums, peer_sums, *grads_qkv
+    )
+    out_got_y = swap(line(add_rounded, out_parts[2], out_corner), ALONG_Y)
+    sums = line(fold, sums, swap(sums[dp_size // 2 :], ALONG_Y))
+    sums = line(fold, sums, swap(sums[dp_size // 4 :], ALONG_X))
+    sums = line(fold, sums, swap(sums[dp_size // 8 :], CORE))
+
+    to_peer = line(
+        lambda *parts: regroup_back(bits, *parts, seq_size, low), peer_mine, peer_got
+    )
+    from_peer = swap(to_peer, ALONG_X)
+    out_sum = line(
+        lambda *parts: sum(part.astype(f32) for part in parts).astype(low),
+        out_parts[0],
+        out_got_x,
+        out_got_y,
+    )
+    out_got = swap(line(lambda rows: rows[:, width // 2 :], out_sum), CORE)
+    theirs = line(lambda rows, weight: their_half(rows, weight, True), activated, w_shrink)
+    shrunk_got = swap(theirs, CORE)
+    out_rows = line(
+        lambda rows, got: weave_columns(core, rows[:, : width // 2], got, depth_rows),
+        out_sum,
+        out_got,
+    )
+
+    def with_vectors(totals, rows):
+        totals = totals.reshape(seq_size, 1, -1).astype(low)
+        totals = jnp.pad(totals, ((0, 0), (0, 15), (0, width - totals.shape[2])))
+        rows = jnp.concatenate([rows.reshape(seq_size, -1, width), totals], 1)
+        return rows.reshape(-1, width)
+
+    out_rows = scatter_z(line(with_vectors, sums, out_rows))
+    mine = line(lambda rows, weight: my_half(rows, weight, True), activated, w_shrink)
+    shrunk = line(lambda *parts: regroup_back(bits, *parts, seq_size, f32), mine, shrunk_got)
+
+    def finish(part, peer, rows, flags, bias):
+        total = part + peer.astype(f32) + bias
+        out = half_rows(rows, core) + half_rows(flags, core) * total
+        return by_parity(out.astype(low).reshape(2, local_len, width))
+
+    out_halves = send(*line(finish, shrunk, from_peer, middle, active, bias_shrink), True)
+
+    half = shrink_rows.shape[0] // 2
+    shrink_got = swap(line(lambda rows: rows[half:], shrink_rows), ALONG_Y)
+    expand_weight_grad = line(lambda rows: rows.astype(f32), expand_rows)
+    tokens_grad = line(paired, *tokens_parts)
+    shrink_rows = line(lambda rows, got: add_rounded(rows[:half], got), shrink_rows, shrink_got)
+    half = half // 2
+    shrink_got = swap(line(lambda rows: rows[half:], shrink_rows), ALONG_X)
+    qkv_weight_grad = line(lambda rows: rows.astype(f32), qkv_rows)
+    shrink_rows = line(
+        lambda rows, got: weave_columns(along_x, rows[:half], got, hidden_block),
+        shrink_rows,
+        shrink_got,
+    )
+    shrink_got = swap(line(lambda rows: rows[heads_rows:], shrink_rows), CORE)
+    shrink_weight_grad = line(
+        lambda rows, got: weave_columns(core, rows[:heads_rows], got, hidden_block).astype(f32),
+        shrink_rows,
+        shrink_got,
+    )
+    output_weight_grad, sums = line(
+        lambda rows: (
+            rows[:heads_rows].astype(f32),
+            rows[heads_rows, : 8 * heads_rows + hidden_rows].astype(f32),
+        ),
+        out_rows,
+    )
+    layer_out = line(paired, *out_halves)
 
     def vector_grad(index):
         return sums[index * heads_rows : (index + 1) * heads_rows]
@@ -1233,55 +1551,52 @@
 
 
 def solution(mesh):
+    chips = mesh.shape["dp"] // 2
+    if chips == 4 and mesh.shape["seq"] == 4:
+        names = ("y", "x", "core", "seq")
+        mesh = Mesh(mesh.devices.reshape(2, 2, 2, 4), names)
+        dp, rows, per_device = names[:3], names, whole_sequence_device
+    else:
+        dp, rows, per_device = "dp", ("dp", "seq"), general_device
     in_specs = (
-        P("dp", "seq", None),
-        P("dp", "seq"),
-        P(("dp", "seq")),
-        P(("dp", "seq")),
-        P(("dp", "seq"), None),
-        P(("dp", "seq")),
-        P(("dp", "seq"), None),
-        P(("dp", "seq"), None),
-        P(("dp", "seq")),
-        P(("dp", "seq"), None),
-        P(("dp", "seq")),
-        P(("dp", "seq")),
-        P(("dp", "seq")),
-        P(("dp", "seq"), None),
-        P(("dp", "seq")),
-        P(("dp", "seq"), None),
-        P(("dp", "seq")),
-        P("dp", "seq", None),
+        P(dp, "seq", None),
+        P(dp, "seq"),
+        P(rows),
+        P(rows),
+        P(rows, None),
+        P(rows),
+        P(rows, None),
+        P(rows, None),
+        P(rows),
+        P(rows, None),
+        P(rows),
+        P(rows),
+        P(rows),
+        P(rows, None),
+        P(rows),
+        P(rows, None),
+        P(rows),
+        P(dp, "seq", None),
     )
     out_specs = (
-        P("dp", "seq", None),
-        P("dp", "seq", None),
-        P(("dp", "seq")),
-        P(("dp", "seq")),
-        P(("dp", "seq"), None),
-        P(("dp", "seq")),
-        P(("dp", "seq"), None),
-        P(("dp", "seq"), None),
-        P(("dp", "seq")),
-        P(("dp", "seq"), None),
-        P(("dp", "seq")),
-        P(("dp", "seq")),
-        P(("dp", "seq")),
-        P(("dp", "seq"), None),
-        P(("dp", "seq")),
-        P(("dp", "seq"), None),
-        P(("dp", "seq")),
-    )
-    def per_device(*arrays):
-        tokens, query_weight = arrays[0], arrays[4]
-        fits = (
-            mesh.shape["dp"] == 8
-            and mesh.shape["seq"] == 4
-            and tokens.shape[0] == 2
-            and query_weight.shape[0] == HEAD_DIM
-        )
-        return (whole_sequence_device if fits else general_device)(*arrays)
-
+        P(dp, "seq", None),
+        P(dp, "seq", None),
+        P(rows),
+        P(rows),
+        P(rows, None),
+        P(rows),
+        P(rows, None),
+        P(rows, None),
+        P(rows),
+        P(rows, None),
+        P(rows),
+        P(rows),
+        P(rows),
+        P(rows, None),
+        P(rows),
+        P(rows, None),
+        P(rows),
+    )
     return jax.shard_map(
         per_device, mesh=mesh, in_specs=in_specs, out_specs=out_specs, check_vma=False
     )

time: 1240 us -> 1080 us (0.87)
  Pallas kernels: 265 us -> 452 us
  waiting for transfers between devices: 546 us -> 359 us
  matrix products: 180 us -> 0 us
  local copies, waits for them, and re-layouts: 54.3 us -> 83.5 us
    pallas_call x1 -> x25, Pallas kernels: 50.1 us -> 257 us  [the longest x7 92.2 us: multiply(): pl.pallas_call(kernel, grid=(columns // tile,), in_specs=[pl.BlockSpec(le...]
    dot_general x17 -> x0, matrix products: 180 us -> none  [the longest x9 91.7 us: through(): return jnp.dot(left, weight, preferred_element_type=jnp.float32)]
    ppermute x55 -> x51, waiting for transfers between devices: 474 us -> 318 us  [the longest x45 257 us: swap(): return lax.ppermute(values, axis, [(0, 1), (1, 0)])]
    ppermute x6 -> x3, waiting for transfers between devices: 40.8 us -> 0.01 us  [shift_z(): lax.ppermute(values, 'seq', [(i, (i + steps) % seq_size) for i in range(s...]
    unnamed x97 -> x133, local copies, waits for them, and re-layouts: 21.3 us -> 42 us
    pallas_call x4 -> x3, Pallas kernels: 42.9 us -> 27.7 us  [arrange(): pl.pallas_call(kernel, grid_spec=pltpu.PrefetchScalarGridSpec(num_scalar_...]
    ppermute x55 -> x51, starting transfers between devices: 58.1 us -> 69.4 us  [the longest x45 53.1 us: swap(): return lax.ppermute(values, axis, [(0, 1), (1, 0)])]
    all_gather x4 -> x3, waiting for transfers between devices: 30.9 us -> 40.7 us  [through_z(): return lax.all_gather(shard, 'seq', axis=0, tiled=True)]
  transfers between devices with their start and end apart: 69 -> 61, of which waited for: 25 -> 24; matrix products, arithmetic and copies ran while one was open for 23% -> 11% of each run, Pallas kernels for 20% -> 42%
where the time goes in v3:
time: 1080 us; the launch traced here: 1070 us
  Pallas kernels  452 us (42%)
  waiting for transfers between devices  359 us (33%)
  other arithmetic  88.6 us (8%)
  local copies, waits for them, and re-layouts  83.5 us (8%)
  starting transfers between devices  74.9 us (7%)
  between operations  15.7 us (1%)
    ppermute x45, waiting for transfers between devices, swap(): return lax.ppermute(values, axis, [(0, 1), (1, 0)])  257 us
    pallas_call x7, Pallas kernels, multiply(): pl.pallas_call(kernel, grid=(columns // tile,), in_specs=[pl.BlockSpec(le...  92.2 us
    pallas_call x10, Pallas kernels, half_dot(): pl.pallas_call(kernel, grid_spec=pltpu.PrefetchScalarGridSpec(num_scalar_...  90.2 us
    pallas_call x7, Pallas kernels, outer_rows_of(): pl.pallas_call(kernel, grid_spec=pltpu.PrefetchScalarGridSpec(num_scalar_...  75.3 us
    ppermute x3, waiting for transfers between devices, send(): lax.ppermute(second, DEVICES, routes[1])  60.7 us
    ppermute x45, starting transfers between devices, swap(): return lax.ppermute(values, axis, [(0, 1), (1, 0)])  53.1 us
    pallas_call x4, Pallas kernels, attend_back(): pl.pallas_call(kernel, grid_spec=pltpu.PrefetchScalarGridSpec(num_scalar_...  53 us
    unnamed x133, local copies, waits for them, and re-layouts  42 us
  transfers between devices with their start and end apart: 61, of which 24 were waited for; matrix products, arithmetic and copies ran while one was open for 11% of the time, Pallas kernels for 42%

profile of v3, /device:TPU:9, one launch (start us, length us, event | category | flops | bytes accessed | tf_op | source)
XLA Modules:
  0.0 1073.7 jit_solution(4699257926789486184)
XLA Ops:
  51.2 40.7 %all-gather.4.cloned.1.call-done = bf16[1024,2048]{1,0:T(8,128)(2,1)} async-done(((bf16[256,2048]{1,0:T(8,128)(2,1)}), bf16[1024,2048]{1,0:T(8,128)(2,1)}) %all-gather.4.cloned.1.call-update) | async-done | bytes 4194320 | tf_op jit(solution)/shard_map/all_gather | solution.py:784
  110.2 15.9 %collective-permute-start.12 = (bf16[256,1024]{1,0:T(8,128)(2,1)}, bf16[256,1024]{1,0:T(8,128)(2,1)S(1)}, u32[]{:S(2)}, u32[]{:S(2)}) collective-permute-start(bf16[256,1024]{1,0:T(8,128)(2,1)} %get-tuple-element.307), channel_id=1, source_target_pairs={{0,4},{4,0},{1,5},{5,1},{2,6},{6,2},{3,7},{7,3},{8,12},{12,8},{9,1... | collective-permute-start | bytes 1572872 | tf_op jit(solution)/shard_map/ppermute | solution.py:54
  128.9 36.4 %collective-permute-done.11.refs_1_ = bf16[768,2048]{1,0:T(8,128)(2,1)} collective-permute-done((bf16[768,2048]{1,0:T(8,128)(2,1)}, bf16[768,2048]{1,0:T(8,128)(2,1)}, u32[]{:S(2)}, u32[]{:S(2)}) %collective-permute-start.11) | collective-permute-done | bytes 3145760 | tf_op jit(solution)/shard_map/ppermute | solution.py:54
  170.8 27.0 %collective-permute-done.1 = bf16[528,2048]{1,0:T(8,128)(2,1)} collective-permute-done((bf16[528,2048]{1,0:T(8,128)(2,1)S(1)}, bf16[528,2048]{1,0:T(8,128)(2,1)}, u32[]{:S(2)}, u32[]{:S(2)}) %collective-permute-start.1) | collective-permute-done | bytes 2162720 | tf_op jit(solution)/shard_map/ppermute | solution.py:762
  256.6 16.9 %multiply.7.rows_ref.refs_0_ = bf16[1024,3072]{1,0:T(8,128)(2,1)} custom-call(bf16[1024,2048]{1,0:T(8,128)(2,1)S(1)} %copy-done.1, bf16[3072,2048]{1,0:T(8,128)(2,1)} %arrange.3.refs_1_.refs_4_.refs_5_.refs_6_.refs_7_, f32[1,3072]{1,0:T(1,128)S(1)} %reshape.511.refs_2_), custom_call_target="tpu_custom_call" | custom-call | flops 1 | bytes 1 | tf_op jit(solution)/shard_map/multiply/pallas_call | solution.py:405
  277.6 29.7 %attend.1.refs_0_.right = bf16[1024,1024]{1,0:T(8,128)(2,1)S(1)} custom-call(bf16[1024,3072]{1,0:T(8,128)(2,1)} %multiply.7.rows_ref.refs_0_, bf16[1024,64]{1,0:T(8,128)(2,1)S(1)} %broadcast_in_dim.44.mask_ref.refs_2_), custom_call_target="tpu_custom_call" | custom-call | flops 1 | bytes 1 | tf_op jit(solution)/shard_map/attend/pallas_call | solution.py:535
  357.9 45.4 %collective-permute-done.25 = bf16[512,2048]{1,0:T(8,128)(2,1)} collective-permute-done((bf16[512,2048]{1,0:T(8,128)(2,1)S(1)}, bf16[512,2048]{1,0:T(8,128)(2,1)}, u32[]{:S(2)}, u32[]{:S(2)}) %collective-permute-start.25) | collective-permute-done | bytes 2097184 | tf_op jit(solution)/shard_map/ppermute | solution.py:54
  405.3 42.9 %collective-permute-done.23 = bf16[512,2048]{1,0:T(8,128)(2,1)S(1)} collective-permute-done((bf16[512,2048]{1,0:T(8,128)(2,1)S(1)}, bf16[512,2048]{1,0:T(8,128)(2,1)S(1)}, u32[]{:S(2)}, u32[]{:S(2)}) %collective-permute-start.23) | collective-permute-done | bytes 2097184 | tf_op jit(solution)/shard_map/ppermute | solution.py:54
  462.6 16.4 %multiply.9 = (bf16[1024,2048]{1,0:T(8,128)(2,1)S(1)}, bf16[1024,2048]{1,0:T(8,128)(2,1)}) custom-call(bf16[1024,2048]{1,0:T(8,128)(2,1)} %get-tuple-element.430.refs_0_.refs_2_, bf16[2048,2048]{1,0:T(8,128)(2,1)} %arrange.5.refs_1_, f32[1,2048]{1,0:T(1,128)S(1)} %reshape.516.refs_2_), custom_call_target="tpu_custom_call" | custom-call | flops 1 | bytes 1 | tf_op jit(solution)/shard_map/multiply/pallas_call | solution.py:405
  486.9 16.4 %multiply.10 = (bf16[1024,2048]{1,0:T(8,128)(2,1)S(1)}, bf16[1024,2048]{1,0:T(8,128)(2,1)}) custom-call(bf16[1024,2048]{1,0:T(8,128)(2,1)} %maximum_select_fusion.2.refs_0_.refs_3_, bf16[2048,2048]{1,0:T(8,128)(2,1)} %arrange.5.refs_1_, f32[1,2048]{1,0:T(1,128)S(1)} %reshape.516.refs_2_), custom_call_target="tpu_custom_call" | custom-call | flops 1 | bytes 1 | tf_op jit(solution)/shard_map/multiply/pallas_call | solution.py:405
  517.0 23.4 %outer_rows_of.7 = bf16[2048,2048]{1,0:T(8,128)(2,1)} custom-call(s32[2]{0:T(128)S(1)} %iota.19.table_ref, bf16[1024,2048]{1,0:T(8,128)(2,1)S(1)} %regroup.2.refs_0_, bf16[1024,2048]{1,0:T(8,128)(2,1)} %copy-done.16, bf16[1024,2048]{1,0:T(8,128)(2,1)} %copy-done.13, bf16[1024,2048]{1,0:T(8,128)(2,1)} %copy-done.14), custom_call_target="tpu_custom_call" | custom-call | flops 1 | bytes 1 | tf_op jit(solution)/shard_map/outer_rows_of/pallas_call | solution.py:184
  540.4 13.2 %multiply.11 = (bf16[1024,2048]{1,0:T(8,128)(2,1)S(1)}, f32[1,2048]{1,0:T(1,128)S(1)}) custom-call(bf16[1024,2048]{1,0:T(8,128)(2,1)} %copy-done.16, bf16[2048,2048]{1,0:T(8,128)(2,1)} %all-gather.8.cloned.1.call-done.refs_1_, bf16[1024,2048]{1,0:T(8,128)(2,1)} %get-tuple-element.376.refs_2_), custom_call_target="tpu_custom_call" | custom-call | flops 1 | bytes 1 | tf_op jit(solution)/shard_map/multiply/pallas_call | solution.py:405
  574.7 13.2 %multiply.12 = (bf16[1024,2048]{1,0:T(8,128)(2,1)S(1)}, f32[1,2048]{1,0:T(1,128)S(1)}) custom-call(bf16[1024,2048]{1,0:T(8,128)(2,1)} %copy-done.15, bf16[2048,2048]{1,0:T(8,128)(2,1)} %all-gather.8.cloned.1.call-done.refs_1_, bf16[1024,2048]{1,0:T(8,128)(2,1)} %get-tuple-element.386.refs_2_), custom_call_target="tpu_custom_call" | custom-call | flops 1 | bytes 1 | tf_op jit(solution)/shard_map/multiply/pallas_call | solution.py:405
  609.8 13.0 %outer_rows_of.8 = bf16[1024,2048]{1,0:T(8,128)(2,1)S(1)} custom-call(s32[1]{0:T(128)} %bitcast.44.table_ref, bf16[1024,2048]{1,0:T(8,128)(2,1)} %copy-done.3, bf16[1024,2048]{1,0:T(8,128)(2,1)} %copy-done.2, bf16[1024,2048]{1,0:T(8,128)(2,1)} %get-tuple-element.430.refs_0_.refs_2_, bf16[1024,2048]{1,0:T(8,128)(2,1)} %maximum_select_fusion.2.refs_0_.refs_3_), custom_call_target="tpu_custom_call" | custom-call | flops 1 | bytes 1 | tf_op jit(solution)/shard_map/outer_rows_of/pallas_call | solution.py:184
  664.4 13.2 %attend_back.4.refs_0_.refs_3_ = bf16[1024,768]{1,0:T(8,128)(2,1)S(1)} custom-call(s32[1]{0:T(128)} %bitcast.48.place_ref, bf16[1024,3072]{1,0:T(8,128)(2,1)} %multiply.7.rows_ref.refs_0_, bf16[1024,1024]{1,0:T(8,128)(2,1)S(1)} %multiply.13.refs_1_, bf16[1024,64]{1,0:T(8,128)(2,1)S(1)} %broadcast_in_dim.44.mask_ref.refs_2_), custom_call_target="tpu_custom_call" | custom-call | flops 1 | bytes 1 | tf_op jit(solution)/shard_map/attend_back/pallas_call | solution.py:557
  685.1 13.4 %attend_back.5.refs_0_.refs_1_ = bf16[1024,768]{1,0:T(8,128)(2,1)S(1)} custom-call(s32[1]{0:T(128)} %bitcast.46.place_ref, bf16[1024,3072]{1,0:T(8,128)(2,1)} %multiply.7.rows_ref.refs_0_, bf16[1024,1024]{1,0:T(8,128)(2,1)S(1)} %multiply.13.refs_1_, bf16[1024,64]{1,0:T(8,128)(2,1)S(1)} %broadcast_in_dim.44.mask_ref.refs_2_), custom_call_target="tpu_custom_call" | custom-call | flops 1 | bytes 1 | tf_op jit(solution)/shard_map/attend_back/pallas_call | solution.py:557
  706.5 13.2 %attend_back.6.refs_0_.refs_2_ = bf16[1024,768]{1,0:T(8,128)(2,1)S(1)} custom-call(s32[1]{0:T(128)} %bitcast.47.place_ref, bf16[1024,3072]{1,0:T(8,128)(2,1)} %multiply.7.rows_ref.refs_0_, bf16[1024,1024]{1,0:T(8,128)(2,1)S(1)} %multiply.13.refs_1_, bf16[1024,64]{1,0:T(8,128)(2,1)S(1)} %broadcast_in_dim.44.mask_ref.refs_2_), custom_call_target="tpu_custom_call" | custom-call | flops 1 | bytes 1 | tf_op jit(solution)/shard_map/attend_back/pallas_call | solution.py:557
  738.7 16.0 %collective-permute-done.33 = bf16[768,2048]{1,0:T(8,128)(2,1)} collective-permute-done((bf16[768,2048]{1,0:T(8,128)(2,1)}, bf16[768,2048]{1,0:T(8,128)(2,1)}, u32[]{:S(2)}, u32[]{:S(2)}) %collective-permute-start.33) | collective-permute-done | bytes 3145760 | tf_op jit(solution)/shard_map/ppermute | solution.py:54
  766.7 13.2 %attend_back.7.refs_0_ = bf16[1024,768]{1,0:T(8,128)(2,1)S(1)} custom-call(s32[1]{0:T(128)} %bitcast.45.place_ref, bf16[1024,3072]{1,0:T(8,128)(2,1)} %multiply.7.rows_ref.refs_0_, bf16[1024,1024]{1,0:T(8,128)(2,1)S(1)} %multiply.13.refs_1_, bf16[1024,64]{1,0:T(8,128)(2,1)S(1)} %broadcast_in_dim.44.mask_ref.refs_2_), custom_call_target="tpu_custom_call" | custom-call | flops 1 | bytes 1 | tf_op jit(solution)/shard_map/attend_back/pallas_call | solution.py:557
  819.4 13.6 %half_dot.17.own = f32[512,2048]{1,0:T(8,128)} custom-call(s32[5]{0:T(128)S(1)} %stack.195.table_ref, bf16[1024,768]{1,0:T(8,128)(2,1)S(1)} %copy-done.11, bf16[1024,768]{1,0:T(8,128)(2,1)S(1)} %copy-done.9, bf16[1024,768]{1,0:T(8,128)(2,1)S(1)} %copy-done.7, bf16[1024,768]{1,0:T(8,128)(2,1)} %copy-done.4, ...), custom_call_target="tpu_custom_call" | custom-call | flops 1 | bytes 1 | tf_op jit(solution)/shard_map/half_dot/pallas_call | solution.py:340
  865.2 24.5 %collective-permute-done.37 = f32[4,4,768]{2,1,0:T(4,128)S(1)} collective-permute-done((f32[4,4,768]{2,1,0:T(4,128)S(1)}, f32[4,4,768]{2,1,0:T(4,128)S(1)}, u32[]{:S(2)}, u32[]{:S(2)}) %collective-permute-start.37) | collective-permute-done | bytes 49184 | tf_op jit(solution)/shard_map/ppermute | solution.py:54
  941.7 17.8 %collective-permute-done.46 = bf16[512,2048]{1,0:T(8,128)(2,1)} collective-permute-done((bf16[512,2048]{1,0:T(8,128)(2,1)S(1)}, bf16[512,2048]{1,0:T(8,128)(2,1)}, u32[]{:S(2)}, u32[]{:S(2)}) %collective-permute-start.46) | collective-permute-done | bytes 2097184 | tf_op jit(solution)/shard_map/ppermute | solution.py:54
  974.7 16.6 %collective-permute-done.49 = bf16[256,2048]{1,0:T(8,128)(2,1)} collective-permute-done((bf16[256,2048]{1,0:T(8,128)(2,1)S(1)}, bf16[256,2048]{1,0:T(8,128)(2,1)}, u32[]{:S(2)}, u32[]{:S(2)}) %collective-permute-start.49) | collective-permute-done | bytes 1048608 | tf_op jit(solution)/shard_map/ppermute | solution.py:54
  1029.7 33.7 %collective-permute-done.48 = bf16[256,2048]{1,0:T(8,128)(2,1)} collective-permute-done((bf16[256,2048]{1,0:T(8,128)(2,1)}, bf16[256,2048]{1,0:T(8,128)(2,1)}, u32[]{:S(2)}, u32[]{:S(2)}) %collective-permute-start.48) | collective-permute-done | bytes 1048608 | tf_op jit(solution)/shard_map/ppermute | solution.py:762
  (425 shorter events, 532.4 us)
Async XLA Ops:
  7.3 84.6 %all-gather.4.cloned.1.call-start = ((), (), s32[]{:S(2)}) async-start(), calls=%async_computation.4 | async-start | bytes 5242880 | tf_op jit(solution)/shard_map/all_gather | solution.py:784
  12.4 295.0 %all-gather.6.cloned.1.call-start = ((), (), s32[]{:S(2)}) async-start(), calls=%async_computation.5 | async-start | bytes 5242880 | tf_op jit(solution)/shard_map/all_gather | solution.py:784
  95.9 69.4 %collective-permute-start.11 = (bf16[768,2048]{1,0:T(8,128)(2,1)}, bf16[768,2048]{1,0:T(8,128)(2,1)}, u32[]{:S(2)}, u32[]{:S(2)}) collective-permute-start(bf16[768,2048]{1,0:T(8,128)(2,1)} %bitcast.9.refs_0_), channel_id=1, source_target_pairs={{0,8},{8,0},{1,9},{9,1},{2,10},{10,2},{3,11},{11,3},{4,12},{12,4},... | collective-permute-start | bytes 9437192 | tf_op jit(solution)/shard_map/ppermute | solution.py:54
  97.2 70.8 %collective-permute-start.10 = (bf16[768,2048]{1,0:T(8,128)(2,1)}, bf16[768,2048]{1,0:T(8,128)(2,1)}, u32[]{:S(2)}, u32[]{:S(2)}) collective-permute-start(bf16[768,2048]{1,0:T(8,128)(2,1)} %bitcast.9.refs_0_), channel_id=1, source_target_pairs={{0,16},{16,0},{1,17},{17,1},{2,18},{18,2},{3,19},{19,3},{4,20},{20... | collective-permute-start | bytes 9437192 | tf_op jit(solution)/shard_map/ppermute | solution.py:54
  98.3 72.4 %collective-permute-start = (bf16[528,2048]{1,0:T(8,128)(2,1)}, bf16[528,2048]{1,0:T(8,128)(2,1)}, u32[]{:S(2)}, u32[]{:S(2)}) collective-permute-start(bf16[528,2048]{1,0:T(8,128)(2,1)} %get-tuple-element.283), channel_id=1, source_target_pairs={{0,0},{1,1},{2,4},{3,5},{4,2},{5,3},{6,6},{7,7},{8,8},{9,9},{10,12... | collective-permute-start | bytes 6488072 | tf_op jit(solution)/shard_map/ppermute | solution.py:762
  103.4 94.3 %collective-permute-start.1 = (bf16[528,2048]{1,0:T(8,128)(2,1)S(1)}, bf16[528,2048]{1,0:T(8,128)(2,1)}, u32[]{:S(2)}, u32[]{:S(2)}) collective-permute-start(bf16[528,2048]{1,0:T(8,128)(2,1)S(1)} %get-tuple-element.284), channel_id=1, source_target_pairs={{0,1},{1,0},{2,5},{3,4},{4,3},{5,2},{6,7},{7,6},{8,9},{9,8},{10,13... | collective-permute-start | bytes 6488072 | tf_op jit(solution)/shard_map/ppermute | solution.py:762
  203.9 336.6 %all-gather.8.cloned.1.call-start = ((), (), s32[]{:S(2)}) async-start(), calls=%async_computation.6 | async-start | bytes 10485760 | tf_op jit(solution)/shard_map/all_gather | solution.py:784
  254.1 53.2 %collective-permute-start.17 = (bf16[256,2048]{1,0:T(8,128)(2,1)S(1)}, bf16[256,2048]{1,0:T(8,128)(2,1)}, u32[]{:S(2)}, u32[]{:S(2)}) collective-permute-start(bf16[256,2048]{1,0:T(8,128)(2,1)S(1)} %constant_dynamic-update-slice_fusion.13.refs_0_), channel_id=1, source_target_pairs={{0,8},{8,0},{1,9},{9,1},{2,10},{10,2},{3,11},{11,3},{4,12},{12,4},... | collective-permute-start | bytes 3145736 | tf_op jit(solution)/shard_map/ppermute | solution.py:54
  327.1 639.2 %reduce-scatter.7.cloned.1.call-start = ((), (), s32[]{:S(2)}) async-start(), calls=%async_computation.8 | async-start | bytes 10485760 | tf_op jit(solution)/shard_map/reduce_scatter | solution.py:982
  335.2 119.0 %collective-permute-start.22 = (bf16[1024,2048]{1,0:T(8,128)(2,1)}, bf16[1024,2048]{1,0:T(8,128)(2,1)}, u32[]{:S(2)}, u32[]{:S(2)}) collective-permute-start(bf16[1024,2048]{1,0:T(8,128)(2,1)} %all-gather.6.cloned.1.call-done.refs_0_), channel_id=1, source_target_pairs={{0,16},{16,0},{1,17},{17,1},{2,18},{18,2},{3,19},{19,3},{4,20},{20... | collective-permute-start | bytes 12582920 | tf_op jit(solution)/shard_map/ppermute | solution.py:54
  357.6 90.7 %collective-permute-start.23 = (bf16[512,2048]{1,0:T(8,128)(2,1)S(1)}, bf16[512,2048]{1,0:T(8,128)(2,1)S(1)}, u32[]{:S(2)}, u32[]{:S(2)}) collective-permute-start(bf16[512,2048]{1,0:T(8,128)(2,1)S(1)} %copy-done.43), channel_id=1, source_target_pairs={{0,8},{8,0},{1,9},{9,1},{2,10},{10,2},{3,11},{11,3},{4,12},{12,4},... | collective-permute-start | bytes 6291464 | tf_op jit(solution)/shard_map/ppermute | solution.py:54
  403.3 77.6 %collective-permute-start.26 = (bf16[512,2048]{1,0:T(8,128)(2,1)}, bf16[512,2048]{1,0:T(8,128)(2,1)}, u32[]{:S(2)}, u32[]{:S(2)}) collective-permute-start(bf16[512,2048]{1,0:T(8,128)(2,1)} %collective-permute-done.25), channel_id=1, source_target_pairs={{0,4},{4,0},{1,5},{5,1},{2,6},{6,2},{3,7},{7,3},{8,12},{12,8},{9,1... | collective-permute-start | bytes 6291464 | tf_op jit(solution)/shard_map/ppermute | solution.py:54
  448.3 56.9 %collective-permute-start.24 = (bf16[512,2048]{1,0:T(8,128)(2,1)S(1)}, bf16[512,2048]{1,0:T(8,128)(2,1)}, u32[]{:S(2)}, u32[]{:S(2)}) collective-permute-start(bf16[512,2048]{1,0:T(8,128)(2,1)S(1)} %collective-permute-done.23), channel_id=1, source_target_pairs={{0,4},{4,0},{1,5},{5,1},{2,6},{6,2},{3,7},{7,3},{8,12},{12,8},{9,1... | collective-permute-start | bytes 6291464 | tf_op jit(solution)/shard_map/ppermute | solution.py:54
  540.4 427.4 %reduce-scatter.9.cloned.1.call-start = ((), (), s32[]{:S(2)}) async-start(), calls=%async_computation.9 | async-start | bytes 5242880 | tf_op jit(solution)/shard_map/reduce_scatter | solution.py:982
  634.6 125.3 %collective-permute-start.32 = (bf16[1024,2048]{1,0:T(8,128)(2,1)S(1)}, bf16[1024,2048]{1,0:T(8,128)(2,1)}, u32[]{:S(2)}, u32[]{:S(2)}) collective-permute-start(bf16[1024,2048]{1,0:T(8,128)(2,1)S(1)} %copy-done.25), channel_id=1, source_target_pairs={{0,16},{16,0},{1,17},{17,1},{2,18},{18,2},{3,19},{19,3},{4,20},{20... | collective-permute-start | bytes 12582920 | tf_op jit(solution)/shard_map/ppermute | solution.py:54
  685.1 69.6 %collective-permute-start.33 = (bf16[768,2048]{1,0:T(8,128)(2,1)}, bf16[768,2048]{1,0:T(8,128)(2,1)}, u32[]{:S(2)}, u32[]{:S(2)}) collective-permute-start(bf16[768,2048]{1,0:T(8,128)(2,1)} %outer_rows_of.9), channel_id=1, source_target_pairs={{0,8},{8,0},{1,9},{9,1},{2,10},{10,2},{3,11},{11,3},{4,12},{12,4},... | collective-permute-start | bytes 9437192 | tf_op jit(solution)/shard_map/ppermute | solution.py:54
  766.3 228.0 %reduce-scatter.11.cloned.1.call-start = ((), (), s32[]{:S(2)}) async-start(), calls=%async_computation.10 | async-start | bytes 3932160 | tf_op jit(solution)/shard_map/reduce_scatter | solution.py:982
  766.4 68.7 %collective-permute-start.35 = (bf16[768,2048]{1,0:T(8,128)(2,1)}, bf16[768,2048]{1,0:T(8,128)(2,1)}, u32[]{:S(2)}, u32[]{:S(2)}) collective-permute-start(bf16[768,2048]{1,0:T(8,128)(2,1)} %copy-done.26), channel_id=1, source_target_pairs={{0,8},{8,0},{1,9},{9,1},{2,10},{10,2},{3,11},{11,3},{4,12},{12,4},... | collective-permute-start | bytes 9437192 | tf_op jit(solution)/shard_map/ppermute | solution.py:54
  766.7 72.4 %collective-permute-start.36 = (bf16[768,2048]{1,0:T(8,128)(2,1)}, bf16[768,2048]{1,0:T(8,128)(2,1)}, u32[]{:S(2)}, u32[]{:S(2)}) collective-permute-start(bf16[768,2048]{1,0:T(8,128)(2,1)} %add_convert_fusion.2), channel_id=1, source_target_pairs={{0,16},{16,0},{1,17},{17,1},{2,18},{18,2},{3,19},{19,3},{4,20},{20... | collective-permute-start | bytes 9437192 | tf_op jit(solution)/shard_map/ppermute | solution.py:54
  811.2 89.4 %collective-permute-start.41 = (bf16[256,2048]{1,0:T(8,128)(2,1)}, bf16[256,2048]{1,0:T(8,128)(2,1)}, u32[]{:S(2)}, u32[]{:S(2)}) collective-permute-start(bf16[256,2048]{1,0:T(8,128)(2,1)} %copy-done.33), channel_id=1, source_target_pairs={{0,8},{8,0},{1,9},{9,1},{2,10},{10,2},{3,11},{11,3},{4,12},{12,4},... | collective-permute-start | bytes 3145736 | tf_op jit(solution)/shard_map/ppermute | solution.py:54
  835.1 60.1 %collective-permute-start.43 = (bf16[512,2048]{1,0:T(8,128)(2,1)}, bf16[512,2048]{1,0:T(8,128)(2,1)}, u32[]{:S(2)}, u32[]{:S(2)}) collective-permute-start(bf16[512,2048]{1,0:T(8,128)(2,1)} %half_dot.14), channel_id=1, source_target_pairs={{0,4},{4,0},{1,5},{5,1},{2,6},{6,2},{3,7},{7,3},{8,12},{12,8},{9,1... | collective-permute-start | bytes 6291464 | tf_op jit(solution)/shard_map/ppermute | solution.py:54
  846.0 180.0 %reduce-scatter.5.cloned.1.call-start = ((), (), s32[]{:S(2)}) async-start(), calls=%async_computation.7 | async-start | bytes 1638400 | tf_op jit(solution)/shard_map/reduce_scatter | solution.py:982
  912.9 57.8 %collective-permute-start.50 = (bf16[256,2048]{1,0:T(8,128)(2,1)}, bf16[256,2048]{1,0:T(8,128)(2,1)}, u32[]{:S(2)}, u32[]{:S(2)}) collective-permute-start(bf16[256,2048]{1,0:T(8,128)(2,1)} %get-tuple-element.543), channel_id=1, source_target_pairs={{0,0},{1,1},{4,2},{5,3},{2,4},{3,5},{6,6},{7,7},{8,8},{9,9},{12,10... | collective-permute-start | bytes 3145736 | tf_op jit(solution)/shard_map/ppermute | solution.py:762
  914.8 55.8 %collective-permute-start.51 = (bf16[256,2048]{1,0:T(8,128)(2,1)}, bf16[256,2048]{1,0:T(8,128)(2,1)}, u32[]{:S(2)}, u32[]{:S(2)}) collective-permute-start(bf16[256,2048]{1,0:T(8,128)(2,1)} %get-tuple-element.542), channel_id=1, source_target_pairs={{1,0},{0,1},{5,2},{4,3},{3,4},{2,5},{7,6},{6,7},{9,8},{8,9},{13,10... | collective-permute-start | bytes 3145736 | tf_op jit(solution)/shard_map/ppermute | solution.py:762
  (97 other events, 1234.7 us)
Sparse Core Ops, SparseCore 0:
  12.5 79.3 all-gather.3
  204.0 76.5 all-gather.5
  327.2 149.4 all-gather.7
  540.5 143.9 reduce-scatter.6
  766.5 76.6 reduce-scatter.8
  846.1 59.5 reduce-scatter.10
  967.8 31.0 reduce-scatter.4

commit v4 on v3

--- a/solution.py
+++ b/solution.py
@@ -356,7 +356,9 @@
     )(table, *lefts, *[right] * count)
 
 
-def multiply(lefts, rights, by_columns, tile=512, bias=None, slope=None, lift=False):
+def multiply(
+    lefts, rights, by_columns, tile=512, bias=None, slope=None, lift=False, halves=False
+):
     rows = lefts[0].shape[0]
     terms = len(lefts)
     columns = rights[0].shape[0] if by_columns else rights[0].shape[1]
@@ -367,6 +369,9 @@
     row = pl.BlockSpec((1, tile), lambda i: (0, i))
     wide = jax.ShapeDtypeStruct((rows, columns), jnp.bfloat16)
     outs = [(across, wide)]
+    if halves:
+        part = pl.BlockSpec((rows // 2, tile), lambda i: (0, i))
+        outs = [(part, jax.ShapeDtypeStruct((rows // 2, columns), jnp.bfloat16))] * 2
     if lift:
         outs.append((across, wide))
     if slope is not None:
@@ -394,6 +399,9 @@
             low = (total * rest[len(extra) - 1][...].astype(jnp.float32)).astype(jnp.bfloat16)
             out[...] = low
             rest[len(extra) + 1][...] = jnp.sum(low.astype(jnp.float32), axis=0, keepdims=True)
+        elif halves:
+            out[...] = total[: rows // 2].astype(jnp.bfloat16)
+            rest[len(extra) + 1][...] = total[rows // 2 :].astype(jnp.bfloat16)
         else:
             out[...] = total.astype(jnp.bfloat16)
 
@@ -600,11 +608,23 @@
 
 
 def middle_kernel(
-    start_ref, tokens, own, upper, lower, active, bias, gain, shift, middle_out, rows_out
+    start_ref,
+    tokens,
+    own_upper,
+    own_lower,
+    upper,
+    lower,
+    active,
+    bias,
+    gain,
+    shift,
+    middle_out,
+    rows_out,
 ):
     in_upper = pl.program_id(0) < pl.num_programs(0) // 2
+    own = jnp.where(in_upper, own_upper[...], own_lower[...])
     got = jnp.where(in_upper, upper[...], lower[...])
-    branch = own[...].astype(jnp.float32) + got.astype(jnp.float32) + bias[...]
+    branch = own.astype(jnp.float32) + got.astype(jnp.float32) + bias[...]
     middle = tokens[...].astype(jnp.float32) + active[...] * branch
     middle_out[...] = middle
     normed, _ = normal_parts(middle)
@@ -699,7 +719,7 @@
     return lax.optimization_barrier((value, others))[0]
 
 
-MIDDLE_KINDS = ("rows", "rows", "upper", "lower", "flag", "vector", "vector", "vector")
+MIDDLE_KINDS = ("rows", "upper", "lower", "upper", "lower", "flag", "vector", "vector", "vector")
 BACK_KINDS = ("from", "from", "rows", "upper", "lower", "rows", "flag from", "vector")
 
 
@@ -798,14 +818,10 @@
 
     vectors = [first_gain, first_shift, query_bias, value_bias, output_bias, second_gain]
     vectors += [second_shift, shrink_bias, expand_bias]
-    shard_a = line(
-        lambda *parts: jnp.concatenate(parts, 0),
-        query_weight,
-        key_weight,
-        value_weight,
-        output_weight,
-    )
-    z_a = through_z(shard_a)
+    shard_qkv = line(
+        lambda *parts: jnp.concatenate(parts, 0), query_weight, key_weight, value_weight
+    )
+    z_qkv = through_z(shard_qkv)
     vectors = line(lambda *parts: jnp.concatenate(parts)[None, None], *vectors)
     shifted = [shift_z(vectors, steps) for steps in range(1, seq_size)]
     alive = (exit_layer > LAYER).astype(low)
@@ -853,16 +869,10 @@
 
     half_qkv = 3 * depth_rows // 2
 
-    def cut_a(rows):
-        cut = rows.reshape(seq_size, -1, width)
-        return (
-            cut[:, : 3 * heads_rows].reshape(-1, width),
-            cut[:, 3 * heads_rows :].reshape(-1, width),
-        )
-
-    arrived = send(*(after(part, z_a) for part in message), False)
-    z_qkv, z_out = line(cut_a, z_a)
+    z_qkv = after(z_qkv, vectors, shard_shrink)
     beside_qkv, across_qkv = swap(z_qkv, ALONG_X), swap(z_qkv, ALONG_Y)
+    z_out = through_z(after(output_weight, z_qkv))
+    arrived = send(*(after(part, z_out) for part in message), False)
     mine, theirs = line(lambda rows: split_columns(core, rows, depth_rows), z_out)
     rows_out = line(
         lambda own, other: jnp.concatenate([own, other], 1), mine, swap(theirs, CORE)
@@ -870,8 +880,21 @@
     upper = line(lambda rows: rows[:half_qkv], beside_qkv)
     lower = line(lambda rows: rows[half_qkv:], across_qkv)
     upper, lower = swap(upper, ALONG_Y), swap(lower, ALONG_X)
+    z_expand = through_z(after(expand_weight, *arrived))
+    w_qkv = line(
+        lambda *pieces: arrange(
+            pieces,
+            (half_qkv, width),
+            [(p, r, 0) for p in range(3) for r in range(2)] + [(3, 0, 0), (4, 0, 0)],
+            [2 * places[d] + r for d in range(4) for r in range(2)],
+        ),
+        z_qkv,
+        beside_qkv,
+        across_qkv,
+        upper,
+        lower,
+    )
     half = line(paired, *arrived)
-    z_expand = through_z(after(expand_weight, half))
     joined = line(by_core, half, swap(half, CORE))
     inputs = joined[:, :local_len].reshape(full_len, width)
     alive = joined[:, local_len, :local_len].reshape(full_len, 1)
@@ -882,11 +905,6 @@
     no_start = jnp.zeros((1,), jnp.int32)
     half_start = (core * (half_len // ROWS)).reshape(1)
 
-    grad_shrunk = line(
-        lambda flags, grads: (flags * grads.astype(f32)).astype(low), active, cotangent_full
-    )
-    sent_gs = line(lambda rows: half_rows(rows, core), grad_shrunk)
-    gs_got = swap(sent_gs, ALONG_X)
     (first_rows,) = line(
         lambda *arrays: by_rows(
             first_kernel,
@@ -900,19 +918,6 @@
         gain_one,
         shift_one,
     )
-    w_qkv = line(
-        lambda *pieces: arrange(
-            pieces,
-            (half_qkv, width),
-            [(p, r, 0) for p in range(3) for r in range(2)] + [(3, 0, 0), (4, 0, 0)],
-            [2 * places[d] + r for d in range(4) for r in range(2)],
-        ),
-        z_qkv,
-        beside_qkv,
-        across_qkv,
-        upper,
-        lower,
-    )
     rows_out = after(rows_out, w_qkv)
     out_beside, out_across = swap(rows_out, ALONG_X), swap(rows_out, ALONG_Y)
     across_expand = swap(z_expand, ALONG_Y)
@@ -921,6 +926,11 @@
         lambda rows, weight: multiply((rows,), (weight,), True, bias=bias_rows), first_rows, w_qkv
     )
     out_corner = swap(line(lambda rows: rows * jnp.bfloat16(1), out_across), ALONG_X)
+    grad_shrunk = line(
+        lambda flags, grads: (flags * grads.astype(f32)).astype(low), active, cotangent_full
+    )
+    sent_gs = line(lambda rows: half_rows(rows, core), grad_shrunk)
+    gs_got = swap(sent_gs, ALONG_X)
     mixed = line(attend, qkv, mask)
     w_out = line(
         lambda *pieces: arrange(
@@ -934,8 +944,10 @@
         out_across,
         out_corner,
     )
-    branch = line(lambda rows, weight: multiply((rows,), (weight,), True), mixed, w_out)
-    branch_got = [swap(part, CORE) for part in jnp.split(branch, 2)]
+    branch = line(
+        lambda rows, weight: multiply((rows,), (weight,), True, halves=True), mixed, w_out
+    )
+    branch_got = [swap(part, CORE) for part in branch]
     shard_shrink = line(stacked, shard_shrink, shrink_across)
     w_shrink = through_z(after(shard_shrink, z_expand, branch))
     middle, second_rows = line(
@@ -948,7 +960,7 @@
             "middle_norm",
         ),
         inputs,
-        branch,
+        *branch,
         *branch_got,
         active,
         bias_out,
@@ -976,7 +988,7 @@
     second_peer = line(by_core, second_got, swap(second_got, CORE))
     activated_peer, slope_peer = line(lift, second_peer, w_expand)
 
-    gs_peer = line(by_core, gs_got, swap(gs_got, CORE))
+    gs_peer = line(by_core, gs_got, swap(after(gs_got, activated), CORE))
     gs_peer = line(lambda rows: regroup(bits, rows, seq_size), gs_peer)
     def scatter_z(total):
         return lax.psum_scatter(total, "seq", scatter_dimension=0, tiled=True)
@@ -1074,30 +1086,35 @@
         )
 
     grad_qkv = {3: attend_piece(3)}
-    corner_got = swap(qkv_part(3, 2 * half_qkv, 0), ALONG_X)
+    corner_got = swap(after(qkv_part(3, 2 * half_qkv, 0), out_corner), ALONG_X)
     grad_qkv[1] = attend_piece(1)
+    out_got_y = swap(line(add_rounded, out_parts[2], out_corner), ALONG_Y)
     qkv_x = swap(qkv_part(1, 2 * half_qkv, 0), ALONG_X)
     grad_qkv[2] = attend_piece(2)
     across = qkv_part(2, 2 * half_qkv, 0)
     expand_here = expand_part(0)
+    grad_qkv[0] = attend_piece(0)
     qkv_y = swap(line(add_rounded, across, corner_got), ALONG_Y)
     expand_sum = line(add_rounded, expand_here, expand_got)
     expand_rows = scatter_z(expand_sum)
-    grad_qkv[0] = attend_piece(0)
     here = qkv_part(0, 2 * half_qkv, 0)
     grads_qkv = tuple(grad_qkv[d] for d in range(4))
 
     def first_half(which, dtype):
         return lambda *arrays: half_dot(which, arrays[:4], arrays[4], False, dtype, places=places)
 
-    peer_theirs = line(
-        lambda rows, weight: their_half(rows, weight, True), activated_peer, w_shrink
-    )
+    peer_theirs = line(lambda rows, weight: their_half(rows, weight, True), activated_peer, w_shrink)
     peer_got = swap(peer_theirs, CORE)
     first_theirs = line(first_half(1 - core, low), *grads_qkv, w_qkv)
     first_got = swap(first_theirs, CORE)
     peer_mine = line(lambda rows, weight: my_half(rows, weight, True), activated_peer, w_shrink)
     first_mine = line(first_half(core, f32), *grads_qkv, w_qkv)
+    to_peer = line(
+        lambda *parts: regroup_back(bits, *parts, seq_size, low), peer_mine, peer_got
+    )
+    from_peer = swap(to_peer, ALONG_X)
+    half = shrink_rows.shape[0] // 2
+    shrink_got = swap(line(lambda rows: rows[half:], shrink_rows), ALONG_Y)
     qkv_sum = line(
         lambda *parts: sum(part.astype(f32) for part in parts).astype(low), here, qkv_x, qkv_y
     )
@@ -1120,6 +1137,11 @@
     tokens_parts = send(
         *line(lambda rows: by_parity(rows.reshape(2, local_len, width)), grad_half), True
     )
+
+    def beside_own(peer, rows, flags, bias):
+        return half_rows(rows, core) + half_rows(flags, core) * (peer.astype(f32) + bias)
+
+    rest = line(beside_own, from_peer, middle, active, bias_shrink)
 
     def column_sum(matrix):
         return jnp.sum(matrix.astype(f32), axis=0)
@@ -1162,15 +1184,19 @@
     sums = line(
         all_sums, first_totals, middle_totals, grad_shrunk, own_sums, peer_sums, *grads_qkv
     )
-    out_got_y = swap(line(add_rounded, out_parts[2], out_corner), ALONG_Y)
+    theirs = line(lambda rows, weight: their_half(rows, weight, True), activated, w_shrink)
+    shrunk_got = swap(theirs, CORE)
     sums = line(fold, sums, swap(sums[dp_size // 2 :], ALONG_Y))
+    mine = line(lambda rows, weight: my_half(rows, weight, True), activated, w_shrink)
     sums = line(fold, sums, swap(sums[dp_size // 4 :], ALONG_X))
+    shrunk = line(lambda *parts: regroup_back(bits, *parts, seq_size, f32), mine, shrunk_got)
+
+    def finish(part, other, flags):
+        out = other + half_rows(flags, core) * part
+        return by_parity(out.astype(low).reshape(2, local_len, width))
+
+    out_halves = send(*line(finish, shrunk, rest, active), True)
     sums = line(fold, sums, swap(sums[dp_size // 8 :], CORE))
-
-    to_peer = line(
-        lambda *parts: regroup_back(bits, *parts, seq_size, low), peer_mine, peer_got
-    )
-    from_peer = swap(to_peer, ALONG_X)
     out_sum = line(
         lambda *parts: sum(part.astype(f32) for part in parts).astype(low),
         out_parts[0],
@@ -1178,8 +1204,7 @@
         out_got_y,
     )
     out_got = swap(line(lambda rows: rows[:, width // 2 :], out_sum), CORE)
-    theirs = line(lambda rows, weight: their_half(rows, weight, True), activated, w_shrink)
-    shrunk_got = swap(theirs, CORE)
+    tokens_grad = line(paired, *tokens_parts)
     out_rows = line(
         lambda rows, got: weave_columns(core, rows[:, : width // 2], got, depth_rows),
         out_sum,
@@ -1193,23 +1218,11 @@
         return rows.reshape(-1, width)
 
     out_rows = scatter_z(line(with_vectors, sums, out_rows))
-    mine = line(lambda rows, weight: my_half(rows, weight, True), activated, w_shrink)
-    shrunk = line(lambda *parts: regroup_back(bits, *parts, seq_size, f32), mine, shrunk_got)
-
-    def finish(part, peer, rows, flags, bias):
-        total = part + peer.astype(f32) + bias
-        out = half_rows(rows, core) + half_rows(flags, core) * total
-        return by_parity(out.astype(low).reshape(2, local_len, width))
-
-    out_halves = send(*line(finish, shrunk, from_peer, middle, active, bias_shrink), True)
-
-    half = shrink_rows.shape[0] // 2
-    shrink_got = swap(line(lambda rows: rows[half:], shrink_rows), ALONG_Y)
-    expand_weight_grad = line(lambda rows: rows.astype(f32), expand_rows)
-    tokens_grad = line(paired, *tokens_parts)
+
     shrink_rows = line(lambda rows, got: add_rounded(rows[:half], got), shrink_rows, shrink_got)
     half = half // 2
     shrink_got = swap(line(lambda rows: rows[half:], shrink_rows), ALONG_X)
+    expand_weight_grad = line(lambda rows: rows.astype(f32), expand_rows)
     qkv_weight_grad = line(lambda rows: rows.astype(f32), qkv_rows)
     shrink_rows = line(
         lambda rows, got: weave_columns(along_x, rows[:half], got, hidden_block),
@@ -1217,6 +1230,7 @@
         shrink_got,
     )
     shrink_got = swap(line(lambda rows: rows[heads_rows:], shrink_rows), CORE)
+    layer_out = line(paired, *out_halves)
     shrink_weight_grad = line(
         lambda rows, got: weave_columns(core, rows[:heads_rows], got, hidden_block).astype(f32),
         shrink_rows,
@@ -1229,7 +1243,6 @@
         ),
         out_rows,
     )
-    layer_out = line(paired, *out_halves)
 
     def vector_grad(index):
         return sums[index * heads_rows : (index + 1) * heads_rows]

time: 1080 us -> 1020 us (0.944)
  waiting for transfers between devices: 359 us -> 316 us
  starting transfers between devices: 74.9 us -> 62.9 us
    ppermute x45, waiting for transfers between devices: 257 us -> 191 us  [swap(): return lax.ppermute(values, axis, [(0, 1), (1, 0)])]
    ppermute x3, waiting for transfers between devices: 60.7 us -> 80.5 us  [send(): lax.ppermute(second, DEVICES, routes[1])]
    all_gather x3 -> x4, waiting for transfers between devices: 40.7 us -> 43.8 us  [through_z(): return lax.all_gather(shard, 'seq', axis=0, tiled=True)]
    unnamed x133 -> x106, local copies, waits for them, and re-layouts: 42 us -> 42.3 us
  transfers between devices with their start and end apart: 61 -> 62, of which waited for: 24 -> 24; matrix products, arithmetic and copies ran while one was open for 11% -> 12% of each run, Pallas kernels for 42% -> 44%
where the time goes in v4:
time: 1020 us
  Pallas kernels  450 us (44%)
  waiting for transfers between devices  316 us (31%)
  other arithmetic  92.3 us (9%)
  local copies, waits for them, and re-layouts  79.9 us (8%)
  starting transfers between devices  62.9 us (6%)
  between operations  15.4 us (2%)
    ppermute x45, waiting for transfers between devices, swap(): return lax.ppermute(values, axis, [(0, 1), (1, 0)])  191 us
    pallas_call x7, Pallas kernels, multiply(): pl.pallas_call(kernel, grid=(columns // tile,), in_specs=[pl.BlockSpec(le...  93.1 us
    pallas_call x10, Pallas kernels, half_dot(): pl.pallas_call(kernel, grid_spec=pltpu.PrefetchScalarGridSpec(num_scalar_...  88.2 us
    ppermute x3, waiting for transfers between devices, send(): lax.ppermute(second, DEVICES, routes[1])  80.5 us
    pallas_call x7, Pallas kernels, outer_rows_of(): pl.pallas_call(kernel, grid_spec=pltpu.PrefetchScalarGridSpec(num_scalar_...  75 us
    pallas_call x4, Pallas kernels, attend_back(): pl.pallas_call(kernel, grid_spec=pltpu.PrefetchScalarGridSpec(num_scalar_...  53.3 us
    ppermute x45, starting transfers between devices, swap(): return lax.ppermute(values, axis, [(0, 1), (1, 0)])  46.8 us
    all_gather x4, waiting for transfers between devices, through_z(): return lax.all_gather(shard, 'seq', axis=0, tiled=True)  43.8 us
  transfers between devices with their start and end apart: 62, of which 24 were waited for; matrix products, arithmetic and copies ran while one was open for 12% of the time, Pallas kernels for 44%

profile of v4, /device:TPU:9, one launch (start us, length us, event | category | flops | bytes accessed | tf_op | source)
XLA Modules:
  0.0 1015.6 jit_solution(16840228259497583628)
XLA Ops:
  57.7 16.1 %all-gather.5.cloned.1.call-done.refs_0_ = bf16[768,2048]{1,0:T(8,128)(2,1)} async-done(((bf16[192,2048]{1,0:T(8,128)(2,1)}), bf16[768,2048]{1,0:T(8,128)(2,1)}) %all-gather.5.cloned.1.call-update) | async-done | bytes 3145744 | tf_op jit(solution)/shard_map/all_gather | solution.py:804
  76.3 27.7 %all-gather.7.cloned.1.call-done.first.second = bf16[256,2048]{1,0:T(8,128)(2,1)} async-done(((bf16[64,2048]{1,0:T(8,128)(2,1)}), bf16[256,2048]{1,0:T(8,128)(2,1)}) %all-gather.7.cloned.1.call-update) | async-done | bytes 1048592 | tf_op jit(solution)/shard_map/all_gather | solution.py:804
  113.2 29.9 %collective-permute-done.10.refs_1_ = bf16[768,2048]{1,0:T(8,128)(2,1)} collective-permute-done((bf16[768,2048]{1,0:T(8,128)(2,1)}, bf16[768,2048]{1,0:T(8,128)(2,1)}, u32[]{:S(2)}, u32[]{:S(2)}) %collective-permute-start.10) | collective-permute-done | bytes 3145760 | tf_op jit(solution)/shard_map/ppermute | solution.py:54
  151.0 32.1 %collective-permute-done.14.refs_4_ = bf16[384,2048]{1,0:T(8,128)(2,1)S(1)} collective-permute-done((bf16[384,2048]{1,0:T(8,128)(2,1)}, bf16[384,2048]{1,0:T(8,128)(2,1)S(1)}, u32[]{:S(2)}, u32[]{:S(2)}) %collective-permute-start.14) | collective-permute-done | bytes 1572896 | tf_op jit(solution)/shard_map/ppermute | solution.py:54
  184.1 11.9 %arrange.3.refs_1_.refs_4_.refs_5_.refs_6_.refs_7_ = bf16[3072,2048]{1,0:T(8,128)(2,1)} custom-call(s32[8]{0:T(128)S(1)} %stack.173.table_ref, bf16[768,2048]{1,0:T(8,128)(2,1)} %all-gather.5.cloned.1.call-done.refs_0_, bf16[768,2048]{1,0:T(8,128)(2,1)} %collective-permute-done.10.refs_1_, bf16[768,2048]{1,0:T(8,128)(2,1)} %collective-permute-done.11.refs_2_, ...), custom_call_target="tpu_custom_call" | custom-call | flops 1 | bytes 1 | tf_op jit(solution)/shard_map/arrange/pallas_call | solution.py:94
  238.5 18.4 %multiply.7.rows_ref.refs_0_ = bf16[1024,3072]{1,0:T(8,128)(2,1)} custom-call(bf16[1024,2048]{1,0:T(8,128)(2,1)S(1)} %first_norm.1.refs_0_.refs_1_, bf16[3072,2048]{1,0:T(8,128)(2,1)} %arrange.3.refs_1_.refs_4_.refs_5_.refs_6_.refs_7_, f32[1,3072]{1,0:T(1,128)S(1)} %reshape.498.refs_2_), custom_call_target="tpu_custom_call" | custom-call | flops 1 | bytes 1 | tf_op jit(solution)/shard_map/multiply/pallas_call | solution.py:413
  265.5 29.6 %attend.1.refs_0_.right = bf16[1024,1024]{1,0:T(8,128)(2,1)S(1)} custom-call(bf16[1024,3072]{1,0:T(8,128)(2,1)} %multiply.7.rows_ref.refs_0_, bf16[1024,64]{1,0:T(8,128)(2,1)S(1)} %broadcast_in_dim.44.mask_ref.refs_2_), custom_call_target="tpu_custom_call" | custom-call | flops 1 | bytes 1 | tf_op jit(solution)/shard_map/attend/pallas_call | solution.py:543
  341.6 45.5 %collective-permute-done.25 = bf16[512,2048]{1,0:T(8,128)(2,1)} collective-permute-done((bf16[512,2048]{1,0:T(8,128)(2,1)S(1)}, bf16[512,2048]{1,0:T(8,128)(2,1)}, u32[]{:S(2)}, u32[]{:S(2)}) %collective-permute-start.25) | collective-permute-done | bytes 2097184 | tf_op jit(solution)/shard_map/ppermute | solution.py:54
  393.9 16.2 %collective-permute-done.22.refs_1_ = bf16[1024,2048]{1,0:T(8,128)(2,1)} collective-permute-done((bf16[1024,2048]{1,0:T(8,128)(2,1)}, bf16[1024,2048]{1,0:T(8,128)(2,1)}, u32[]{:S(2)}, u32[]{:S(2)}) %collective-permute-start.22) | collective-permute-done | bytes 4194336 | tf_op jit(solution)/shard_map/ppermute | solution.py:54
  417.5 16.5 %multiply.9 = (bf16[1024,2048]{1,0:T(8,128)(2,1)S(1)}, bf16[1024,2048]{1,0:T(8,128)(2,1)}) custom-call(bf16[1024,2048]{1,0:T(8,128)(2,1)} %get-tuple-element.447.refs_0_.refs_2_, bf16[2048,2048]{1,0:T(8,128)(2,1)} %arrange.5.refs_1_, f32[1,2048]{1,0:T(1,128)S(1)} %reshape.504.refs_2_), custom_call_target="tpu_custom_call" | custom-call | flops 1 | bytes 1 | tf_op jit(solution)/shard_map/multiply/pallas_call | solution.py:413
  443.2 16.4 %multiply.10 = (bf16[1024,2048]{1,0:T(8,128)(2,1)S(1)}, bf16[1024,2048]{1,0:T(8,128)(2,1)}) custom-call(bf16[1024,2048]{1,0:T(8,128)(2,1)} %maximum_select_fusion.2.refs_0_.refs_3_, bf16[2048,2048]{1,0:T(8,128)(2,1)} %arrange.5.refs_1_, f32[1,2048]{1,0:T(1,128)S(1)} %reshape.504.refs_2_), custom_call_target="tpu_custom_call" | custom-call | flops 1 | bytes 1 | tf_op jit(solution)/shard_map/multiply/pallas_call | solution.py:413
  473.3 23.4 %outer_rows_of.7 = bf16[2048,2048]{1,0:T(8,128)(2,1)} custom-call(s32[2]{0:T(128)S(1)} %iota.19.table_ref, bf16[1024,2048]{1,0:T(8,128)(2,1)S(1)} %regroup.2.refs_0_, bf16[1024,2048]{1,0:T(8,128)(2,1)} %copy-done.13, bf16[1024,2048]{1,0:T(8,128)(2,1)} %copy-done.10, bf16[1024,2048]{1,0:T(8,128)(2,1)} %copy-done.11), custom_call_target="tpu_custom_call" | custom-call | flops 1 | bytes 1 | tf_op jit(solution)/shard_map/outer_rows_of/pallas_call | solution.py:184
  496.7 13.2 %multiply.11 = (bf16[1024,2048]{1,0:T(8,128)(2,1)S(1)}, f32[1,2048]{1,0:T(1,128)S(1)}) custom-call(bf16[1024,2048]{1,0:T(8,128)(2,1)} %copy-done.13, bf16[2048,2048]{1,0:T(8,128)(2,1)} %all-gather.11.cloned.1.call-done.refs_1_, bf16[1024,2048]{1,0:T(8,128)(2,1)} %get-tuple-element.389.refs_2_), custom_call_target="tpu_custom_call" | custom-call | flops 1 | bytes 1 | tf_op jit(solution)/shard_map/multiply/pallas_call | solution.py:413
  530.0 13.2 %multiply.12 = (bf16[1024,2048]{1,0:T(8,128)(2,1)S(1)}, f32[1,2048]{1,0:T(1,128)S(1)}) custom-call(bf16[1024,2048]{1,0:T(8,128)(2,1)} %copy-done.12, bf16[2048,2048]{1,0:T(8,128)(2,1)} %all-gather.11.cloned.1.call-done.refs_1_, bf16[1024,2048]{1,0:T(8,128)(2,1)} %get-tuple-element.399.refs_2_), custom_call_target="tpu_custom_call" | custom-call | flops 1 | bytes 1 | tf_op jit(solution)/shard_map/multiply/pallas_call | solution.py:413
  565.2 13.7 %outer_rows_of.8 = bf16[1024,2048]{1,0:T(8,128)(2,1)} custom-call(s32[1]{0:T(128)} %bitcast.41.table_ref, bf16[1024,2048]{1,0:T(8,128)(2,1)} %copy-done.2, bf16[1024,2048]{1,0:T(8,128)(2,1)} %copy-done.1, bf16[1024,2048]{1,0:T(8,128)(2,1)} %get-tuple-element.447.refs_0_.refs_2_, bf16[1024,2048]{1,0:T(8,128)(2,1)} %maximum_select_fusion.2.refs_0_.refs_3_), custom_call_target="tpu_custom_call" | custom-call | flops 1 | bytes 1 | tf_op jit(solution)/shard_map/outer_rows_of/pallas_call | solution.py:184
  618.8 13.2 %attend_back.4.refs_0_.refs_3_ = bf16[1024,768]{1,0:T(8,128)(2,1)S(1)} custom-call(s32[1]{0:T(128)} %bitcast.45.place_ref, bf16[1024,3072]{1,0:T(8,128)(2,1)} %multiply.7.rows_ref.refs_0_, bf16[1024,1024]{1,0:T(8,128)(2,1)S(1)} %multiply.13.refs_1_, bf16[1024,64]{1,0:T(8,128)(2,1)S(1)} %broadcast_in_dim.44.mask_ref.refs_2_), custom_call_target="tpu_custom_call" | custom-call | flops 1 | bytes 1 | tf_op jit(solution)/shard_map/attend_back/pallas_call | solution.py:565
  642.2 13.3 %attend_back.5.refs_0_.refs_1_ = bf16[1024,768]{1,0:T(8,128)(2,1)S(1)} custom-call(s32[1]{0:T(128)} %bitcast.43.place_ref, bf16[1024,3072]{1,0:T(8,128)(2,1)} %multiply.7.rows_ref.refs_0_, bf16[1024,1024]{1,0:T(8,128)(2,1)S(1)} %multiply.13.refs_1_, bf16[1024,64]{1,0:T(8,128)(2,1)S(1)} %broadcast_in_dim.44.mask_ref.refs_2_), custom_call_target="tpu_custom_call" | custom-call | flops 1 | bytes 1 | tf_op jit(solution)/shard_map/attend_back/pallas_call | solution.py:565
  664.3 13.4 %attend_back.6.refs_0_.refs_2_ = bf16[1024,768]{1,0:T(8,128)(2,1)S(1)} custom-call(s32[1]{0:T(128)} %bitcast.44.place_ref, bf16[1024,3072]{1,0:T(8,128)(2,1)} %multiply.7.rows_ref.refs_0_, bf16[1024,1024]{1,0:T(8,128)(2,1)S(1)} %multiply.13.refs_1_, bf16[1024,64]{1,0:T(8,128)(2,1)S(1)} %broadcast_in_dim.44.mask_ref.refs_2_), custom_call_target="tpu_custom_call" | custom-call | flops 1 | bytes 1 | tf_op jit(solution)/shard_map/attend_back/pallas_call | solution.py:565
  683.4 12.7 %outer_rows_of.12 = bf16[1024,2048]{1,0:T(8,128)(2,1)S(1)} custom-call(s32[1]{0:T(128)} %bitcast.table_ref, bf16[1024,2048]{1,0:T(8,128)(2,1)} %copy-done.2, bf16[1024,2048]{1,0:T(8,128)(2,1)} %copy-done.1, bf16[1024,2048]{1,0:T(8,128)(2,1)} %get-tuple-element.447.refs_0_.refs_2_, bf16[1024,2048]{1,0:T(8,128)(2,1)} %maximum_select_fusion.2.refs_0_.refs_3_), custom_call_target="tpu_custom_call" | custom-call | flops 1 | bytes 1 | tf_op jit(solution)/shard_map/outer_rows_of/pallas_call | solution.py:184
  696.1 13.4 %attend_back.7.refs_0_ = bf16[1024,768]{1,0:T(8,128)(2,1)S(1)} custom-call(s32[1]{0:T(128)} %bitcast.42.place_ref, bf16[1024,3072]{1,0:T(8,128)(2,1)} %multiply.7.rows_ref.refs_0_, bf16[1024,1024]{1,0:T(8,128)(2,1)S(1)} %multiply.13.refs_1_, bf16[1024,64]{1,0:T(8,128)(2,1)S(1)} %broadcast_in_dim.44.mask_ref.refs_2_), custom_call_target="tpu_custom_call" | custom-call | flops 1 | bytes 1 | tf_op jit(solution)/shard_map/attend_back/pallas_call | solution.py:565
  765.8 12.7 %half_dot.17.own = f32[512,2048]{1,0:T(8,128)} custom-call(s32[5]{0:T(128)S(1)} %stack.195.table_ref, bf16[1024,768]{1,0:T(8,128)(2,1)S(1)} %copy-done.8, bf16[1024,768]{1,0:T(8,128)(2,1)S(1)} %attend_back.5.refs_0_.refs_1_, bf16[1024,768]{1,0:T(8,128)(2,1)S(1)} %attend_back.6.refs_0_.refs_2_, bf16[1024,768]{1,0:T(8,128)(2,1)} %copy-done.3, ...), custom_call_target="tpu_custom_call" | custom-call | flops 1 | bytes 1 | tf_op jit(solution)/shard_map/half_dot/pallas_call | solution.py:340
  809.9 25.2 %collective-permute-done.39 = bf16[512,2048]{1,0:T(8,128)(2,1)} collective-permute-done((bf16[512,2048]{1,0:T(8,128)(2,1)}, bf16[512,2048]{1,0:T(8,128)(2,1)}, u32[]{:S(2)}, u32[]{:S(2)}) %collective-permute-start.39) | collective-permute-done | bytes 2097184 | tf_op jit(solution)/shard_map/ppermute | solution.py:54
  890.8 23.2 %collective-permute-done.51 = bf16[256,2048]{1,0:T(8,128)(2,1)S(1)} collective-permute-done((bf16[256,2048]{1,0:T(8,128)(2,1)S(1)}, bf16[256,2048]{1,0:T(8,128)(2,1)S(1)}, u32[]{:S(2)}, u32[]{:S(2)}) %collective-permute-start.51) | collective-permute-done | bytes 1048608 | tf_op jit(solution)/shard_map/ppermute | solution.py:782
  945.3 47.1 %collective-permute-done.44 = bf16[256,2048]{1,0:T(8,128)(2,1)} collective-permute-done((bf16[256,2048]{1,0:T(8,128)(2,1)}, bf16[256,2048]{1,0:T(8,128)(2,1)}, u32[]{:S(2)}, u32[]{:S(2)}) %collective-permute-start.44) | collective-permute-done | bytes 1048608 | tf_op jit(solution)/shard_map/ppermute | solution.py:782
  (400 shorter events, 502.4 us)
Async XLA Ops:
  7.2 66.5 %all-gather.5.cloned.1.call-start = ((), (), s32[]{:S(2)}) async-start(), calls=%async_computation.4 | async-start | bytes 3932160 | tf_op jit(solution)/shard_map/all_gather | solution.py:804
  11.2 92.8 %all-gather.7.cloned.1.call-start = ((), (), s32[]{:S(2)}) async-start(), calls=%async_computation.5 | async-start | bytes 1310720 | tf_op jit(solution)/shard_map/all_gather | solution.py:804
  73.7 69.3 %collective-permute-start.10 = (bf16[768,2048]{1,0:T(8,128)(2,1)}, bf16[768,2048]{1,0:T(8,128)(2,1)}, u32[]{:S(2)}, u32[]{:S(2)}) collective-permute-start(bf16[768,2048]{1,0:T(8,128)(2,1)} %all-gather.5.cloned.1.call-done.refs_0_), channel_id=1, source_target_pairs={{0,8},{8,0},{1,9},{9,1},{2,10},{10,2},{3,11},{11,3},{4,12},{12,4},... | collective-permute-start | bytes 9437192 | tf_op jit(solution)/shard_map/ppermute | solution.py:54
  75.0 70.7 %collective-permute-start.11 = (bf16[768,2048]{1,0:T(8,128)(2,1)}, bf16[768,2048]{1,0:T(8,128)(2,1)}, u32[]{:S(2)}, u32[]{:S(2)}) collective-permute-start(bf16[768,2048]{1,0:T(8,128)(2,1)} %all-gather.5.cloned.1.call-done.refs_0_), channel_id=1, source_target_pairs={{0,16},{16,0},{1,17},{17,1},{2,18},{18,2},{3,19},{19,3},{4,20},{20... | collective-permute-start | bytes 9437192 | tf_op jit(solution)/shard_map/ppermute | solution.py:54
  76.2 220.2 %all-gather.9.cloned.1.call-start = ((), (), s32[]{:S(2)}) async-start(), calls=%async_computation.6 | async-start | bytes 5242880 | tf_op jit(solution)/shard_map/all_gather | solution.py:804
  108.3 87.7 %collective-permute-start.8 = (bf16[528,2048]{1,0:T(8,128)(2,1)}, bf16[528,2048]{1,0:T(8,128)(2,1)}, u32[]{:S(2)}, u32[]{:S(2)}) collective-permute-start(bf16[528,2048]{1,0:T(8,128)(2,1)} %get-tuple-element.312), channel_id=1, source_target_pairs={{0,0},{1,1},{2,4},{3,5},{4,2},{5,3},{6,6},{7,7},{8,8},{9,9},{10,12... | collective-permute-start | bytes 6488072 | tf_op jit(solution)/shard_map/ppermute | solution.py:782
  110.8 95.4 %collective-permute-start.9 = (bf16[528,2048]{1,0:T(8,128)(2,1)}, bf16[528,2048]{1,0:T(8,128)(2,1)}, u32[]{:S(2)}, u32[]{:S(2)}) collective-permute-start(bf16[528,2048]{1,0:T(8,128)(2,1)} %get-tuple-element.313), channel_id=1, source_target_pairs={{0,1},{1,0},{2,5},{3,4},{4,3},{5,2},{6,7},{7,6},{8,9},{9,8},{10,13... | collective-permute-start | bytes 6488072 | tf_op jit(solution)/shard_map/ppermute | solution.py:782
  212.2 284.5 %all-gather.11.cloned.1.call-start = ((), (), s32[]{:S(2)}) async-start(), calls=%async_computation.7 | async-start | bytes 10485760 | tf_op jit(solution)/shard_map/all_gather | solution.py:804
  212.9 98.8 %collective-permute-start.21 = (bf16[256,2048]{1,0:T(8,128)(2,1)}, bf16[256,2048]{1,0:T(8,128)(2,1)}, u32[]{:S(2)}, u32[]{:S(2)}) collective-permute-start(bf16[256,2048]{1,0:T(8,128)(2,1)} %constant_dynamic-update-slice_fusion.10), channel_id=1, source_target_pairs={{0,16},{16,0},{1,17},{17,1},{2,18},{18,2},{3,19},{19,3},{4,20},{20... | collective-permute-start | bytes 3145736 | tf_op jit(solution)/shard_map/ppermute | solution.py:54
  215.1 81.3 %collective-permute-start.17 = (bf16[256,2048]{1,0:T(8,128)(2,1)S(1)}, bf16[256,2048]{1,0:T(8,128)(2,1)S(1)}, u32[]{:S(2)}, u32[]{:S(2)}) collective-permute-start(bf16[256,2048]{1,0:T(8,128)(2,1)S(1)} %constant_dynamic-update-slice_fusion.12.refs_0_), channel_id=1, source_target_pairs={{0,8},{8,0},{1,9},{9,1},{2,10},{10,2},{3,11},{11,3},{4,12},{12,4},... | collective-permute-start | bytes 3145736 | tf_op jit(solution)/shard_map/ppermute | solution.py:54
  316.3 468.8 %reduce-scatter.5.cloned.1.call-start = ((), (), s32[]{:S(2)}) async-start(), calls=%async_computation.8 | async-start | bytes 10485760 | tf_op jit(solution)/shard_map/reduce_scatter | solution.py:994
  318.0 92.0 %collective-permute-start.22 = (bf16[1024,2048]{1,0:T(8,128)(2,1)}, bf16[1024,2048]{1,0:T(8,128)(2,1)}, u32[]{:S(2)}, u32[]{:S(2)}) collective-permute-start(bf16[1024,2048]{1,0:T(8,128)(2,1)} %all-gather.9.cloned.1.call-done.refs_0_), channel_id=1, source_target_pairs={{0,16},{16,0},{1,17},{17,1},{2,18},{18,2},{3,19},{19,3},{4,20},{20... | collective-permute-start | bytes 12582920 | tf_op jit(solution)/shard_map/ppermute | solution.py:54
  340.4 95.5 %collective-permute-start.23 = (bf16[512,2048]{1,0:T(8,128)(2,1)S(1)}, bf16[512,2048]{1,0:T(8,128)(2,1)}, u32[]{:S(2)}, u32[]{:S(2)}) collective-permute-start(bf16[512,2048]{1,0:T(8,128)(2,1)S(1)} %copy-done.39), channel_id=1, source_target_pairs={{0,8},{8,0},{1,9},{9,1},{2,10},{10,2},{3,11},{11,3},{4,12},{12,4},... | collective-permute-start | bytes 6291464 | tf_op jit(solution)/shard_map/ppermute | solution.py:54
  496.7 431.3 %reduce-scatter.9.cloned.1.call-start = ((), (), s32[]{:S(2)}) async-start(), calls=%async_computation.10 | async-start | bytes 5242880 | tf_op jit(solution)/shard_map/reduce_scatter | solution.py:994
  617.7 97.7 %collective-permute-start.33 = (bf16[1024,2048]{1,0:T(8,128)(2,1)}, bf16[1024,2048]{1,0:T(8,128)(2,1)}, u32[]{:S(2)}, u32[]{:S(2)}) collective-permute-start(bf16[1024,2048]{1,0:T(8,128)(2,1)} %outer_rows_of.8), channel_id=1, source_target_pairs={{0,16},{16,0},{1,17},{17,1},{2,18},{18,2},{3,19},{19,3},{4,20},{20... | collective-permute-start | bytes 12582920 | tf_op jit(solution)/shard_map/ppermute | solution.py:54
  641.0 68.9 %collective-permute-start.34 = (bf16[768,2048]{1,0:T(8,128)(2,1)}, bf16[768,2048]{1,0:T(8,128)(2,1)}, u32[]{:S(2)}, u32[]{:S(2)}) collective-permute-start(bf16[768,2048]{1,0:T(8,128)(2,1)} %outer_rows_of.9), channel_id=1, source_target_pairs={{0,8},{8,0},{1,9},{9,1},{2,10},{10,2},{3,11},{11,3},{4,12},{12,4},... | collective-permute-start | bytes 9437192 | tf_op jit(solution)/shard_map/ppermute | solution.py:54
  721.8 209.0 %reduce-scatter.7.cloned.1.call-start = ((), (), s32[]{:S(2)}) async-start(), calls=%async_computation.9 | async-start | bytes 3932160 | tf_op jit(solution)/shard_map/reduce_scatter | solution.py:994
  721.9 68.2 %collective-permute-start.36 = (bf16[768,2048]{1,0:T(8,128)(2,1)}, bf16[768,2048]{1,0:T(8,128)(2,1)}, u32[]{:S(2)}, u32[]{:S(2)}) collective-permute-start(bf16[768,2048]{1,0:T(8,128)(2,1)} %copy-done.20), channel_id=1, source_target_pairs={{0,8},{8,0},{1,9},{9,1},{2,10},{10,2},{3,11},{11,3},{4,12},{12,4},... | collective-permute-start | bytes 9437192 | tf_op jit(solution)/shard_map/ppermute | solution.py:54
  722.9 67.7 %collective-permute-start.37 = (bf16[768,2048]{1,0:T(8,128)(2,1)}, bf16[768,2048]{1,0:T(8,128)(2,1)}, u32[]{:S(2)}, u32[]{:S(2)}) collective-permute-start(bf16[768,2048]{1,0:T(8,128)(2,1)} %add_convert_fusion.2), channel_id=1, source_target_pairs={{0,16},{16,0},{1,17},{17,1},{2,18},{18,2},{3,19},{19,3},{4,20},{20... | collective-permute-start | bytes 9437192 | tf_op jit(solution)/shard_map/ppermute | solution.py:54
  806.7 198.2 %reduce-scatter.11.cloned.1.call-start = ((), (), s32[]{:S(2)}) async-start(), calls=%async_computation.11 | async-start | bytes 1638400 | tf_op jit(solution)/shard_map/reduce_scatter | solution.py:994
  863.0 50.9 %collective-permute-start.50 = (bf16[256,2048]{1,0:T(8,128)(2,1)S(1)}, bf16[256,2048]{1,0:T(8,128)(2,1)S(1)}, u32[]{:S(2)}, u32[]{:S(2)}) collective-permute-start(bf16[256,2048]{1,0:T(8,128)(2,1)S(1)} %copy-done.42), channel_id=1, source_target_pairs={{0,0},{1,1},{4,2},{5,3},{2,4},{3,5},{6,6},{7,7},{8,8},{9,9},{12,10... | collective-permute-start | bytes 3145736 | tf_op jit(solution)/shard_map/ppermute | solution.py:782
  922.3 70.1 %collective-permute-start.43 = (bf16[256,2048]{1,0:T(8,128)(2,1)}, bf16[256,2048]{1,0:T(8,128)(2,1)}, u32[]{:S(2)}, u32[]{:S(2)}) collective-permute-start(bf16[256,2048]{1,0:T(8,128)(2,1)} %get-tuple-element.559), channel_id=1, source_target_pairs={{0,0},{1,1},{4,2},{5,3},{2,4},{3,5},{6,6},{7,7},{8,8},{9,9},{12,10... | collective-permute-start | bytes 3145736 | tf_op jit(solution)/shard_map/ppermute | solution.py:782
  924.2 68.2 %collective-permute-start.44 = (bf16[256,2048]{1,0:T(8,128)(2,1)}, bf16[256,2048]{1,0:T(8,128)(2,1)}, u32[]{:S(2)}, u32[]{:S(2)}) collective-permute-start(bf16[256,2048]{1,0:T(8,128)(2,1)} %get-tuple-element.558), channel_id=1, source_target_pairs={{1,0},{0,1},{5,2},{4,3},{3,4},{2,5},{7,6},{6,7},{9,8},{8,9},{13,10... | collective-permute-start | bytes 3145736 | tf_op jit(solution)/shard_map/ppermute | solution.py:782
  940.3 57.5 %collective-permute-start.53 = (bf16[64,4096]{1,0:T(8,128)(2,1)S(1)}, bf16[64,4096]{1,0:T(8,128)(2,1)S(1)}, u32[]{:S(2)}, u32[]{:S(2)}) collective-permute-start(bf16[64,4096]{1,0:T(8,128)(2,1)S(1)} %slice.241), channel_id=1, source_target_pairs={{0,4},{4,0},{1,5},{5,1},{2,6},{6,2},{3,7},{7,3},{8,12},{12,8},{9,1... | collective-permute-start | bytes 1572872 | tf_op jit(solution)/shard_map/ppermute | solution.py:54
  (85 other events, 1328.9 us)
Sparse Core Ops, SparseCore 0:
  11.3 62.3 all-gather.4
  76.3 27.6 all-gather.6
  212.3 77.2 all-gather.8
  316.4 146.2 all-gather.10
  496.8 142.1 reduce-scatter.4
  721.9 77.3 reduce-scatter.8
  806.8 62.9 reduce-scatter.6
  922.4 46.2 reduce-scatter.10

commit v5 on v4

--- a/solution.py
+++ b/solution.py
@@ -100,7 +100,7 @@
             out_specs=pl.BlockSpec(block, lambda step, table_ref: (table_ref[step], 0)),
         ),
         out_shape=jax.ShapeDtypeStruct((steps * block[0], block[1]), pieces[0].dtype),
-        compiler_params=pltpu.CompilerParams(vmem_limit_bytes=48 << 20),
+        compiler_params=pltpu.CompilerParams(vmem_limit_bytes=28 << 20),
         cost_estimate=BRIEF,
         name="arrange",
     )(table, *pieces)
@@ -127,6 +127,7 @@
             out_specs=[pl.BlockSpec((rows, block), lambda i, core_ref: (0, i))] * 2,
         ),
         out_shape=(piece, piece),
+        compiler_params=pltpu.CompilerParams(vmem_limit_bytes=28 << 20),
         cost_estimate=BRIEF,
         name="split_columns",
     )(core.reshape(1), matrix, matrix)
@@ -157,6 +158,7 @@
             out_specs=pl.BlockSpec((rows, 2 * block), lambda i, core_ref: (0, i)),
         ),
         out_shape=jax.ShapeDtypeStruct((rows, 2 * columns), mine.dtype),
+        compiler_params=pltpu.CompilerParams(vmem_limit_bytes=28 << 20),
         cost_estimate=BRIEF,
         name="weave_columns",
     )(core.reshape(1), mine, theirs)
@@ -191,7 +193,7 @@
             out_specs=pl.BlockSpec((rows, tile), lambda i, j, ref: (i, j)),
         ),
         out_shape=jax.ShapeDtypeStruct((blocks * rows, columns), jnp.bfloat16),
-        compiler_params=pltpu.CompilerParams(vmem_limit_bytes=48 << 20),
+        compiler_params=pltpu.CompilerParams(vmem_limit_bytes=28 << 20),
         cost_estimate=BRIEF,
         name="outer_rows_of",
     )(table, *lefts, *rights)
@@ -228,7 +230,7 @@
             out_specs=[pl.BlockSpec((rows, columns), side_of(piece)) for piece in range(pieces)],
         ),
         out_shape=[jax.ShapeDtypeStruct((rows, 2 * columns), jnp.bfloat16)] * pieces,
-        compiler_params=pltpu.CompilerParams(vmem_limit_bytes=48 << 20),
+        compiler_params=pltpu.CompilerParams(vmem_limit_bytes=28 << 20),
         cost_estimate=BRIEF,
         name="outer_sides",
     )(table, left, right)
@@ -264,7 +266,7 @@
             out_specs=pl.BlockSpec((block, columns), lambda i, bits_ref: (i, 0)),
         ),
         out_shape=jax.ShapeDtypeStruct((rows, columns), matrix.dtype),
-        compiler_params=pltpu.CompilerParams(vmem_limit_bytes=48 << 20),
+        compiler_params=pltpu.CompilerParams(vmem_limit_bytes=28 << 20),
         cost_estimate=BRIEF,
         name="regroup",
     )(bits, matrix)
@@ -305,7 +307,7 @@
             out_specs=spec,
         ),
         out_shape=jax.ShapeDtypeStruct((rows, columns), dtype),
-        compiler_params=pltpu.CompilerParams(vmem_limit_bytes=48 << 20),
+        compiler_params=pltpu.CompilerParams(vmem_limit_bytes=28 << 20),
         cost_estimate=BRIEF,
         name="regroup_back",
     )(bits, mine, got)
@@ -350,7 +352,7 @@
             out_specs=pl.BlockSpec((rows // 2, tile), lambda i, table_ref: (0, i)),
         ),
         out_shape=jax.ShapeDtypeStruct((rows // 2, columns), dtype),
-        compiler_params=pltpu.CompilerParams(vmem_limit_bytes=48 << 20),
+        compiler_params=pltpu.CompilerParams(vmem_limit_bytes=28 << 20),
         cost_estimate=BRIEF,
         name="half_dot",
     )(table, *lefts, *[right] * count)
@@ -419,7 +421,7 @@
         + ([] if slope is None else [across]),
         out_specs=[spec for spec, _ in outs],
         out_shape=[shape for _, shape in outs],
-        compiler_params=pltpu.CompilerParams(vmem_limit_bytes=48 << 20),
+        compiler_params=pltpu.CompilerParams(vmem_limit_bytes=28 << 20),
         cost_estimate=BRIEF,
         name="multiply",
     )(*lefts, *rights, *extra)
@@ -549,7 +551,7 @@
         ],
         out_specs=pl.BlockSpec((count, 2 * HEAD_DIM), lambda i: (0, i)),
         out_shape=jax.ShapeDtypeStruct((count, pairs * 2 * HEAD_DIM), jnp.bfloat16),
-        compiler_params=pltpu.CompilerParams(vmem_limit_bytes=48 << 20),
+        compiler_params=pltpu.CompilerParams(vmem_limit_bytes=28 << 20),
         cost_estimate=BRIEF,
         name="attend",
     )(rows, mask)
@@ -580,7 +582,7 @@
             scratch_shapes=[pltpu.VMEM((count, HEAD_DIM), jnp.float32)] * 2,
         ),
         out_shape=jax.ShapeDtypeStruct((count, columns // 4), jnp.bfloat16),
-        compiler_params=pltpu.CompilerParams(vmem_limit_bytes=48 << 20),
+        compiler_params=pltpu.CompilerParams(vmem_limit_bytes=28 << 20),
         cost_estimate=BRIEF,
         name="attend_back",
     )(place.reshape(1), rows, grad, mask)
@@ -709,7 +711,7 @@
             out_specs=[specs[kind] for kind, _ in outs],
         ),
         out_shape=shapes,
-        compiler_params=pltpu.CompilerParams(vmem_limit_bytes=48 << 20),
+        compiler_params=pltpu.CompilerParams(vmem_limit_bytes=28 << 20),
         cost_estimate=BRIEF,
         name=name,
     )(start, *[array for array, _ in arrays])

time: 1020 us -> 1010 us (level)
  Pallas kernels: 450 us -> 345 us
  local copies, waits for them, and re-layouts: 79.9 us -> 168 us
  waiting for transfers between devices: 316 us -> 337 us
    unnamed x106 -> x230, local copies, waits for them, and re-layouts: 42.3 us -> 135 us
    pallas_call x10, Pallas kernels: 88.2 us -> 64.2 us  [half_dot(): pl.pallas_call(kernel, grid_spec=pltpu.PrefetchScalarGridSpec(num_scalar_...]
    pallas_call x7, Pallas kernels: 93.1 us -> 73.8 us  [multiply(): pl.pallas_call(kernel, grid=(columns // tile,), in_specs=[pl.BlockSpec(le...]
    pallas_call x3, Pallas kernels: 25.9 us -> 14.5 us  [arrange(): pl.pallas_call(kernel, grid_spec=pltpu.PrefetchScalarGridSpec(num_scalar_...]
    pallas_call x7, Pallas kernels: 75 us -> 64.1 us  [outer_rows_of(): pl.pallas_call(kernel, grid_spec=pltpu.PrefetchScalarGridSpec(num_scalar_...]
    pallas_call x4, Pallas kernels: 34.1 us -> 23.7 us  [by_rows(): pl.pallas_call(kernel, grid_spec=pltpu.PrefetchScalarGridSpec(num_scalar_...]
  transfers between devices with their start and end apart: 62 -> 62, of which waited for: 24 -> 24; matrix products, arithmetic and copies ran while one was open for 12% -> 11% of each run, Pallas kernels for 44% -> 34%
where the time goes in v5:
time: 1010 us; the launch traced here: 1000 us
  Pallas kernels  345 us (34%)
  waiting for transfers between devices  337 us (33%)
  local copies, waits for them, and re-layouts  168 us (17%)
  other arithmetic  85 us (8%)
  starting transfers between devices  54.3 us (5%)
  between operations  16.1 us (2%)
    ppermute x45, waiting for transfers between devices, swap(): return lax.ppermute(values, axis, [(0, 1), (1, 0)])  195 us
    unnamed x230, local copies, waits for them, and re-layouts  135 us
    ppermute x3, waiting for transfers between devices, send(): lax.ppermute(second, DEVICES, routes[1])  89.8 us
    pallas_call x7, Pallas kernels, multiply(): pl.pallas_call(kernel, grid=(columns // tile,), in_specs=[pl.BlockSpec(le...  73.8 us
    pallas_call x10, Pallas kernels, half_dot(): pl.pallas_call(kernel, grid_spec=pltpu.PrefetchScalarGridSpec(num_scalar_...  64.2 us
    pallas_call x7, Pallas kernels, outer_rows_of(): pl.pallas_call(kernel, grid_spec=pltpu.PrefetchScalarGridSpec(num_scalar_...  64.1 us
    all_gather x4, waiting for transfers between devices, through_z(): return lax.all_gather(shard, 'seq', axis=0, tiled=True)  52.1 us
    pallas_call x4, Pallas kernels, attend_back(): pl.pallas_call(kernel, grid_spec=pltpu.PrefetchScalarGridSpec(num_scalar_...  50.4 us
  transfers between devices with their start and end apart: 62, of which 24 were waited for; matrix products, arithmetic and copies ran while one was open for 11% of the time, Pallas kernels for 34%

profile of v5, /device:TPU:9, one launch (start us, length us, event | category | flops | bytes accessed | tf_op | source)
XLA Modules:
  0.0 1004.7 jit_solution(13717154683236734300)
XLA Ops:
  33.8 11.0 %collective-permute-done.4 = bf16[2,4,768]{2,1,0:T(4,128)(2,1)S(1)} collective-permute-done((bf16[2,4,768]{2,1,0:T(4,128)(2,1)S(1)}, bf16[2,4,768]{2,1,0:T(4,128)(2,1)S(1)}, u32[]{:S(2)}, u32[]{:S(2)}) %collective-permute-start.4) | collective-permute-done | bytes 12320 | tf_op jit(solution)/shard_map/ppermute | solution.py:54
  49.4 24.3 %all-gather.5.cloned.1.call-done.refs_0_ = bf16[768,2048]{1,0:T(8,128)(2,1)} async-done(((bf16[192,2048]{1,0:T(8,128)(2,1)}), bf16[768,2048]{1,0:T(8,128)(2,1)}) %all-gather.5.cloned.1.call-update) | async-done | bytes 3145744 | tf_op jit(solution)/shard_map/all_gather | solution.py:806
  76.3 27.7 %all-gather.7.cloned.1.call-done.first.second = bf16[256,2048]{1,0:T(8,128)(2,1)} async-done(((bf16[64,2048]{1,0:T(8,128)(2,1)}), bf16[256,2048]{1,0:T(8,128)(2,1)}) %all-gather.7.cloned.1.call-update) | async-done | bytes 1048592 | tf_op jit(solution)/shard_map/all_gather | solution.py:806
  112.0 31.0 %collective-permute-done.10.refs_1_ = bf16[768,2048]{1,0:T(8,128)(2,1)S(1)} collective-permute-done((bf16[768,2048]{1,0:T(8,128)(2,1)}, bf16[768,2048]{1,0:T(8,128)(2,1)S(1)}, u32[]{:S(2)}, u32[]{:S(2)}) %collective-permute-start.10) | collective-permute-done | bytes 3145760 | tf_op jit(solution)/shard_map/ppermute | solution.py:54
  149.5 32.1 %collective-permute-done.14.refs_4_ = bf16[384,2048]{1,0:T(8,128)(2,1)} collective-permute-done((bf16[384,2048]{1,0:T(8,128)(2,1)}, bf16[384,2048]{1,0:T(8,128)(2,1)}, u32[]{:S(2)}, u32[]{:S(2)}) %collective-permute-start.14) | collective-permute-done | bytes 1572896 | tf_op jit(solution)/shard_map/ppermute | solution.py:54
  194.5 10.1 %collective-permute-done.9 = bf16[528,2048]{1,0:T(8,128)(2,1)} collective-permute-done((bf16[528,2048]{1,0:T(8,128)(2,1)}, bf16[528,2048]{1,0:T(8,128)(2,1)}, u32[]{:S(2)}, u32[]{:S(2)}) %collective-permute-start.9) | collective-permute-done | bytes 2162720 | tf_op jit(solution)/shard_map/ppermute | solution.py:784
  218.4 9.9 maximum_select_fusion
  238.6 14.7 %multiply.7.rows_ref.refs_0_ = bf16[1024,3072]{1,0:T(8,128)(2,1)S(1)} custom-call(bf16[1024,2048]{1,0:T(8,128)(2,1)S(1)} %first_norm.1.refs_0_.refs_1_, bf16[3072,2048]{1,0:T(8,128)(2,1)S(1)} %bitcast.104, f32[1,3072]{1,0:T(1,128)S(1)} %reshape.498.refs_2_), custom_call_target="tpu_custom_call" | custom-call | flops 1 | bytes 1 | tf_op jit(solution)/shard_map/multiply/pallas_call | solution.py:415
  264.7 29.3 %attend.1.refs_0_.right = bf16[1024,1024]{1,0:T(8,128)(2,1)S(1)} custom-call(bf16[1024,3072]{1,0:T(8,128)(2,1)S(1)} %multiply.7.rows_ref.refs_0_, bf16[1024,64]{1,0:T(8,128)(2,1)S(1)} %broadcast_in_dim.44.mask_ref.refs_2_), custom_call_target="tpu_custom_call" | custom-call | flops 1 | bytes 1 | tf_op jit(solution)/shard_map/attend/pallas_call | solution.py:545
  341.6 45.5 %collective-permute-done.25 = bf16[512,2048]{1,0:T(8,128)(2,1)} collective-permute-done((bf16[512,2048]{1,0:T(8,128)(2,1)S(1)}, bf16[512,2048]{1,0:T(8,128)(2,1)}, u32[]{:S(2)}, u32[]{:S(2)}) %collective-permute-start.25) | collective-permute-done | bytes 2097184 | tf_op jit(solution)/shard_map/ppermute | solution.py:54
  409.9 12.9 %multiply.9 = (bf16[1024,2048]{1,0:T(8,128)(2,1)S(1)}, bf16[1024,2048]{1,0:T(8,128)(2,1)S(1)}) custom-call(bf16[1024,2048]{1,0:T(8,128)(2,1)S(1)} %copy-done.31, bf16[2048,2048]{1,0:T(8,128)(2,1)S(1)} %arrange.5.refs_1_, f32[1,2048]{1,0:T(1,128)S(1)} %reshape.504.refs_2_), custom_call_target="tpu_custom_call" | custom-call | flops 1 | bytes 1 | tf_op jit(solution)/shard_map/multiply/pallas_call | solution.py:415
  438.0 12.9 %multiply.10 = (bf16[1024,2048]{1,0:T(8,128)(2,1)S(1)}, bf16[1024,2048]{1,0:T(8,128)(2,1)S(1)}) custom-call(bf16[1024,2048]{1,0:T(8,128)(2,1)S(1)} %maximum_select_fusion.2.refs_0_.refs_3_, bf16[2048,2048]{1,0:T(8,128)(2,1)S(1)} %arrange.5.refs_1_, f32[1,2048]{1,0:T(1,128)S(1)} %reshape.504.refs_2_), custom_call_target="tpu_custom_call" | custom-call | flops 1 | bytes 1 | tf_op jit(solution)/shard_map/multiply/pallas_call | solution.py:415
  461.8 22.1 %outer_rows_of.7 = bf16[2048,2048]{1,0:T(8,128)(2,1)S(1)} custom-call(s32[2]{0:T(128)S(1)} %iota.19.table_ref, bf16[1024,2048]{1,0:T(8,128)(2,1)S(1)} %copy-done.56, bf16[1024,2048]{1,0:T(8,128)(2,1)S(1)} %regroup.3.refs_1_.refs_0_, bf16[1024,2048]{1,0:T(8,128)(2,1)S(1)} %copy-done.48, bf16[1024,2048]{1,0:T(8,128)(2,1)S(1)} %get-tuple-element.466.refs_3_.refs_0_), custom_call_target="tpu_custom_call" | custom-call | flops 1 | bytes 1 | tf_op jit(solution)/shard_map/outer_rows_of/pallas_call | solution.py:186
  498.1 11.0 %multiply.11 = (bf16[1024,2048]{1,0:T(8,128)(2,1)S(1)}, f32[1,2048]{1,0:T(1,128)S(1)}) custom-call(bf16[1024,2048]{1,0:T(8,128)(2,1)S(1)} %copy-done.59, bf16[2048,2048]{1,0:T(8,128)(2,1)S(1)} %copy-done.5, bf16[1024,2048]{1,0:T(8,128)(2,1)S(1)} %copy-done.79), custom_call_target="tpu_custom_call" | custom-call | flops 1 | bytes 1 | tf_op jit(solution)/shard_map/multiply/pallas_call | solution.py:415
  528.8 11.0 %multiply.12 = (bf16[1024,2048]{1,0:T(8,128)(2,1)S(1)}, f32[1,2048]{1,0:T(1,128)S(1)}) custom-call(bf16[1024,2048]{1,0:T(8,128)(2,1)S(1)} %copy-done.57, bf16[2048,2048]{1,0:T(8,128)(2,1)S(1)} %copy-done.6, bf16[1024,2048]{1,0:T(8,128)(2,1)S(1)} %copy-done.77), custom_call_target="tpu_custom_call" | custom-call | flops 1 | bytes 1 | tf_op jit(solution)/shard_map/multiply/pallas_call | solution.py:415
  559.4 11.5 %outer_rows_of.8 = bf16[1024,2048]{1,0:T(8,128)(2,1)} custom-call(s32[1]{0:T(128)} %bitcast.41.table_ref, bf16[1024,2048]{1,0:T(8,128)(2,1)S(1)} %copy-done.19, bf16[1024,2048]{1,0:T(8,128)(2,1)S(1)} %copy-done.16, bf16[1024,2048]{1,0:T(8,128)(2,1)S(1)} %copy-done.32, bf16[1024,2048]{1,0:T(8,128)(2,1)S(1)} %copy-done.25), custom_call_target="tpu_custom_call" | custom-call | flops 1 | bytes 1 | tf_op jit(solution)/shard_map/outer_rows_of/pallas_call | solution.py:186
  610.6 12.4 %attend_back.4.refs_0_.refs_3_ = bf16[1024,768]{1,0:T(8,128)(2,1)S(1)} custom-call(s32[1]{0:T(128)} %bitcast.45.place_ref, bf16[1024,3072]{1,0:T(8,128)(2,1)S(1)} %bitcast.108, bf16[1024,1024]{1,0:T(8,128)(2,1)S(1)} %multiply.13.refs_1_, bf16[1024,64]{1,0:T(8,128)(2,1)S(1)} %broadcast_in_dim.44.mask_ref.refs_2_), custom_call_target="tpu_custom_call" | custom-call | flops 1 | bytes 1 | tf_op jit(solution)/shard_map/attend_back/pallas_call | solution.py:567
  633.9 12.8 %attend_back.5.refs_0_.refs_1_ = bf16[1024,768]{1,0:T(8,128)(2,1)S(1)} custom-call(s32[1]{0:T(128)} %bitcast.43.place_ref, bf16[1024,3072]{1,0:T(8,128)(2,1)S(1)} %bitcast.108, bf16[1024,1024]{1,0:T(8,128)(2,1)S(1)} %multiply.13.refs_1_, bf16[1024,64]{1,0:T(8,128)(2,1)S(1)} %broadcast_in_dim.44.mask_ref.refs_2_), custom_call_target="tpu_custom_call" | custom-call | flops 1 | bytes 1 | tf_op jit(solution)/shard_map/attend_back/pallas_call | solution.py:567
  654.5 12.6 %attend_back.6.refs_0_.refs_2_ = bf16[1024,768]{1,0:T(8,128)(2,1)S(1)} custom-call(s32[1]{0:T(128)} %bitcast.44.place_ref, bf16[1024,3072]{1,0:T(8,128)(2,1)S(1)} %bitcast.108, bf16[1024,1024]{1,0:T(8,128)(2,1)S(1)} %multiply.13.refs_1_, bf16[1024,64]{1,0:T(8,128)(2,1)S(1)} %broadcast_in_dim.44.mask_ref.refs_2_), custom_call_target="tpu_custom_call" | custom-call | flops 1 | bytes 1 | tf_op jit(solution)/shard_map/attend_back/pallas_call | solution.py:567
  678.9 10.8 %outer_rows_of.12 = bf16[1024,2048]{1,0:T(8,128)(2,1)S(1)} custom-call(s32[1]{0:T(128)} %bitcast.table_ref, bf16[1024,2048]{1,0:T(8,128)(2,1)S(1)} %copy-done.20, bf16[1024,2048]{1,0:T(8,128)(2,1)S(1)} %copy-done.17, bf16[1024,2048]{1,0:T(8,128)(2,1)S(1)} %copy-done.33, bf16[1024,2048]{1,0:T(8,128)(2,1)S(1)} %copy-done.26), custom_call_target="tpu_custom_call" | custom-call | flops 1 | bytes 1 | tf_op jit(solution)/shard_map/outer_rows_of/pallas_call | solution.py:186
  689.6 12.6 %attend_back.7.refs_0_ = bf16[1024,768]{1,0:T(8,128)(2,1)S(1)} custom-call(s32[1]{0:T(128)} %bitcast.42.place_ref, bf16[1024,3072]{1,0:T(8,128)(2,1)S(1)} %bitcast.108, bf16[1024,1024]{1,0:T(8,128)(2,1)S(1)} %multiply.13.refs_1_, bf16[1024,64]{1,0:T(8,128)(2,1)S(1)} %broadcast_in_dim.44.mask_ref.refs_2_), custom_call_target="tpu_custom_call" | custom-call | flops 1 | bytes 1 | tf_op jit(solution)/shard_map/attend_back/pallas_call | solution.py:567
  814.2 20.6 %collective-permute-done.39 = bf16[512,2048]{1,0:T(8,128)(2,1)} collective-permute-done((bf16[512,2048]{1,0:T(8,128)(2,1)}, bf16[512,2048]{1,0:T(8,128)(2,1)}, u32[]{:S(2)}, u32[]{:S(2)}) %collective-permute-start.39) | collective-permute-done | bytes 2097184 | tf_op jit(solution)/shard_map/ppermute | solution.py:54
  889.7 24.5 %collective-permute-done.51 = bf16[256,2048]{1,0:T(8,128)(2,1)S(1)} collective-permute-done((bf16[256,2048]{1,0:T(8,128)(2,1)S(1)}, bf16[256,2048]{1,0:T(8,128)(2,1)S(1)}, u32[]{:S(2)}, u32[]{:S(2)}) %collective-permute-start.51) | collective-permute-done | bytes 1048608 | tf_op jit(solution)/shard_map/ppermute | solution.py:784
  932.5 55.2 %collective-permute-done.44 = bf16[256,2048]{1,0:T(8,128)(2,1)} collective-permute-done((bf16[256,2048]{1,0:T(8,128)(2,1)}, bf16[256,2048]{1,0:T(8,128)(2,1)}, u32[]{:S(2)}, u32[]{:S(2)}) %collective-permute-start.44) | collective-permute-done | bytes 1048608 | tf_op jit(solution)/shard_map/ppermute | solution.py:784
  (527 shorter events, 510.0 us)
Async XLA Ops:
  7.2 66.5 %all-gather.5.cloned.1.call-start = ((), (), s32[]{:S(2)}) async-start(), calls=%async_computation.4 | async-start | bytes 3932160 | tf_op jit(solution)/shard_map/all_gather | solution.py:806
  11.2 92.8 %all-gather.7.cloned.1.call-start = ((), (), s32[]{:S(2)}) async-start(), calls=%async_computation.5 | async-start | bytes 1310720 | tf_op jit(solution)/shard_map/all_gather | solution.py:806
  73.7 69.3 %collective-permute-start.10 = (bf16[768,2048]{1,0:T(8,128)(2,1)}, bf16[768,2048]{1,0:T(8,128)(2,1)S(1)}, u32[]{:S(2)}, u32[]{:S(2)}) collective-permute-start(bf16[768,2048]{1,0:T(8,128)(2,1)} %all-gather.5.cloned.1.call-done.refs_0_), channel_id=1, source_target_pairs={{0,8},{8,0},{1,9},{9,1},{2,10},{10,2},{3,11},{11,3},{4,12},{12,4},... | collective-permute-start | bytes 9437192 | tf_op jit(solution)/shard_map/ppermute | solution.py:54
  75.0 69.3 %collective-permute-start.11 = (bf16[768,2048]{1,0:T(8,128)(2,1)}, bf16[768,2048]{1,0:T(8,128)(2,1)}, u32[]{:S(2)}, u32[]{:S(2)}) collective-permute-start(bf16[768,2048]{1,0:T(8,128)(2,1)} %all-gather.5.cloned.1.call-done.refs_0_), channel_id=1, source_target_pairs={{0,16},{16,0},{1,17},{17,1},{2,18},{18,2},{3,19},{19,3},{4,20},{20... | collective-permute-start | bytes 9437192 | tf_op jit(solution)/shard_map/ppermute | solution.py:54
  76.2 217.8 %all-gather.9.cloned.1.call-start = ((), (), s32[]{:S(2)}) async-start(), calls=%async_computation.6 | async-start | bytes 5242880 | tf_op jit(solution)/shard_map/all_gather | solution.py:806
  106.7 87.9 %collective-permute-start.8 = (bf16[528,2048]{1,0:T(8,128)(2,1)}, bf16[528,2048]{1,0:T(8,128)(2,1)}, u32[]{:S(2)}, u32[]{:S(2)}) collective-permute-start(bf16[528,2048]{1,0:T(8,128)(2,1)} %get-tuple-element.312), channel_id=1, source_target_pairs={{0,0},{1,1},{2,4},{3,5},{4,2},{5,3},{6,6},{7,7},{8,8},{9,9},{10,12... | collective-permute-start | bytes 6488072 | tf_op jit(solution)/shard_map/ppermute | solution.py:784
  109.2 95.4 %collective-permute-start.9 = (bf16[528,2048]{1,0:T(8,128)(2,1)}, bf16[528,2048]{1,0:T(8,128)(2,1)}, u32[]{:S(2)}, u32[]{:S(2)}) collective-permute-start(bf16[528,2048]{1,0:T(8,128)(2,1)} %get-tuple-element.313), channel_id=1, source_target_pairs={{0,1},{1,0},{2,5},{3,4},{4,3},{5,2},{6,7},{7,6},{8,9},{9,8},{10,13... | collective-permute-start | bytes 6488072 | tf_op jit(solution)/shard_map/ppermute | solution.py:784
  210.8 278.6 %all-gather.11.cloned.1.call-start = ((), (), s32[]{:S(2)}) async-start(), calls=%async_computation.7 | async-start | bytes 10485760 | tf_op jit(solution)/shard_map/all_gather | solution.py:806
  211.2 95.7 %collective-permute-start.21 = (bf16[256,2048]{1,0:T(8,128)(2,1)}, bf16[256,2048]{1,0:T(8,128)(2,1)}, u32[]{:S(2)}, u32[]{:S(2)}) collective-permute-start(bf16[256,2048]{1,0:T(8,128)(2,1)} %constant_dynamic-update-slice_fusion.10), channel_id=1, source_target_pairs={{0,16},{16,0},{1,17},{17,1},{2,18},{18,2},{3,19},{19,3},{4,20},{20... | collective-permute-start | bytes 3145736 | tf_op jit(solution)/shard_map/ppermute | solution.py:54
  213.4 80.6 %collective-permute-start.17 = (bf16[256,2048]{1,0:T(8,128)(2,1)}, bf16[256,2048]{1,0:T(8,128)(2,1)S(1)}, u32[]{:S(2)}, u32[]{:S(2)}) collective-permute-start(bf16[256,2048]{1,0:T(8,128)(2,1)} %constant_dynamic-update-slice_fusion.12.refs_0_), channel_id=1, source_target_pairs={{0,8},{8,0},{1,9},{9,1},{2,10},{10,2},{3,11},{11,3},{4,12},{12,4},... | collective-permute-start | bytes 3145736 | tf_op jit(solution)/shard_map/ppermute | solution.py:54
  311.5 476.5 %reduce-scatter.5.cloned.1.call-start = ((), (), s32[]{:S(2)}) async-start(), calls=%async_computation.8 | async-start | bytes 10485760 | tf_op jit(solution)/shard_map/reduce_scatter | solution.py:996
  313.4 92.0 %collective-permute-start.22 = (bf16[1024,2048]{1,0:T(8,128)(2,1)}, bf16[1024,2048]{1,0:T(8,128)(2,1)}, u32[]{:S(2)}, u32[]{:S(2)}) collective-permute-start(bf16[1024,2048]{1,0:T(8,128)(2,1)} %all-gather.9.cloned.1.call-done.refs_0_), channel_id=1, source_target_pairs={{0,16},{16,0},{1,17},{17,1},{2,18},{18,2},{3,19},{19,3},{4,20},{20... | collective-permute-start | bytes 12582920 | tf_op jit(solution)/shard_map/ppermute | solution.py:54
  340.7 91.4 %collective-permute-start.23 = (bf16[512,2048]{1,0:T(8,128)(2,1)}, bf16[512,2048]{1,0:T(8,128)(2,1)}, u32[]{:S(2)}, u32[]{:S(2)}) collective-permute-start(bf16[512,2048]{1,0:T(8,128)(2,1)} %constant_dynamic-slice_fusion.3), channel_id=1, source_target_pairs={{0,8},{8,0},{1,9},{9,1},{2,10},{10,2},{3,11},{11,3},{4,12},{12,4},... | collective-permute-start | bytes 6291464 | tf_op jit(solution)/shard_map/ppermute | solution.py:54
  489.3 433.9 %reduce-scatter.9.cloned.1.call-start = ((), (), s32[]{:S(2)}) async-start(), calls=%async_computation.10 | async-start | bytes 5242880 | tf_op jit(solution)/shard_map/reduce_scatter | solution.py:996
  609.4 98.3 %collective-permute-start.33 = (bf16[1024,2048]{1,0:T(8,128)(2,1)}, bf16[1024,2048]{1,0:T(8,128)(2,1)}, u32[]{:S(2)}, u32[]{:S(2)}) collective-permute-start(bf16[1024,2048]{1,0:T(8,128)(2,1)} %outer_rows_of.8), channel_id=1, source_target_pairs={{0,16},{16,0},{1,17},{17,1},{2,18},{18,2},{3,19},{19,3},{4,20},{20... | collective-permute-start | bytes 12582920 | tf_op jit(solution)/shard_map/ppermute | solution.py:54
  633.5 68.8 %collective-permute-start.34 = (bf16[768,2048]{1,0:T(8,128)(2,1)}, bf16[768,2048]{1,0:T(8,128)(2,1)}, u32[]{:S(2)}, u32[]{:S(2)}) collective-permute-start(bf16[768,2048]{1,0:T(8,128)(2,1)} %outer_rows_of.9), channel_id=1, source_target_pairs={{0,8},{8,0},{1,9},{9,1},{2,10},{10,2},{3,11},{11,3},{4,12},{12,4},... | collective-permute-start | bytes 9437192 | tf_op jit(solution)/shard_map/ppermute | solution.py:54
  713.8 212.2 %reduce-scatter.7.cloned.1.call-start = ((), (), s32[]{:S(2)}) async-start(), calls=%async_computation.9 | async-start | bytes 3932160 | tf_op jit(solution)/shard_map/reduce_scatter | solution.py:996
  713.9 76.4 %collective-permute-start.36 = (bf16[768,2048]{1,0:T(8,128)(2,1)}, bf16[768,2048]{1,0:T(8,128)(2,1)}, u32[]{:S(2)}, u32[]{:S(2)}) collective-permute-start(bf16[768,2048]{1,0:T(8,128)(2,1)} %copy-done.80), channel_id=1, source_target_pairs={{0,8},{8,0},{1,9},{9,1},{2,10},{10,2},{3,11},{11,3},{4,12},{12,4},... | collective-permute-start | bytes 9437192 | tf_op jit(solution)/shard_map/ppermute | solution.py:54
  715.0 75.3 %collective-permute-start.37 = (bf16[768,2048]{1,0:T(8,128)(2,1)}, bf16[768,2048]{1,0:T(8,128)(2,1)}, u32[]{:S(2)}, u32[]{:S(2)}) collective-permute-start(bf16[768,2048]{1,0:T(8,128)(2,1)} %add_convert_fusion.2), channel_id=1, source_target_pairs={{0,16},{16,0},{1,17},{17,1},{2,18},{18,2},{3,19},{19,3},{4,20},{20... | collective-permute-start | bytes 9437192 | tf_op jit(solution)/shard_map/ppermute | solution.py:54
  811.2 182.8 %reduce-scatter.11.cloned.1.call-start = ((), (), s32[]{:S(2)}) async-start(), calls=%async_computation.11 | async-start | bytes 1638400 | tf_op jit(solution)/shard_map/reduce_scatter | solution.py:996
  863.4 50.8 %collective-permute-start.50 = (bf16[256,2048]{1,0:T(8,128)(2,1)S(1)}, bf16[256,2048]{1,0:T(8,128)(2,1)S(1)}, u32[]{:S(2)}, u32[]{:S(2)}) collective-permute-start(bf16[256,2048]{1,0:T(8,128)(2,1)S(1)} %copy-done.98), channel_id=1, source_target_pairs={{0,0},{1,1},{4,2},{5,3},{2,4},{3,5},{6,6},{7,7},{8,8},{9,9},{12,10... | collective-permute-start | bytes 3145736 | tf_op jit(solution)/shard_map/ppermute | solution.py:784
  917.6 70.2 %collective-permute-start.43 = (bf16[256,2048]{1,0:T(8,128)(2,1)}, bf16[256,2048]{1,0:T(8,128)(2,1)S(1)}, u32[]{:S(2)}, u32[]{:S(2)}) collective-permute-start(bf16[256,2048]{1,0:T(8,128)(2,1)} %get-tuple-element.559), channel_id=1, source_target_pairs={{0,0},{1,1},{4,2},{5,3},{2,4},{3,5},{6,6},{7,7},{8,8},{9,9},{12,10... | collective-permute-start | bytes 3145736 | tf_op jit(solution)/shard_map/ppermute | solution.py:784
  919.5 68.3 %collective-permute-start.44 = (bf16[256,2048]{1,0:T(8,128)(2,1)}, bf16[256,2048]{1,0:T(8,128)(2,1)}, u32[]{:S(2)}, u32[]{:S(2)}) collective-permute-start(bf16[256,2048]{1,0:T(8,128)(2,1)} %get-tuple-element.558), channel_id=1, source_target_pairs={{1,0},{0,1},{5,2},{4,3},{3,4},{2,5},{7,6},{6,7},{9,8},{8,9},{13,10... | collective-permute-start | bytes 3145736 | tf_op jit(solution)/shard_map/ppermute | solution.py:784
  932.4 59.7 %collective-permute-start.53 = (bf16[64,4096]{1,0:T(8,128)(2,1)S(1)}, bf16[64,4096]{1,0:T(8,128)(2,1)S(1)}, u32[]{:S(2)}, u32[]{:S(2)}) collective-permute-start(bf16[64,4096]{1,0:T(8,128)(2,1)S(1)} %slice.241), channel_id=1, source_target_pairs={{0,4},{4,0},{1,5},{5,1},{2,6},{6,2},{3,7},{7,3},{8,12},{12,8},{9,1... | collective-permute-start | bytes 1572872 | tf_op jit(solution)/shard_map/ppermute | solution.py:54
  (147 other events, 1487.6 us)
Sparse Core Ops, SparseCore 0:
  11.3 62.3 all-gather.4
  76.3 27.6 all-gather.6
  210.9 77.2 all-gather.8
  311.6 146.3 all-gather.10
  489.4 142.4 reduce-scatter.4
  713.9 77.1 reduce-scatter.8
  811.3 58.7 reduce-scatter.6
  917.7 56.4 reduce-scatter.10

commit v6 on v5

--- a/solution.py
+++ b/solution.py
@@ -1143,6 +1143,9 @@
     def beside_own(peer, rows, flags, bias):
         return half_rows(rows, core) + half_rows(flags, core) * (peer.astype(f32) + bias)
 
+    theirs = line(lambda rows, weight: their_half(rows, weight, True), activated, w_shrink)
+    shrunk_got = swap(theirs, CORE)
+    mine = line(lambda rows, weight: my_half(rows, weight, True), activated, w_shrink)
     rest = line(beside_own, from_peer, middle, active, bias_shrink)
 
     def column_sum(matrix):
@@ -1186,18 +1189,10 @@
     sums = line(
         all_sums, first_totals, middle_totals, grad_shrunk, own_sums, peer_sums, *grads_qkv
     )
-    theirs = line(lambda rows, weight: their_half(rows, weight, True), activated, w_shrink)
-    shrunk_got = swap(theirs, CORE)
     sums = line(fold, sums, swap(sums[dp_size // 2 :], ALONG_Y))
-    mine = line(lambda rows, weight: my_half(rows, weight, True), activated, w_shrink)
     sums = line(fold, sums, swap(sums[dp_size // 4 :], ALONG_X))
     shrunk = line(lambda *parts: regroup_back(bits, *parts, seq_size, f32), mine, shrunk_got)
 
-    def finish(part, other, flags):
-        out = other + half_rows(flags, core) * part
-        return by_parity(out.astype(low).reshape(2, local_len, width))
-
-    out_halves = send(*line(finish, shrunk, rest, active), True)
     sums = line(fold, sums, swap(sums[dp_size // 8 :], CORE))
     out_sum = line(
         lambda *parts: sum(part.astype(f32) for part in parts).astype(low),
@@ -1206,7 +1201,6 @@
         out_got_y,
     )
     out_got = swap(line(lambda rows: rows[:, width // 2 :], out_sum), CORE)
-    tokens_grad = line(paired, *tokens_parts)
     out_rows = line(
         lambda rows, got: weave_columns(core, rows[:, : width // 2], got, depth_rows),
         out_sum,
@@ -1221,6 +1215,12 @@
 
     out_rows = scatter_z(line(with_vectors, sums, out_rows))
 
+    def finish(part, other, flags):
+        out = other + half_rows(flags, core) * part
+        return by_parity(out.astype(low).reshape(2, local_len, width))
+
+    out_halves = send(*line(finish, shrunk, rest, active), True)
+    tokens_grad = line(paired, *tokens_parts)
     shrink_rows = line(lambda rows, got: add_rounded(rows[:half], got), shrink_rows, shrink_got)
     half = half // 2
     shrink_got = swap(line(lambda rows: rows[half:], shrink_rows), ALONG_X)

time: 1010 us -> 1010 us (level)
  waiting for transfers between devices: 337 us -> 323 us
    ppermute x45, waiting for transfers between devices: 195 us -> 177 us  [swap(): return lax.ppermute(values, axis, [(0, 1), (1, 0)])]
    unnamed x230 -> x224, local copies, waits for them, and re-layouts: 135 us -> 127 us
  transfers between devices with their start and end apart: 62 -> 62, of which waited for: 24 -> 24; matrix products, arithmetic and copies ran while one was open for 11% -> 12% of each run, Pallas kernels for 34% -> 35%
where the time goes in v6:
time: 1010 us; the launch traced here: 999 us
  Pallas kernels  347 us (34%)
  waiting for transfers between devices  323 us (32%)
  local copies, waits for them, and re-layouts  160 us (16%)
  other arithmetic  93.3 us (9%)
  starting transfers between devices  59.6 us (6%)
  between operations  16.1 us (2%)
    ppermute x45, waiting for transfers between devices, swap(): return lax.ppermute(values, axis, [(0, 1), (1, 0)])  177 us
    unnamed x224, local copies, waits for them, and re-layouts  127 us
    ppermute x3, waiting for transfers between devices, send(): lax.ppermute(second, DEVICES, routes[1])  93.9 us
    pallas_call x7, Pallas kernels, multiply(): pl.pallas_call(kernel, grid=(columns // tile,), in_specs=[pl.BlockSpec(le...  73.8 us
    pallas_call x10, Pallas kernels, half_dot(): pl.pallas_call(kernel, grid_spec=pltpu.PrefetchScalarGridSpec(num_scalar_...  64.9 us
    pallas_call x7, Pallas kernels, outer_rows_of(): pl.pallas_call(kernel, grid_spec=pltpu.PrefetchScalarGridSpec(num_scalar_...  64 us
    all_gather x4, waiting for transfers between devices, through_z(): return lax.all_gather(shard, 'seq', axis=0, tiled=True)  52.1 us
    pallas_call x4, Pallas kernels, attend_back(): pl.pallas_call(kernel, grid_spec=pltpu.PrefetchScalarGridSpec(num_scalar_...  50.4 us
  transfers between devices with their start and end apart: 62, of which 24 were waited for; matrix products, arithmetic and copies ran while one was open for 12% of the time, Pallas kernels for 35%

profile of v6, /device:TPU:9, one launch (start us, length us, event | category | flops | bytes accessed | tf_op | source)
XLA Modules:
  0.0 998.5 jit_solution(10478203045600898861)
XLA Ops:
  33.8 11.0 %collective-permute-done.4 = bf16[2,4,768]{2,1,0:T(4,128)(2,1)S(1)} collective-permute-done((bf16[2,4,768]{2,1,0:T(4,128)(2,1)S(1)}, bf16[2,4,768]{2,1,0:T(4,128)(2,1)S(1)}, u32[]{:S(2)}, u32[]{:S(2)}) %collective-permute-start.4) | collective-permute-done | bytes 12320 | tf_op jit(solution)/shard_map/ppermute | solution.py:54
  49.4 24.3 %all-gather.5.cloned.1.call-done.refs_0_ = bf16[768,2048]{1,0:T(8,128)(2,1)} async-done(((bf16[192,2048]{1,0:T(8,128)(2,1)}), bf16[768,2048]{1,0:T(8,128)(2,1)}) %all-gather.5.cloned.1.call-update) | async-done | bytes 3145744 | tf_op jit(solution)/shard_map/all_gather | solution.py:806
  76.3 27.7 %all-gather.7.cloned.1.call-done.first.second = bf16[256,2048]{1,0:T(8,128)(2,1)} async-done(((bf16[64,2048]{1,0:T(8,128)(2,1)}), bf16[256,2048]{1,0:T(8,128)(2,1)}) %all-gather.7.cloned.1.call-update) | async-done | bytes 1048592 | tf_op jit(solution)/shard_map/all_gather | solution.py:806
  112.0 31.0 %collective-permute-done.10.refs_1_ = bf16[768,2048]{1,0:T(8,128)(2,1)S(1)} collective-permute-done((bf16[768,2048]{1,0:T(8,128)(2,1)}, bf16[768,2048]{1,0:T(8,128)(2,1)S(1)}, u32[]{:S(2)}, u32[]{:S(2)}) %collective-permute-start.10) | collective-permute-done | bytes 3145760 | tf_op jit(solution)/shard_map/ppermute | solution.py:54
  149.5 32.1 %collective-permute-done.14.refs_4_ = bf16[384,2048]{1,0:T(8,128)(2,1)} collective-permute-done((bf16[384,2048]{1,0:T(8,128)(2,1)}, bf16[384,2048]{1,0:T(8,128)(2,1)}, u32[]{:S(2)}, u32[]{:S(2)}) %collective-permute-start.14) | collective-permute-done | bytes 1572896 | tf_op jit(solution)/shard_map/ppermute | solution.py:54
  194.5 10.1 %collective-permute-done.9 = bf16[528,2048]{1,0:T(8,128)(2,1)} collective-permute-done((bf16[528,2048]{1,0:T(8,128)(2,1)}, bf16[528,2048]{1,0:T(8,128)(2,1)}, u32[]{:S(2)}, u32[]{:S(2)}) %collective-permute-start.9) | collective-permute-done | bytes 2162720 | tf_op jit(solution)/shard_map/ppermute | solution.py:784
  218.4 9.9 maximum_select_fusion
  238.6 14.7 %multiply.7.rows_ref.refs_0_ = bf16[1024,3072]{1,0:T(8,128)(2,1)S(1)} custom-call(bf16[1024,2048]{1,0:T(8,128)(2,1)S(1)} %first_norm.1.refs_0_.refs_1_, bf16[3072,2048]{1,0:T(8,128)(2,1)S(1)} %bitcast.104, f32[1,3072]{1,0:T(1,128)S(1)} %reshape.498.refs_2_), custom_call_target="tpu_custom_call" | custom-call | flops 1 | bytes 1 | tf_op jit(solution)/shard_map/multiply/pallas_call | solution.py:415
  264.7 29.3 %attend.1.refs_0_.right = bf16[1024,1024]{1,0:T(8,128)(2,1)S(1)} custom-call(bf16[1024,3072]{1,0:T(8,128)(2,1)S(1)} %multiply.7.rows_ref.refs_0_, bf16[1024,64]{1,0:T(8,128)(2,1)S(1)} %broadcast_in_dim.44.mask_ref.refs_2_), custom_call_target="tpu_custom_call" | custom-call | flops 1 | bytes 1 | tf_op jit(solution)/shard_map/attend/pallas_call | solution.py:545
  341.6 45.5 %collective-permute-done.25 = bf16[512,2048]{1,0:T(8,128)(2,1)} collective-permute-done((bf16[512,2048]{1,0:T(8,128)(2,1)S(1)}, bf16[512,2048]{1,0:T(8,128)(2,1)}, u32[]{:S(2)}, u32[]{:S(2)}) %collective-permute-start.25) | collective-permute-done | bytes 2097184 | tf_op jit(solution)/shard_map/ppermute | solution.py:54
  395.7 9.7 collective-permute-done.22.refs_1_
  409.9 12.9 %multiply.9 = (bf16[1024,2048]{1,0:T(8,128)(2,1)S(1)}, bf16[1024,2048]{1,0:T(8,128)(2,1)S(1)}) custom-call(bf16[1024,2048]{1,0:T(8,128)(2,1)S(1)} %copy-done.30, bf16[2048,2048]{1,0:T(8,128)(2,1)S(1)} %arrange.5.refs_1_, f32[1,2048]{1,0:T(1,128)S(1)} %reshape.504.refs_2_), custom_call_target="tpu_custom_call" | custom-call | flops 1 | bytes 1 | tf_op jit(solution)/shard_map/multiply/pallas_call | solution.py:415
  437.9 12.9 %multiply.10 = (bf16[1024,2048]{1,0:T(8,128)(2,1)S(1)}, bf16[1024,2048]{1,0:T(8,128)(2,1)S(1)}) custom-call(bf16[1024,2048]{1,0:T(8,128)(2,1)S(1)} %maximum_select_fusion.2.refs_0_.refs_3_, bf16[2048,2048]{1,0:T(8,128)(2,1)S(1)} %arrange.5.refs_1_, f32[1,2048]{1,0:T(1,128)S(1)} %reshape.504.refs_2_), custom_call_target="tpu_custom_call" | custom-call | flops 1 | bytes 1 | tf_op jit(solution)/shard_map/multiply/pallas_call | solution.py:415
  459.6 22.1 %outer_rows_of.7 = bf16[2048,2048]{1,0:T(8,128)(2,1)S(1)} custom-call(s32[2]{0:T(128)S(1)} %iota.19.table_ref, bf16[1024,2048]{1,0:T(8,128)(2,1)S(1)} %copy-done.50, bf16[1024,2048]{1,0:T(8,128)(2,1)S(1)} %regroup.3.refs_1_.refs_0_, bf16[1024,2048]{1,0:T(8,128)(2,1)S(1)} %get-tuple-element.487.refs_2_.refs_0_, ...), custom_call_target="tpu_custom_call" | custom-call | flops 1 | bytes 1 | tf_op jit(solution)/shard_map/outer_rows_of/pallas_call | solution.py:186
  495.8 11.0 %multiply.11 = (bf16[1024,2048]{1,0:T(8,128)(2,1)S(1)}, f32[1,2048]{1,0:T(1,128)S(1)}) custom-call(bf16[1024,2048]{1,0:T(8,128)(2,1)S(1)} %copy-done.53, bf16[2048,2048]{1,0:T(8,128)(2,1)S(1)} %copy-done.5, bf16[1024,2048]{1,0:T(8,128)(2,1)S(1)} %copy-done.76), custom_call_target="tpu_custom_call" | custom-call | flops 1 | bytes 1 | tf_op jit(solution)/shard_map/multiply/pallas_call | solution.py:415
  526.5 11.0 %multiply.12 = (bf16[1024,2048]{1,0:T(8,128)(2,1)S(1)}, f32[1,2048]{1,0:T(1,128)S(1)}) custom-call(bf16[1024,2048]{1,0:T(8,128)(2,1)S(1)} %copy-done.51, bf16[2048,2048]{1,0:T(8,128)(2,1)S(1)} %copy-done.6, bf16[1024,2048]{1,0:T(8,128)(2,1)S(1)} %copy-done.74), custom_call_target="tpu_custom_call" | custom-call | flops 1 | bytes 1 | tf_op jit(solution)/shard_map/multiply/pallas_call | solution.py:415
  557.0 11.5 %outer_rows_of.8 = bf16[1024,2048]{1,0:T(8,128)(2,1)} custom-call(s32[1]{0:T(128)} %bitcast.41.table_ref, bf16[1024,2048]{1,0:T(8,128)(2,1)S(1)} %copy-done.19, bf16[1024,2048]{1,0:T(8,128)(2,1)S(1)} %copy-done.16, bf16[1024,2048]{1,0:T(8,128)(2,1)S(1)} %copy-done.31, bf16[1024,2048]{1,0:T(8,128)(2,1)S(1)} %copy-done.25), custom_call_target="tpu_custom_call" | custom-call | flops 1 | bytes 1 | tf_op jit(solution)/shard_map/outer_rows_of/pallas_call | solution.py:186
  608.4 12.4 %attend_back.4.refs_0_.refs_3_ = bf16[1024,768]{1,0:T(8,128)(2,1)S(1)} custom-call(s32[1]{0:T(128)} %bitcast.45.place_ref, bf16[1024,3072]{1,0:T(8,128)(2,1)S(1)} %bitcast.108, bf16[1024,1024]{1,0:T(8,128)(2,1)S(1)} %multiply.13.refs_1_, bf16[1024,64]{1,0:T(8,128)(2,1)S(1)} %broadcast_in_dim.44.mask_ref.refs_2_), custom_call_target="tpu_custom_call" | custom-call | flops 1 | bytes 1 | tf_op jit(solution)/shard_map/attend_back/pallas_call | solution.py:567
  631.6 12.8 %attend_back.5.refs_0_.refs_1_ = bf16[1024,768]{1,0:T(8,128)(2,1)S(1)} custom-call(s32[1]{0:T(128)} %bitcast.43.place_ref, bf16[1024,3072]{1,0:T(8,128)(2,1)S(1)} %bitcast.108, bf16[1024,1024]{1,0:T(8,128)(2,1)S(1)} %multiply.13.refs_1_, bf16[1024,64]{1,0:T(8,128)(2,1)S(1)} %broadcast_in_dim.44.mask_ref.refs_2_), custom_call_target="tpu_custom_call" | custom-call | flops 1 | bytes 1 | tf_op jit(solution)/shard_map/attend_back/pallas_call | solution.py:567
  652.1 12.6 %attend_back.6.refs_0_.refs_2_ = bf16[1024,768]{1,0:T(8,128)(2,1)S(1)} custom-call(s32[1]{0:T(128)} %bitcast.44.place_ref, bf16[1024,3072]{1,0:T(8,128)(2,1)S(1)} %bitcast.108, bf16[1024,1024]{1,0:T(8,128)(2,1)S(1)} %multiply.13.refs_1_, bf16[1024,64]{1,0:T(8,128)(2,1)S(1)} %broadcast_in_dim.44.mask_ref.refs_2_), custom_call_target="tpu_custom_call" | custom-call | flops 1 | bytes 1 | tf_op jit(solution)/shard_map/attend_back/pallas_call | solution.py:567
  674.3 10.8 %outer_rows_of.12 = bf16[1024,2048]{1,0:T(8,128)(2,1)S(1)} custom-call(s32[1]{0:T(128)} %bitcast.table_ref, bf16[1024,2048]{1,0:T(8,128)(2,1)S(1)} %copy-done.20, bf16[1024,2048]{1,0:T(8,128)(2,1)S(1)} %copy-done.17, bf16[1024,2048]{1,0:T(8,128)(2,1)S(1)} %copy-done.32, bf16[1024,2048]{1,0:T(8,128)(2,1)S(1)} %copy-done.26), custom_call_target="tpu_custom_call" | custom-call | flops 1 | bytes 1 | tf_op jit(solution)/shard_map/outer_rows_of/pallas_call | solution.py:186
  685.1 12.6 %attend_back.7.refs_0_ = bf16[1024,768]{1,0:T(8,128)(2,1)S(1)} custom-call(s32[1]{0:T(128)} %bitcast.42.place_ref, bf16[1024,3072]{1,0:T(8,128)(2,1)S(1)} %bitcast.108, bf16[1024,1024]{1,0:T(8,128)(2,1)S(1)} %multiply.13.refs_1_, bf16[1024,64]{1,0:T(8,128)(2,1)S(1)} %broadcast_in_dim.44.mask_ref.refs_2_), custom_call_target="tpu_custom_call" | custom-call | flops 1 | bytes 1 | tf_op jit(solution)/shard_map/attend_back/pallas_call | solution.py:567
  881.4 58.3 %collective-permute-done.51 = bf16[256,2048]{1,0:T(8,128)(2,1)} collective-permute-done((bf16[256,2048]{1,0:T(8,128)(2,1)S(1)}, bf16[256,2048]{1,0:T(8,128)(2,1)}, u32[]{:S(2)}, u32[]{:S(2)}) %collective-permute-start.51) | collective-permute-done | bytes 1048608 | tf_op jit(solution)/shard_map/ppermute | solution.py:784
  955.3 25.5 %collective-permute-done.48 = bf16[256,2048]{1,0:T(8,128)(2,1)} collective-permute-done((bf16[256,2048]{1,0:T(8,128)(2,1)}, bf16[256,2048]{1,0:T(8,128)(2,1)}, u32[]{:S(2)}, u32[]{:S(2)}) %collective-permute-start.48) | collective-permute-done | bytes 1048608 | tf_op jit(solution)/shard_map/ppermute | solution.py:784
  (521 shorter events, 510.6 us)
Async XLA Ops:
  11.2 92.8 %all-gather.7.cloned.1.call-start = ((), (), s32[]{:S(2)}) async-start(), calls=%async_computation.5 | async-start | bytes 1310720 | tf_op jit(solution)/shard_map/all_gather | solution.py:806
  73.7 69.3 %collective-permute-start.10 = (bf16[768,2048]{1,0:T(8,128)(2,1)}, bf16[768,2048]{1,0:T(8,128)(2,1)S(1)}, u32[]{:S(2)}, u32[]{:S(2)}) collective-permute-start(bf16[768,2048]{1,0:T(8,128)(2,1)} %all-gather.5.cloned.1.call-done.refs_0_), channel_id=1, source_target_pairs={{0,8},{8,0},{1,9},{9,1},{2,10},{10,2},{3,11},{11,3},{4,12},{12,4},... | collective-permute-start | bytes 9437192 | tf_op jit(solution)/shard_map/ppermute | solution.py:54
  75.0 69.3 %collective-permute-start.11 = (bf16[768,2048]{1,0:T(8,128)(2,1)}, bf16[768,2048]{1,0:T(8,128)(2,1)}, u32[]{:S(2)}, u32[]{:S(2)}) collective-permute-start(bf16[768,2048]{1,0:T(8,128)(2,1)} %all-gather.5.cloned.1.call-done.refs_0_), channel_id=1, source_target_pairs={{0,16},{16,0},{1,17},{17,1},{2,18},{18,2},{3,19},{19,3},{4,20},{20... | collective-permute-start | bytes 9437192 | tf_op jit(solution)/shard_map/ppermute | solution.py:54
  76.2 217.8 %all-gather.9.cloned.1.call-start = ((), (), s32[]{:S(2)}) async-start(), calls=%async_computation.6 | async-start | bytes 5242880 | tf_op jit(solution)/shard_map/all_gather | solution.py:806
  106.7 87.9 %collective-permute-start.8 = (bf16[528,2048]{1,0:T(8,128)(2,1)}, bf16[528,2048]{1,0:T(8,128)(2,1)}, u32[]{:S(2)}, u32[]{:S(2)}) collective-permute-start(bf16[528,2048]{1,0:T(8,128)(2,1)} %get-tuple-element.312), channel_id=1, source_target_pairs={{0,0},{1,1},{2,4},{3,5},{4,2},{5,3},{6,6},{7,7},{8,8},{9,9},{10,12... | collective-permute-start | bytes 6488072 | tf_op jit(solution)/shard_map/ppermute | solution.py:784
  109.2 95.4 %collective-permute-start.9 = (bf16[528,2048]{1,0:T(8,128)(2,1)}, bf16[528,2048]{1,0:T(8,128)(2,1)}, u32[]{:S(2)}, u32[]{:S(2)}) collective-permute-start(bf16[528,2048]{1,0:T(8,128)(2,1)} %get-tuple-element.313), channel_id=1, source_target_pairs={{0,1},{1,0},{2,5},{3,4},{4,3},{5,2},{6,7},{7,6},{8,9},{9,8},{10,13... | collective-permute-start | bytes 6488072 | tf_op jit(solution)/shard_map/ppermute | solution.py:784
  210.8 276.3 %all-gather.11.cloned.1.call-start = ((), (), s32[]{:S(2)}) async-start(), calls=%async_computation.7 | async-start | bytes 10485760 | tf_op jit(solution)/shard_map/all_gather | solution.py:806
  211.2 95.7 %collective-permute-start.21 = (bf16[256,2048]{1,0:T(8,128)(2,1)}, bf16[256,2048]{1,0:T(8,128)(2,1)}, u32[]{:S(2)}, u32[]{:S(2)}) collective-permute-start(bf16[256,2048]{1,0:T(8,128)(2,1)} %constant_dynamic-update-slice_fusion.10), channel_id=1, source_target_pairs={{0,16},{16,0},{1,17},{17,1},{2,18},{18,2},{3,19},{19,3},{4,20},{20... | collective-permute-start | bytes 3145736 | tf_op jit(solution)/shard_map/ppermute | solution.py:54
  213.4 80.7 %collective-permute-start.17 = (bf16[256,2048]{1,0:T(8,128)(2,1)}, bf16[256,2048]{1,0:T(8,128)(2,1)S(1)}, u32[]{:S(2)}, u32[]{:S(2)}) collective-permute-start(bf16[256,2048]{1,0:T(8,128)(2,1)} %constant_dynamic-update-slice_fusion.12.refs_0_), channel_id=1, source_target_pairs={{0,8},{8,0},{1,9},{9,1},{2,10},{10,2},{3,11},{11,3},{4,12},{12,4},... | collective-permute-start | bytes 3145736 | tf_op jit(solution)/shard_map/ppermute | solution.py:54
  311.5 472.7 %reduce-scatter.5.cloned.1.call-start = ((), (), s32[]{:S(2)}) async-start(), calls=%async_computation.8 | async-start | bytes 10485760 | tf_op jit(solution)/shard_map/reduce_scatter | solution.py:996
  313.4 92.0 %collective-permute-start.22 = (bf16[1024,2048]{1,0:T(8,128)(2,1)}, bf16[1024,2048]{1,0:T(8,128)(2,1)}, u32[]{:S(2)}, u32[]{:S(2)}) collective-permute-start(bf16[1024,2048]{1,0:T(8,128)(2,1)} %all-gather.9.cloned.1.call-done.refs_0_), channel_id=1, source_target_pairs={{0,16},{16,0},{1,17},{17,1},{2,18},{18,2},{3,19},{19,3},{4,20},{20... | collective-permute-start | bytes 12582920 | tf_op jit(solution)/shard_map/ppermute | solution.py:54
  340.7 91.4 %collective-permute-start.23 = (bf16[512,2048]{1,0:T(8,128)(2,1)}, bf16[512,2048]{1,0:T(8,128)(2,1)}, u32[]{:S(2)}, u32[]{:S(2)}) collective-permute-start(bf16[512,2048]{1,0:T(8,128)(2,1)} %constant_dynamic-slice_fusion.3), channel_id=1, source_target_pairs={{0,8},{8,0},{1,9},{9,1},{2,10},{10,2},{3,11},{11,3},{4,12},{12,4},... | collective-permute-start | bytes 6291464 | tf_op jit(solution)/shard_map/ppermute | solution.py:54
  487.0 459.8 %reduce-scatter.9.cloned.1.call-start = ((), (), s32[]{:S(2)}) async-start(), calls=%async_computation.10 | async-start | bytes 5242880 | tf_op jit(solution)/shard_map/reduce_scatter | solution.py:996
  607.2 97.7 %collective-permute-start.33 = (bf16[1024,2048]{1,0:T(8,128)(2,1)}, bf16[1024,2048]{1,0:T(8,128)(2,1)}, u32[]{:S(2)}, u32[]{:S(2)}) collective-permute-start(bf16[1024,2048]{1,0:T(8,128)(2,1)} %outer_rows_of.8), channel_id=1, source_target_pairs={{0,16},{16,0},{1,17},{17,1},{2,18},{18,2},{3,19},{19,3},{4,20},{20... | collective-permute-start | bytes 12582920 | tf_op jit(solution)/shard_map/ppermute | solution.py:54
  631.2 68.8 %collective-permute-start.34 = (bf16[768,2048]{1,0:T(8,128)(2,1)}, bf16[768,2048]{1,0:T(8,128)(2,1)}, u32[]{:S(2)}, u32[]{:S(2)}) collective-permute-start(bf16[768,2048]{1,0:T(8,128)(2,1)} %outer_rows_of.9), channel_id=1, source_target_pairs={{0,8},{8,0},{1,9},{9,1},{2,10},{10,2},{3,11},{11,3},{4,12},{12,4},... | collective-permute-start | bytes 9437192 | tf_op jit(solution)/shard_map/ppermute | solution.py:54
  711.0 238.6 %reduce-scatter.7.cloned.1.call-start = ((), (), s32[]{:S(2)}) async-start(), calls=%async_computation.9 | async-start | bytes 3932160 | tf_op jit(solution)/shard_map/reduce_scatter | solution.py:996
  711.0 75.6 %collective-permute-start.36 = (bf16[768,2048]{1,0:T(8,128)(2,1)}, bf16[768,2048]{1,0:T(8,128)(2,1)}, u32[]{:S(2)}, u32[]{:S(2)}) collective-permute-start(bf16[768,2048]{1,0:T(8,128)(2,1)} %copy-done.77), channel_id=1, source_target_pairs={{0,8},{8,0},{1,9},{9,1},{2,10},{10,2},{3,11},{11,3},{4,12},{12,4},... | collective-permute-start | bytes 9437192 | tf_op jit(solution)/shard_map/ppermute | solution.py:54
  711.5 75.1 %collective-permute-start.37 = (bf16[768,2048]{1,0:T(8,128)(2,1)}, bf16[768,2048]{1,0:T(8,128)(2,1)}, u32[]{:S(2)}, u32[]{:S(2)}) collective-permute-start(bf16[768,2048]{1,0:T(8,128)(2,1)} %add_convert_fusion.2), channel_id=1, source_target_pairs={{0,16},{16,0},{1,17},{17,1},{2,18},{18,2},{3,19},{19,3},{4,20},{20... | collective-permute-start | bytes 9437192 | tf_op jit(solution)/shard_map/ppermute | solution.py:54
  794.6 193.2 %reduce-scatter.11.cloned.1.call-start = ((), (), s32[]{:S(2)}) async-start(), calls=%async_computation.11 | async-start | bytes 1638400 | tf_op jit(solution)/shard_map/reduce_scatter | solution.py:996
  795.0 66.5 %collective-permute-start.44 = (bf16[256,2048]{1,0:T(8,128)(2,1)}, bf16[256,2048]{1,0:T(8,128)(2,1)}, u32[]{:S(2)}, u32[]{:S(2)}) collective-permute-start(bf16[256,2048]{1,0:T(8,128)(2,1)} %copy-done.89), channel_id=1, source_target_pairs={{0,8},{8,0},{1,9},{9,1},{2,10},{10,2},{3,11},{11,3},{4,12},{12,4},... | collective-permute-start | bytes 3145736 | tf_op jit(solution)/shard_map/ppermute | solution.py:54
  865.4 78.2 %collective-permute-start.49 = (bf16[256,2048]{1,0:T(8,128)(2,1)}, bf16[256,2048]{1,0:T(8,128)(2,1)S(1)}, u32[]{:S(2)}, u32[]{:S(2)}) collective-permute-start(bf16[256,2048]{1,0:T(8,128)(2,1)} %slice.217), channel_id=1, source_target_pairs={{0,16},{16,0},{1,17},{17,1},{2,18},{18,2},{3,19},{19,3},{4,20},{20... | collective-permute-start | bytes 3145736 | tf_op jit(solution)/shard_map/ppermute | solution.py:54
  865.4 74.2 %collective-permute-start.50 = (bf16[256,2048]{1,0:T(8,128)(2,1)S(1)}, bf16[256,2048]{1,0:T(8,128)(2,1)}, u32[]{:S(2)}, u32[]{:S(2)}) collective-permute-start(bf16[256,2048]{1,0:T(8,128)(2,1)S(1)} %copy-done.94), channel_id=1, source_target_pairs={{0,0},{1,1},{4,2},{5,3},{2,4},{3,5},{6,6},{7,7},{8,8},{9,9},{12,10... | collective-permute-start | bytes 3145736 | tf_op jit(solution)/shard_map/ppermute | solution.py:784
  867.6 72.1 %collective-permute-start.51 = (bf16[256,2048]{1,0:T(8,128)(2,1)S(1)}, bf16[256,2048]{1,0:T(8,128)(2,1)}, u32[]{:S(2)}, u32[]{:S(2)}) collective-permute-start(bf16[256,2048]{1,0:T(8,128)(2,1)S(1)} %copy-done.95), channel_id=1, source_target_pairs={{1,0},{0,1},{5,2},{4,3},{3,4},{2,5},{7,6},{6,7},{9,8},{8,9},{13,10... | collective-permute-start | bytes 3145736 | tf_op jit(solution)/shard_map/ppermute | solution.py:784
  875.9 104.9 %collective-permute-start.47 = (bf16[256,2048]{1,0:T(8,128)(2,1)}, bf16[256,2048]{1,0:T(8,128)(2,1)}, u32[]{:S(2)}, u32[]{:S(2)}) collective-permute-start(bf16[256,2048]{1,0:T(8,128)(2,1)} %get-tuple-element.559), channel_id=1, source_target_pairs={{0,0},{1,1},{4,2},{5,3},{2,4},{3,5},{6,6},{7,7},{8,8},{9,9},{12,10... | collective-permute-start | bytes 3145736 | tf_op jit(solution)/shard_map/ppermute | solution.py:784
  (144 other events, 1664.2 us)
Sparse Core Ops, SparseCore 0:
  11.3 62.3 all-gather.4
  76.3 27.6 all-gather.6
  210.9 77.2 all-gather.8
  311.7 146.3 all-gather.10
  487.2 142.5 reduce-scatter.4
  711.1 77.0 reduce-scatter.8
  794.7 57.9 reduce-scatter.6
  870.7 47.0 reduce-scatter.10
